TPU v7x, 512 devices: a whole 4x4x16 slice. The times are simulated.
512 devices in a mesh: ka: 64 (over z_lo, x, core), vert: 8 (over y, z_hi).
Axes of the slice: x: 4, y: 4, z: 16 (z_hi: 2, z_lo: 8; z = z_hi * 8 + z_lo), core: 2. Of those that a mesh axis runs over, the one named last changes fastest.
Arguments:
- amplitudes: bfloat16 [2, 64, 4, 2, 128, 128], P(None, 'ka', None, None, 'vert'), may hold values from -6 to 6
- factors: bfloat16 [2, 64, 2, 24, 128, 128], P(None, 'ka', None, 'vert'), may hold values from -0.109375 to 0.109375
- kminus: int32 [64, 64], replicated, may hold values from 0 to 63, as said below
- kj_rows: int32 [2], replicated, may hold values from 0 to 63
- kshift: int32 [1], replicated, may hold values from 0 to 63
Outputs:
- sigma: bfloat16 [2, 64, 4, 2, 128, 128], P(None, 'ka', None, None, 'vert')
Inputs may be any that keep to these rules, and one draw needn't show every extreme that they name: kminus[x, y] is the label of the difference x - y in the group of the 64 k-points of a mesh of side 4 in each direction, under a labelling drawn once; each row and column is a permutation.
All inputs are finite; a program needn't handle non-finite values.
Results may differ from a plain program's by a relative error of at most 0.0058.
Values may be sent and summed in bfloat16 or wider, within the bound.
No kernel may reach another device: no remote copies, remote signals or barrier semaphores. Data moves between devices by JAX's collectives and lax.ppermute only.
A program may use at most 64 MiB of HBM per device.

v0:
```python
import jax
import jax.numpy as jnp
from jax import lax
from jax.sharding import PartitionSpec as P


def passed_along(value, axis, by):
    size = lax.axis_size(axis)
    return lax.ppermute(value, axis, [(i, (i + by) % size) for i in range(size)])


def route_factor(block, partners):
    count = partners.shape[0]
    flat = block.reshape(count, -1)
    spread = lax.all_to_all(flat, "ka", split_axis=0, concat_axis=0, tiled=True)
    chosen = jnp.take(spread, partners, axis=0)
    back = lax.all_to_all(chosen, "ka", split_axis=0, concat_axis=0, tiled=True)
    return back.reshape(block.shape)


def route_whole(block, partners):
    count = partners.shape[0]
    flat = block.reshape(count, -1)
    spread = lax.all_to_all(flat, "ka", split_axis=0, concat_axis=0, tiled=True)
    chosen = jnp.take(spread, partners, axis=0)
    back = lax.all_to_all(chosen, "ka", split_axis=0, concat_axis=0, tiled=True)
    return back.reshape(block.shape)


def ladder_block(tilde, own_factor, other_factor):
    occ = tilde.shape[0]
    width = tilde.shape[3]
    left_rows = jnp.transpose(tilde, (0, 2, 1, 3)).reshape(occ * width, 2 * width)
    total = jnp.zeros((2 * width, occ * width), jnp.float32)
    for lane in range(own_factor.shape[1]):
        part_real = other_factor[0, lane]
        part_imag = other_factor[1, lane]
        right = jnp.concatenate(
            [
                jnp.concatenate([part_real, -part_imag], 1),
                jnp.concatenate([part_imag, part_real], 1),
            ],
            0,
        )
        inner = lax.dot_general(
            left_rows, right, (((1,), (1,)), ((), ())), preferred_element_type=jnp.float32
        ).astype(jnp.bfloat16)
        inner = jnp.transpose(inner.reshape(occ, width, 2, width), (2, 1, 0, 3)).reshape(
            2 * width, occ * width
        )
        own_real = own_factor[0, lane]
        own_imag = own_factor[1, lane]
        left = jnp.concatenate(
            [jnp.concatenate([own_real, -own_imag], 1), jnp.concatenate([own_imag, own_real], 1)], 0
        )
        total = total + jnp.dot(left, inner, preferred_element_type=jnp.float32)
    return total.reshape(2, width, occ, width)


def per_device(amplitudes, factors, kminus, kj_rows, kshift):
    rows = amplitudes.shape[0]
    steps = factors.shape[0]
    results = []
    for row in range(rows):
        target = kminus[kj_rows[row], kshift[0]]
        partners = kminus[target]
        own_block = amplitudes[row, 0]
        partner_factor = route_factor(factors[:, 0], partners)
        whole = lax.all_gather(own_block, "vert", axis=2, tiled=True)
        mirror = route_whole(whole, partners)
        tilde = (
            2.0 * whole.astype(jnp.float32) - jnp.swapaxes(mirror, 2, 3).astype(jnp.float32)
        ).astype(jnp.bfloat16)
        total = jnp.zeros((2, whole.shape[2], whole.shape[0], whole.shape[3]), jnp.float32)
        for step in range(steps):
            if step > 0:
                tilde = passed_along(tilde, "ka", 1)
            total = total + ladder_block(tilde, factors[step, 0], partner_factor[step])
        share = lax.psum_scatter(total, "vert", scatter_dimension=1, tiled=True)
        results.append(jnp.transpose(share, (2, 0, 1, 3)).astype(jnp.bfloat16))
    return jnp.stack(results)[:, None]


def solution(mesh):
    in_specs = (
        P(None, "ka", None, None, "vert", None),
        P(None, "ka", None, "vert", None, None),
        P(),
        P(),
        P(),
    )
    out_specs = P(None, "ka", None, None, "vert", None)
    return jax.shard_map(
        per_device, mesh=mesh, in_specs=in_specs, out_specs=out_specs, check_vma=False
    )
```

profile of v0, /device:TPU:6, one launch (start us, length us, event | category | flops | bytes accessed | tf_op | source)
XLA Modules:
  0.0 576.9 jit_solution(8722169848848537973)
XLA Ops:
  6.5 0.8 fusion.182
  7.3 67.3 %all-gather.1 = bf16[1,1,4,2,128,128]{5,4,3,2,1,0:T(8,128)(2,1)S(1)} all-gather(bf16[1,1,4,2,16,128]{5,4,3,2,1,0:T(8,128)(2,1)S(1)} %get-tuple-element.72), channel_id=3, replica_groups=mesh['ka'=64,'vert'=8] {'vert'}, dimensions={4}, use_global_device_ids=true | all-gather | bytes 294912 | tf_op jit(solution)/shard_map/all_gather | solution.py:69
  74.8 0.5 broadcast.31
  75.3 2.2 reduce.8
  77.5 0.9 reshape.233
  78.4 13.0 %all-to-all-start.4 = ((bf16[64,2,1024]{2,1,0:T(2,128)(2,1)}), bf16[64,2,1024]{2,1,0:T(2,128)(2,1)S(1)}, u32[]{:S(2)}, u32[]{:S(2)}) async-start(bf16[64,2,1024]{2,1,0:T(2,128)(2,1)} %reshape.233), calls=%async_computation.5 | async-start | bytes 524288 | tf_op jit(solution)/shard_map/all_to_all | solution.py:24
  91.3 64.1 %all-gather = bf16[1,1,4,2,128,128]{5,4,3,2,1,0:T(8,128)(2,1)S(1)} all-gather(bf16[1,1,4,2,16,128]{5,4,3,2,1,0:T(8,128)(2,1)S(1)} %get-tuple-element.71), channel_id=2, replica_groups=mesh['ka'=64,'vert'=8] {'vert'}, dimensions={4}, use_global_device_ids=true | all-gather | bytes 294912 | tf_op jit(solution)/shard_map/all_gather | solution.py:69
  155.6 2.2 reduce.9
  157.7 0.9 reshape.241
  158.6 20.1 %all-to-all-start = ((bf16[64,2,1024]{2,1,0:T(2,128)(2,1)}), bf16[64,2,1024]{2,1,0:T(2,128)(2,1)S(1)}, u32[]{:S(2)}, u32[]{:S(2)}) async-start(bf16[64,2,1024]{2,1,0:T(2,128)(2,1)} %reshape.241), calls=%async_computation | async-start | bytes 524288 | tf_op jit(solution)/shard_map/all_to_all | solution.py:24
  178.9 3.0 reduce.11
  181.9 1.0 reshape.237
  182.9 13.9 %all-to-all-done = bf16[64,2,1024]{2,1,0:T(2,128)(2,1)S(1)} async-done(((bf16[64,2,1024]{2,1,0:T(2,128)(2,1)}), bf16[64,2,1024]{2,1,0:T(2,128)(2,1)S(1)}, u32[]{:S(2)}, u32[]{:S(2)}) %all-to-all-start) | async-done | bytes 262176 | tf_op jit(solution)/shard_map/all_to_all | solution.py:24
  196.8 7.7 %all-to-all-start.2 = ((bf16[64,2,1536]{2,1,0:T(2,128)(2,1)}), bf16[64,2,1536]{2,1,0:T(2,128)(2,1)S(1)}, u32[]{:S(2)}, u32[]{:S(2)}) async-start(bf16[64,2,1536]{2,1,0:T(2,128)(2,1)} %reshape.237), calls=%async_computation.2 | async-start | bytes 786432 | tf_op jit(solution)/shard_map/all_to_all | solution.py:15
  204.5 0.6 fusion.184
  209.7 1.4 fusion.183
  214.9 0.7 compare_and_fusion.1
  216.5 0.7 gather_fusion.2
  217.2 0.7 gather_fusion
  218.1 0.8 reduce.10
  218.9 0.9 reshape.235
  219.8 8.0 %all-to-all-done.2 = bf16[64,2,1536]{2,1,0:T(2,128)(2,1)S(1)} async-done(((bf16[64,2,1536]{2,1,0:T(2,128)(2,1)}), bf16[64,2,1536]{2,1,0:T(2,128)(2,1)S(1)}, u32[]{:S(2)}, u32[]{:S(2)}) %all-to-all-start.2) | async-done | bytes 393248 | tf_op jit(solution)/shard_map/all_to_all | solution.py:15
  227.7 8.2 %all-to-all-start.5 = ((bf16[64,2,1024]{2,1,0:T(2,128)(2,1)}), bf16[64,2,1024]{2,1,0:T(2,128)(2,1)S(1)}, u32[]{:S(2)}, u32[]{:S(2)}) async-start(bf16[64,2,1024]{2,1,0:T(2,128)(2,1)} %reshape.235), calls=%async_computation.6 | async-start | bytes 524288 | tf_op jit(solution)/shard_map/all_to_all | solution.py:26
  235.9 0.8 reduce.13
  236.7 0.9 reshape.243
  237.6 16.5 %all-to-all-done.5 = bf16[64,2,1024]{2,1,0:T(2,128)(2,1)S(1)} async-done(((bf16[64,2,1024]{2,1,0:T(2,128)(2,1)}), bf16[64,2,1024]{2,1,0:T(2,128)(2,1)S(1)}, u32[]{:S(2)}, u32[]{:S(2)}) %all-to-all-start.5) | async-done | bytes 262176 | tf_op jit(solution)/shard_map/all_to_all | solution.py:26
  254.0 7.7 %all-to-all-start.1 = ((bf16[64,2,1024]{2,1,0:T(2,128)(2,1)}), bf16[64,2,1024]{2,1,0:T(2,128)(2,1)S(1)}, u32[]{:S(2)}, u32[]{:S(2)}) async-start(bf16[64,2,1024]{2,1,0:T(2,128)(2,1)} %reshape.243), calls=%async_computation.1 | async-start | bytes 524288 | tf_op jit(solution)/shard_map/all_to_all | solution.py:26
  262.2 0.8 gather_fusion.3
  263.0 0.8 gather_fusion.1
  263.9 0.9 reduce.12
  264.8 1.0 reshape.239
  265.8 14.0 %all-to-all-done.1 = bf16[64,2,1024]{2,1,0:T(2,128)(2,1)S(1)} async-done(((bf16[64,2,1024]{2,1,0:T(2,128)(2,1)}), bf16[64,2,1024]{2,1,0:T(2,128)(2,1)S(1)}, u32[]{:S(2)}, u32[]{:S(2)}) %all-to-all-start.1) | async-done | bytes 262176 | tf_op jit(solution)/shard_map/all_to_all | solution.py:26
  279.8 7.7 %all-to-all-start.6 = ((bf16[64,2,1536]{2,1,0:T(2,128)(2,1)}), bf16[64,2,1536]{2,1,0:T(2,128)(2,1)S(1)}, u32[]{:S(2)}, u32[]{:S(2)}) async-start(bf16[64,2,1536]{2,1,0:T(2,128)(2,1)} %reshape.239), calls=%async_computation.7 | async-start | bytes 786432 | tf_op jit(solution)/shard_map/all_to_all | solution.py:17
  287.5 0.9 reduce.14
  288.4 1.0 reshape.245
  289.7 0.5 convert_element_type.107
  290.5 2.1 collective-permute-start.1
  292.8 0.5 convert_element_type.106
  293.6 3.3 collective-permute-start
  297.0 19.3 %all-to-all-done.6 = bf16[64,2,1536]{2,1,0:T(2,128)(2,1)S(1)} async-done(((bf16[64,2,1536]{2,1,0:T(2,128)(2,1)}), bf16[64,2,1536]{2,1,0:T(2,128)(2,1)S(1)}, u32[]{:S(2)}, u32[]{:S(2)}) %all-to-all-start.6) | async-done | bytes 393248 | tf_op jit(solution)/shard_map/all_to_all | solution.py:17
  316.3 6.3 %all-to-all-start.3 = ((bf16[64,2,1536]{2,1,0:T(2,128)(2,1)}), bf16[64,2,1536]{2,1,0:T(2,128)(2,1)S(1)}, u32[]{:S(2)}, u32[]{:S(2)}) async-start(bf16[64,2,1536]{2,1,0:T(2,128)(2,1)} %reshape.245), calls=%async_computation.3 | async-start | bytes 786432 | tf_op jit(solution)/shard_map/all_to_all | solution.py:17
  322.9 1.0 copy.71
  325.1 1.6 slice_reduce_fusion
  327.0 0.6 fusion.181
  327.6 0.7 slice_bitcast_fusion.2
  328.3 17.6 %all-to-all-done.3 = bf16[64,2,1536]{2,1,0:T(2,128)(2,1)S(1)} async-done(((bf16[64,2,1536]{2,1,0:T(2,128)(2,1)}), bf16[64,2,1536]{2,1,0:T(2,128)(2,1)S(1)}, u32[]{:S(2)}, u32[]{:S(2)}) %all-to-all-start.3) | async-done | bytes 393248 | tf_op jit(solution)/shard_map/all_to_all | solution.py:17
  346.2 1.6 slice_reduce_fusion.2
  348.0 0.7 fusion.169
  348.7 0.6 slice_bitcast_fusion.14
  349.4 0.6 fusion.175
  352.3 0.5 copy-done.7
  353.4 0.5 copy-done.5
  356.1 0.8 copy.80
  358.5 0.5 copy-done.3
  359.8 0.5 copy-done.11
  362.1 0.5 copy-done.10
  362.6 1.0 convolution_convert_fusion.6
  364.4 0.7 copy-done.2
  366.6 0.8 copy.67
  367.5 93.1 %reduce-scatter.5.cloned.1.call-done = f32[2,16,4,128]{3,1,0,2:T(8,128)} async-done(((f32[2,128,4,128]{3,1,0,2:T(8,128)}), f32[2,16,4,128]{3,1,0,2:T(8,128)}) %reduce-scatter.5.cloned.1.call-update) | async-done | bytes 65552 | tf_op jit(solution)/shard_map/reduce_scatter | solution.py:79
  460.6 0.8 convert_bitcast_fusion
  461.4 107.2 %reduce-scatter.3.cloned.1.call-done = f32[2,16,4,128]{3,1,0,2:T(8,128)} async-done(((f32[2,128,4,128]{3,1,0,2:T(8,128)}), f32[2,16,4,128]{3,1,0,2:T(8,128)}) %reduce-scatter.3.cloned.1.call-update) | async-done | bytes 65552 | tf_op jit(solution)/shard_map/reduce_scatter | solution.py:79
  568.6 0.8 convert_bitcast_fusion.1
  569.4 0.6 maximum_bitcast_fusion
  (120 shorter events, 16.3 us)
Async XLA Ops:
  78.4 80.2 %all-to-all-start.4 = ((bf16[64,2,1024]{2,1,0:T(2,128)(2,1)}), bf16[64,2,1024]{2,1,0:T(2,128)(2,1)S(1)}, u32[]{:S(2)}, u32[]{:S(2)}) async-start(bf16[64,2,1024]{2,1,0:T(2,128)(2,1)} %reshape.233), calls=%async_computation.5 | async-start | bytes 524288 | tf_op jit(solution)/shard_map/all_to_all | solution.py:24
  158.6 20.1 %copy-start = (bf16[2,1,2,3,128,128]{5,4,3,2,1,0:T(8,128)(2,1)S(1)}, bf16[2,1,2,3,128,128]{5,4,3,2,1,0:T(8,128)(2,1)}, u32[]{:S(2)}) copy-start(bf16[2,1,2,3,128,128]{5,4,3,2,1,0:T(8,128)(2,1)} %param.10) | copy-start | bytes 1179652
  158.6 38.2 %all-to-all-start = ((bf16[64,2,1024]{2,1,0:T(2,128)(2,1)}), bf16[64,2,1024]{2,1,0:T(2,128)(2,1)S(1)}, u32[]{:S(2)}, u32[]{:S(2)}) async-start(bf16[64,2,1024]{2,1,0:T(2,128)(2,1)} %reshape.241), calls=%async_computation | async-start | bytes 524288 | tf_op jit(solution)/shard_map/all_to_all | solution.py:24
  182.9 21.6 %copy-start.17 = (s32[2]{0:T(128)S(1)}, s32[2]{0:T(128)}, u32[]{:S(2)}) copy-start(s32[2]{0:T(128)} %param.12) | copy-start | bytes 28
  196.8 30.9 %all-to-all-start.2 = ((bf16[64,2,1536]{2,1,0:T(2,128)(2,1)}), bf16[64,2,1536]{2,1,0:T(2,128)(2,1)S(1)}, u32[]{:S(2)}, u32[]{:S(2)}) async-start(bf16[64,2,1536]{2,1,0:T(2,128)(2,1)} %reshape.237), calls=%async_computation.2 | async-start | bytes 786432 | tf_op jit(solution)/shard_map/all_to_all | solution.py:15
  227.7 26.3 %all-to-all-start.5 = ((bf16[64,2,1024]{2,1,0:T(2,128)(2,1)}), bf16[64,2,1024]{2,1,0:T(2,128)(2,1)S(1)}, u32[]{:S(2)}, u32[]{:S(2)}) async-start(bf16[64,2,1024]{2,1,0:T(2,128)(2,1)} %reshape.235), calls=%async_computation.6 | async-start | bytes 524288 | tf_op jit(solution)/shard_map/all_to_all | solution.py:26
  254.0 25.8 %all-to-all-start.1 = ((bf16[64,2,1024]{2,1,0:T(2,128)(2,1)}), bf16[64,2,1024]{2,1,0:T(2,128)(2,1)S(1)}, u32[]{:S(2)}, u32[]{:S(2)}) async-start(bf16[64,2,1024]{2,1,0:T(2,128)(2,1)} %reshape.243), calls=%async_computation.1 | async-start | bytes 524288 | tf_op jit(solution)/shard_map/all_to_all | solution.py:26
  279.8 36.5 %all-to-all-start.6 = ((bf16[64,2,1536]{2,1,0:T(2,128)(2,1)}), bf16[64,2,1536]{2,1,0:T(2,128)(2,1)S(1)}, u32[]{:S(2)}, u32[]{:S(2)}) async-start(bf16[64,2,1536]{2,1,0:T(2,128)(2,1)} %reshape.239), calls=%async_computation.7 | async-start | bytes 786432 | tf_op jit(solution)/shard_map/all_to_all | solution.py:17
  290.5 33.7 %collective-permute-start.1 = (bf16[4,2,128,128]{3,2,1,0:T(8,128)(2,1)S(1)}, bf16[4,2,128,128]{3,2,1,0:T(8,128)(2,1)S(1)}, u32[]{:S(2)}, u32[]{:S(2)}) collective-permute-start(bf16[4,2,128,128]{3,2,1,0:T(8,128)(2,1)S(1)} %fusion.2), channel_id=1, source_target_pairs={{0,8},{8,16},{16,24},{24,32},{32,40},{40,48},{48,56},{56,64},{64,7... | collective-permute-start | bytes 786440 | tf_op jit(solution)/shard_map/ppermute | solution.py:9
  293.6 30.8 %collective-permute-start = (bf16[4,2,128,128]{3,2,1,0:T(8,128)(2,1)S(1)}, bf16[4,2,128,128]{3,2,1,0:T(8,128)(2,1)S(1)}, u32[]{:S(2)}, u32[]{:S(2)}) collective-permute-start(bf16[4,2,128,128]{3,2,1,0:T(8,128)(2,1)S(1)} %fusion.3), channel_id=1, source_target_pairs={{0,8},{8,16},{16,24},{24,32},{32,40},{40,48},{48,56},{56,64},{64,7... | collective-permute-start | bytes 786440 | tf_op jit(solution)/shard_map/ppermute | solution.py:9
  316.3 29.6 %all-to-all-start.3 = ((bf16[64,2,1536]{2,1,0:T(2,128)(2,1)}), bf16[64,2,1536]{2,1,0:T(2,128)(2,1)S(1)}, u32[]{:S(2)}, u32[]{:S(2)}) async-start(bf16[64,2,1536]{2,1,0:T(2,128)(2,1)} %reshape.245), calls=%async_computation.3 | async-start | bytes 786432 | tf_op jit(solution)/shard_map/all_to_all | solution.py:17
  322.6 138.0 %reduce-scatter.5.cloned.1.call-start = ((), (), s32[]{:S(2)}) async-start(), calls=%async_computation.10 | async-start | bytes 589824 | tf_op jit(solution)/shard_map/reduce_scatter | solution.py:79
  348.7 1.3 copy-start.1
  352.0 0.8 copy-start.7
  352.0 0.8 copy-start.8
  352.0 0.8 copy-start.16
  353.1 0.8 copy-start.5
  353.2 0.8 copy-start.6
  353.2 0.8 copy-start.15
  356.9 0.8 copy-start.13
  356.9 211.6 %reduce-scatter.3.cloned.1.call-start = ((), (), s32[]{:S(2)}) async-start(), calls=%async_computation.9 | async-start | bytes 589824 | tf_op jit(solution)/shard_map/reduce_scatter | solution.py:79
  358.2 0.8 copy-start.3
  358.2 0.8 copy-start.4
  358.3 0.8 copy-start.14
  359.6 0.8 copy-start.11
  360.3 0.8 copy-start.9
  361.1 0.8 copy-start.12
  361.9 0.8 copy-start.10
  364.2 1.0 copy-start.2
Sparse Core Ops, SparseCore 0:
  357.1 103.4 reduce-scatter.4
  465.7 102.8 reduce-scatter.2
where the time goes:
time: 579 us; the launch traced here: 577 us
  waiting for transfers between devices  290 us (50%)
  blocking collectives  131 us (23%)
  starting transfers between devices  76.5 us (13%)
  local copies, waits for them, and re-layouts  33.1 us (6%)
  between operations  22.7 us (4%)
  other arithmetic  17.1 us (3%)
  matrix products  6.53 us (1%)
    reduce_scatter x2, waiting for transfers between devices, per_device(): share = lax.psum_scatter(total, 'vert', scatter_dimension=1, tiled=True)  200 us
    all_gather x2, blocking collectives, per_device(): whole = lax.all_gather(own_block, 'vert', axis=2, tiled=True)  131 us
    all_to_all x2, waiting for transfers between devices, route_factor(): back = lax.all_to_all(chosen, 'ka', split_axis=0, concat_axis=0, tiled=True)  36.9 us
    all_to_all x2, starting transfers between devices, route_whole(): spread = lax.all_to_all(flat, 'ka', split_axis=0, concat_axis=0, tiled=True)  33.1 us
    all_to_all x2, waiting for transfers between devices, route_whole(): back = lax.all_to_all(chosen, 'ka', split_axis=0, concat_axis=0, tiled=True)  30.5 us
    all_to_all x2, starting transfers between devices, route_whole(): back = lax.all_to_all(chosen, 'ka', split_axis=0, concat_axis=0, tiled=True)  15.8 us
    all_to_all x2, starting transfers between devices, route_factor(): back = lax.all_to_all(chosen, 'ka', split_axis=0, concat_axis=0, tiled=True)  13.9 us
    all_to_all x2, waiting for transfers between devices, route_whole(): spread = lax.all_to_all(flat, 'ka', split_axis=0, concat_axis=0, tiled=True)  13.9 us
  transfers between devices with their start and end apart: 11, of which 8 were waited for; matrix products, arithmetic and copies ran while one was open for 6% of the time, Pallas kernels for 0%

commit v1 on v0

v1 whole, which is shorter than its diff:
```python
import functools

import jax
import jax.numpy as jnp
from jax import lax
from jax.experimental import pallas as pl
from jax.experimental.pallas import tpu as pltpu
from jax.sharding import PartitionSpec as P


def exchange(value, axis):
    return lax.all_to_all(value, axis, split_axis=0, concat_axis=0, tiled=True)


def pick(spread, index):
    return spread.at[index].get(mode="promise_in_bounds")


def tilde_kernel(place_ref, *refs):
    own = refs[0:4]
    mirror = refs[4:8]
    out_ref, own_all, mirror_all = refs[8:11]
    for turn in range(4):
        for half in range(2):
            start = pl.multiple_of(place_ref[turn * 2 + half], 16)
            own_all[:, pl.ds(start, 16), :] = own[turn][half]
            mirror_all[:, pl.ds(start, 16), :] = mirror[turn][half]
    for step in range(2):
        for row in range(2):
            for occ in range(4):
                for part in range(2):
                    block = ((step * 2 + row) * 4 + occ) * 2 + part
                    flipped = jnp.transpose(mirror_all[block].astype(jnp.float32))
                    value = 2.0 * own_all[block].astype(jnp.float32) - flipped
                    out_ref[
                        row, step, occ * 128 : (occ + 1) * 128, part * 128 : (part + 1) * 128
                    ] = value.astype(jnp.bfloat16)


def spin_adapted(place, own, mirror):
    return pl.pallas_call(
        tilde_kernel,
        out_shape=jax.ShapeDtypeStruct((2, 2, 512, 256), jnp.bfloat16),
        in_specs=[pl.BlockSpec(memory_space=pltpu.SMEM)]
        + [pl.BlockSpec(memory_space=pltpu.VMEM)] * 8,
        out_specs=pl.BlockSpec(memory_space=pltpu.VMEM),
        scratch_shapes=[
            pltpu.VMEM((32, 128, 128), jnp.bfloat16),
            pltpu.VMEM((32, 128, 128), jnp.bfloat16),
        ],
        compiler_params=pltpu.CompilerParams(vmem_limit_bytes=32 * 1024 * 1024),
        cost_estimate=pl.CostEstimate(flops=2000000, bytes_accessed=3200000, transcendentals=0),
        name="spin_adapted",
    )(place, *own, *mirror)


def complex_matrix(real, imag):
    return jnp.concatenate(
        [jnp.concatenate([real, -imag], 1), jnp.concatenate([imag, real], 1)], 0
    )


def ladder_kernel(tilde_ref, own_ref, other_ref, out_ref, left, right, inner):
    for step in range(2):
        for lane in range(3):
            at = (step * 3 + lane) * 256
            left[:, at : at + 256] = complex_matrix(own_ref[step, 0, lane], own_ref[step, 1, lane])
    for row in range(2):
        for step in range(2):
            for lane in range(3):
                right[lane * 256 : (lane + 1) * 256, :] = complex_matrix(
                    other_ref[row, step, 0, lane], other_ref[row, step, 1, lane]
                )
            product = lax.dot_general(
                tilde_ref[row, step],
                right[...],
                (((1,), (1,)), ((), ())),
                preferred_element_type=jnp.float32,
            ).astype(jnp.bfloat16)
            for lane in range(3):
                for part in range(2):
                    at = (step * 3 + lane) * 256 + part * 128
                    column = lane * 256 + part * 128
                    for occ in range(4):
                        inner[at : at + 128, occ * 128 : (occ + 1) * 128] = product[
                            occ * 128 : (occ + 1) * 128, column : column + 128
                        ]
        total = jnp.dot(left[...], inner[...], preferred_element_type=jnp.float32)
        total = total.astype(jnp.bfloat16)
        for part in range(2):
            for place in range(4):
                at = part * 128 + place * 32
                out_ref[place, row, part] = total[at : at + 32]


def ladder(tilde, own, other):
    return pl.pallas_call(
        ladder_kernel,
        out_shape=jax.ShapeDtypeStruct((4, 2, 2, 32, 512), jnp.bfloat16),
        in_specs=[pl.BlockSpec(memory_space=pltpu.VMEM)] * 3,
        out_specs=pl.BlockSpec(memory_space=pltpu.VMEM),
        scratch_shapes=[
            pltpu.VMEM((256, 1536), jnp.bfloat16),
            pltpu.VMEM((768, 256), jnp.bfloat16),
            pltpu.VMEM((1536, 512), jnp.bfloat16),
        ],
        compiler_params=pltpu.CompilerParams(vmem_limit_bytes=32 * 1024 * 1024),
        cost_estimate=pl.CostEstimate(
            flops=1610612736, bytes_accessed=2900000, transcendentals=0
        ),
        name="ladder",
    )(tilde, own, other)


def gathered(shard):
    other = lax.ppermute(shard, "vert", [(v, v ^ 1) for v in range(8)])
    pair = jnp.stack([shard, other])
    turns = [pair]
    for turn in range(1, 4):
        turns.append(lax.ppermute(pair, "vert", [(v, (v + 2 * turn) % 8) for v in range(8)]))
    return turns


def per_device(amplitudes, factors, kminus, kj_rows, kshift):
    spot = lax.axis_index("ka")
    vert = lax.axis_index("vert")
    partners = [kminus[kminus[kj_rows[row], kshift[0]]] for row in range(2)]
    mine = jnp.where(spot < 32, partners[0], partners[1])

    shard = amplitudes[:, 0]
    behind = lax.ppermute(shard, "ka", [(i, (i + 1) % 64) for i in range(64)])
    own = gathered(jnp.stack([shard, behind]).reshape(32, 16, 128))

    spread = exchange(shard.reshape(64, 4, 128), "ka")
    chosen = jnp.concatenate([pick(spread, mine), pick(spread, jnp.roll(mine, 1))], 1)
    both = exchange(
        jnp.concatenate([chosen, factors[:, 0].reshape(64, 24, 128)], 1), "ka"
    )
    mirror = jnp.stack([both[:, 0:4], both[:, 4:8]]).reshape(32, 16, 128)
    mirror = gathered(mirror)
    spread = both[:, 8:32]
    chosen = jnp.concatenate([pick(spread, partners[0]), pick(spread, partners[1])], 1)
    other = exchange(chosen, "ka")
    other = jnp.stack([other[:, 0:24], other[:, 24:48]]).reshape(2, 2, 2, 3, 128, 128)

    high = lax.rem(vert, 2)
    level = lax.div(vert, 2)
    place = jnp.stack(
        [
            lax.rem(level + 4 - turn, 4) * 32 + (high if half == 0 else 1 - high) * 16
            for turn in range(4)
            for half in range(2)
        ]
    ).astype(jnp.int32)
    tilde = spin_adapted(place, own, mirror)
    partial = ladder(tilde, factors[:, 0], other)

    groups = [[0, 2, 4, 6], [1, 3, 5, 7]]
    pieces = lax.all_to_all(
        partial, "vert", split_axis=0, concat_axis=0, tiled=True, axis_index_groups=groups
    )
    total = jnp.sum(pieces.astype(jnp.float32), 0).reshape(2, 2, 2, 16, 4, 128)
    keep = jnp.where(high == 0, total[:, :, 0], total[:, :, 1])
    give = jnp.where(high == 0, total[:, :, 1], total[:, :, 0]).astype(jnp.bfloat16)
    taken = lax.ppermute(give, "vert", [(v, v ^ 1) for v in range(8)])
    total = (keep + taken.astype(jnp.float32)).astype(jnp.bfloat16)
    return jnp.transpose(total, (0, 3, 1, 2, 4))[:, None]


def solution(mesh):
    in_specs = (
        P(None, "ka", None, None, "vert", None),
        P(None, "ka", None, "vert", None, None),
        P(),
        P(),
        P(),
    )
    out_specs = P(None, "ka", None, None, "vert", None)
    return jax.shard_map(
        per_device, mesh=mesh, in_specs=in_specs, out_specs=out_specs, check_vma=False
    )
```

time: 579 us -> 224 us (0.39)
  the two profiles are of different devices: /device:TPU:6 before, /device:TPU:128 now
where the time goes in v1:
time: 224 us; the launch traced here: 223 us
  waiting for transfers between devices  106 us (47%)
  starting transfers between devices  91.1 us (41%)
  local copies, waits for them, and re-layouts  9.08 us (4%)
  between operations  8.62 us (4%)
  other arithmetic  4.79 us (2%)
  Pallas kernels  3.86 us (2%)
    ppermute x1, waiting for transfers between devices, per_device(): behind = lax.ppermute(shard, 'ka', [(i, (i + 1) % 64) for i in range(64)])  49.9 us
    all_to_all x3, starting transfers between devices, exchange(): return lax.all_to_all(value, axis, split_axis=0, concat_axis=0, tiled=True)  39.7 us
    all_to_all x3, waiting for transfers between devices, exchange(): return lax.all_to_all(value, axis, split_axis=0, concat_axis=0, tiled=True)  25 us
    ppermute x6, starting transfers between devices, gathered(): lax.ppermute(pair, 'vert', [(v, (v + 2 * turn) % 8) for v in range(8)])  19.7 us
    ppermute x2, starting transfers between devices, gathered(): other = lax.ppermute(shard, 'vert', [(v, v ^ 1) for v in range(8)])  18.5 us
    ppermute x2, waiting for transfers between devices, gathered(): other = lax.ppermute(shard, 'vert', [(v, v ^ 1) for v in range(8)])  8.46 us
    all_to_all x1, waiting for transfers between devices, per_device(): lax.all_to_all(partial, 'vert', split_axis=0, concat_axis=0, tiled=True,...  8.04 us
    ppermute x1, starting transfers between devices, per_device(): taken = lax.ppermute(give, 'vert', [(v, v ^ 1) for v in range(8)])  7.67 us
  transfers between devices with their start and end apart: 14, of which 9 were waited for; matrix products, arithmetic and copies ran while one was open for 2% of the time, Pallas kernels for 1%

profile of v1, /device:TPU:128, one launch (start us, length us, event | category | flops | bytes accessed | tf_op | source)
XLA Modules:
  0.0 223.5 jit_solution(9225726740368680345)
XLA Ops:
  0.0 14.4 %all-to-all-start = ((bf16[64,4,128]{2,1,0:T(4,128)(2,1)}), bf16[64,4,128]{2,1,0:T(4,128)(2,1)S(1)}, u32[]{:S(2)}, u32[]{:S(2)}) async-start(bf16[64,4,128]{2,1,0:T(4,128)(2,1)} %bitcast.99), calls=%async_computation | async-start | bytes 131072 | tf_op jit(solution)/shard_map/all_to_all | solution.py:12
  14.4 1.3 fusion.11
  20.2 1.3 fusion.10
  25.3 0.7 fusion.7
  26.0 0.1 copy.16
  26.1 0.1 copy.15
  26.2 0.5 slice.58
  26.8 0.1 slice_reduce_fusion
  26.9 0.7 fusion.5
  27.6 0.0 all-to-all-done
  27.6 0.7 gather_fusion
  28.3 0.7 gather_fusion.1
  28.9 1.9 pad_maximum_fusion.2
  30.9 13.2 %all-to-all-start.1 = ((bf16[64,32,128]{2,1,0:T(8,128)(2,1)}), bf16[64,32,128]{2,1,0:T(8,128)(2,1)S(1)}, u32[]{:S(2)}, u32[]{:S(2)}) async-start(bf16[64,32,128]{2,1,0:T(8,128)(2,1)} %pad_maximum_fusion.2), calls=%async_computation.1 | async-start | bytes 1048576 | tf_op jit(solution)/shard_map/all_to_all | solution.py:12
  44.0 25.0 %all-to-all-done.1 = bf16[64,32,128]{2,1,0:T(8,128)(2,1)S(1)} async-done(((bf16[64,32,128]{2,1,0:T(8,128)(2,1)}), bf16[64,32,128]{2,1,0:T(8,128)(2,1)S(1)}, u32[]{:S(2)}, u32[]{:S(2)}) %all-to-all-start.1) | async-done | bytes 524320 | tf_op jit(solution)/shard_map/all_to_all | solution.py:12
  69.0 0.7 gather_fusion.3
  69.7 0.6 gather_fusion.2
  70.4 1.0 pad_maximum_fusion
  71.3 0.0 copy-start.1
  71.3 12.1 %all-to-all-start.2 = ((bf16[64,48,128]{2,1,0:T(8,128)(2,1)}), bf16[64,48,128]{2,1,0:T(8,128)(2,1)}, u32[]{:S(2)}, u32[]{:S(2)}) async-start(bf16[64,48,128]{2,1,0:T(8,128)(2,1)} %pad_maximum_fusion), calls=%async_computation.2 | async-start | bytes 1572864 | tf_op jit(solution)/shard_map/all_to_all | solution.py:12
  83.5 0.0 copy-done.1
  83.5 2.1 collective-permute-start
  85.6 49.9 %collective-permute-done = bf16[2,4,2,16,128]{4,3,2,1,0:T(8,128)(2,1)S(1)} collective-permute-done((bf16[2,4,2,16,128]{4,3,2,1,0:T(8,128)(2,1)S(1)}, bf16[2,4,2,16,128]{4,3,2,1,0:T(8,128)(2,1)S(1)}, u32[]{:S(2)}, u32[]{:S(2)}) %collective-permute-start) | collective-permute-done | bytes 65568 | tf_op jit(solution)/shard_map/ppermute | solution.py:131
  135.5 10.1 %collective-permute-start.1 = (bf16[32,16,128]{2,1,0:T(8,128)(2,1)S(1)}, bf16[32,16,128]{2,1,0:T(8,128)(2,1)S(1)}, u32[]{:S(2)}, u32[]{:S(2)}) collective-permute-start(bf16[32,16,128]{2,1,0:T(8,128)(2,1)S(1)} %bitcast.97), channel_id=1, source_target_pairs={{0,1},{1,0},{2,3},{3,2},{4,5},{5,4},{6,7},{7,6},{8,9},{9,8},{10,11... | collective-permute-start | bytes 393224 | tf_op jit(solution)/shard_map/ppermute | solution.py:116
  145.6 5.9 %collective-permute-done.1 = bf16[32,16,128]{2,1,0:T(8,128)(2,1)S(1)} collective-permute-done((bf16[32,16,128]{2,1,0:T(8,128)(2,1)S(1)}, bf16[32,16,128]{2,1,0:T(8,128)(2,1)S(1)}, u32[]{:S(2)}, u32[]{:S(2)}) %collective-permute-start.1) | collective-permute-done | bytes 131104 | tf_op jit(solution)/shard_map/ppermute | solution.py:116
  151.6 7.1 %collective-permute-start.4 = (bf16[2,32,16,128]{3,2,1,0:T(8,128)(2,1)S(1)}, bf16[2,32,16,128]{3,2,1,0:T(8,128)(2,1)S(1)}, u32[]{:S(2)}, u32[]{:S(2)}) collective-permute-start(bf16[2,32,16,128]{3,2,1,0:T(8,128)(2,1)S(1)} %pad_maximum_fusion.3.refs_0_), channel_id=1, source_target_pairs={{0,6},{1,7},{2,0},{3,1},{4,2},{5,3},{6,4},{7,5},{8,14},{9,15},{10,... | collective-permute-start | bytes 786440 | tf_op jit(solution)/shard_map/ppermute | solution.py:120
  158.7 0.1 pad_maximum_fusion.6
  158.8 8.4 %collective-permute-start.5 = (bf16[32,16,128]{2,1,0:T(8,128)(2,1)S(1)}, bf16[32,16,128]{2,1,0:T(8,128)(2,1)S(1)}, u32[]{:S(2)}, u32[]{:S(2)}) collective-permute-start(bf16[32,16,128]{2,1,0:T(8,128)(2,1)S(1)} %bitcast.95), channel_id=1, source_target_pairs={{0,1},{1,0},{2,3},{3,2},{4,5},{5,4},{6,7},{7,6},{8,9},{9,8},{10,11... | collective-permute-start | bytes 393224 | tf_op jit(solution)/shard_map/ppermute | solution.py:116
  167.2 1.9 collective-permute-start.3
  169.2 2.8 %collective-permute-start.2 = (bf16[2,32,16,128]{3,2,1,0:T(8,128)(2,1)S(1)}, bf16[2,32,16,128]{3,2,1,0:T(8,128)(2,1)S(1)}, u32[]{:S(2)}, u32[]{:S(2)}) collective-permute-start(bf16[2,32,16,128]{3,2,1,0:T(8,128)(2,1)S(1)} %pad_maximum_fusion.3.refs_0_), channel_id=1, source_target_pairs={{0,2},{1,3},{2,4},{3,5},{4,6},{5,7},{6,0},{7,1},{8,10},{9,11},{10,... | collective-permute-start | bytes 786440 | tf_op jit(solution)/shard_map/ppermute | solution.py:120
  171.9 2.6 %collective-permute-done.5 = bf16[32,16,128]{2,1,0:T(8,128)(2,1)S(1)} collective-permute-done((bf16[32,16,128]{2,1,0:T(8,128)(2,1)S(1)}, bf16[32,16,128]{2,1,0:T(8,128)(2,1)S(1)}, u32[]{:S(2)}, u32[]{:S(2)}) %collective-permute-start.5) | collective-permute-done | bytes 131104 | tf_op jit(solution)/shard_map/ppermute | solution.py:116
  174.5 3.0 %collective-permute-start.8 = (bf16[2,32,16,128]{3,2,1,0:T(8,128)(2,1)S(1)}, bf16[2,32,16,128]{3,2,1,0:T(8,128)(2,1)S(1)}, u32[]{:S(2)}, u32[]{:S(2)}) collective-permute-start(bf16[2,32,16,128]{3,2,1,0:T(8,128)(2,1)S(1)} %pad_maximum_fusion.4.refs_4_), channel_id=1, source_target_pairs={{0,6},{1,7},{2,0},{3,1},{4,2},{5,3},{6,4},{7,5},{8,14},{9,15},{10,... | collective-permute-start | bytes 786440 | tf_op jit(solution)/shard_map/ppermute | solution.py:120
  177.5 3.0 %collective-permute-start.7 = (bf16[2,32,16,128]{3,2,1,0:T(8,128)(2,1)S(1)}, bf16[2,32,16,128]{3,2,1,0:T(8,128)(2,1)S(1)}, u32[]{:S(2)}, u32[]{:S(2)}) collective-permute-start(bf16[2,32,16,128]{3,2,1,0:T(8,128)(2,1)S(1)} %pad_maximum_fusion.4.refs_4_), channel_id=1, source_target_pairs={{0,4},{1,5},{2,6},{3,7},{4,0},{5,1},{6,2},{7,3},{8,12},{9,13},{10,... | collective-permute-start | bytes 786440 | tf_op jit(solution)/shard_map/ppermute | solution.py:120
  180.5 0.0 collective-permute-done.4.refs_3_
  180.5 1.9 collective-permute-start.6
  182.5 0.1 stack.71.place_ref
  182.6 0.0 collective-permute-done.3.refs_2_
  182.6 0.0 collective-permute-done.2.refs_1_
  182.6 0.2 collective-permute-done.8.refs_7_
  182.8 4.5 %collective-permute-done.7.refs_6_ = bf16[2,32,16,128]{3,2,1,0:T(8,128)(2,1)S(1)} collective-permute-done((bf16[2,32,16,128]{3,2,1,0:T(8,128)(2,1)S(1)}, bf16[2,32,16,128]{3,2,1,0:T(8,128)(2,1)S(1)}, u32[]{:S(2)}, u32[]{:S(2)}) %collective-permute-start.7) | collective-permute-done | bytes 262176 | tf_op jit(solution)/shard_map/ppermute | solution.py:120
  187.3 2.8 %collective-permute-done.6.refs_5_ = bf16[2,32,16,128]{3,2,1,0:T(8,128)(2,1)S(1)} collective-permute-done((bf16[2,32,16,128]{3,2,1,0:T(8,128)(2,1)S(1)}, bf16[2,32,16,128]{3,2,1,0:T(8,128)(2,1)S(1)}, u32[]{:S(2)}, u32[]{:S(2)}) %collective-permute-start.6) | collective-permute-done | bytes 262176 | tf_op jit(solution)/shard_map/ppermute | solution.py:120
  190.1 1.2 spin_adapted.1.tilde_ref
  191.3 0.0 all-to-all-done.2
  191.3 1.2 fusion.9
  192.5 0.0 copy-start
  192.5 0.1 pad_maximum_fusion.1.other_ref
  192.6 0.9 copy-done
  193.5 2.6 %ladder.1 = bf16[4,2,2,32,512]{4,3,2,1,0:T(8,128)(2,1)} custom-call(bf16[2,2,512,256]{3,2,1,0:T(8,128)(2,1)S(1)} %spin_adapted.1.tilde_ref, bf16[2,2,3,128,128]{4,3,2,1,0:T(8,128)(2,1)S(1)} %bitcast.92, bf16[2,2,2,3,128,128]{5,4,3,2,1,0:T(8,128)(2,1)S(1)} %pad_maximum_fusion.1.other_ref), custom_call_target="tpu_custom_call" | custom-call | flops 1610612736 | bytes 2900000 | tf_op jit(solution)/shard_map/ladder/pallas_call | solution.py:97
  196.2 3.5 %all-to-all-start.3 = ((bf16[4,2,2,32,512]{4,3,2,1,0:T(8,128)(2,1)}), bf16[4,2,2,32,512]{4,3,2,1,0:T(8,128)(2,1)S(1)}, u32[]{:S(2)}, u32[]{:S(2)}) async-start(bf16[4,2,2,32,512]{4,3,2,1,0:T(8,128)(2,1)} %ladder.1), calls=%async_computation.3 | async-start | bytes 1048576 | tf_op jit(solution)/shard_map/all_to_all | solution.py:159
  199.6 8.0 %all-to-all-done.3 = bf16[4,2,2,32,512]{4,3,2,1,0:T(8,128)(2,1)S(1)} async-done(((bf16[4,2,2,32,512]{4,3,2,1,0:T(8,128)(2,1)}), bf16[4,2,2,32,512]{4,3,2,1,0:T(8,128)(2,1)S(1)}, u32[]{:S(2)}, u32[]{:S(2)}) %all-to-all-start.3) | async-done | bytes 524320 | tf_op jit(solution)/shard_map/all_to_all | solution.py:159
  207.7 0.1 convert_reduce_fusion
  207.8 0.1 reshape.192
  207.9 7.7 %collective-permute-start.9 = (bf16[2,2,16,4,128]{4,3,2,1,0:T(4,128)(2,1)S(1)}, bf16[2,2,16,4,128]{4,3,2,1,0:T(4,128)(2,1)S(1)}, u32[]{:S(2)}, u32[]{:S(2)}) collective-permute-start(bf16[2,2,16,4,128]{4,3,2,1,0:T(4,128)(2,1)S(1)} %fusion.3), channel_id=1, source_target_pairs={{0,1},{1,0},{2,3},{3,2},{4,5},{5,4},{6,7},{7,6},{8,9},{9,8},{10,11... | collective-permute-start | bytes 196616 | tf_op jit(solution)/shard_map/ppermute | solution.py:165
  215.6 7.2 %collective-permute-done.9 = bf16[2,2,16,4,128]{4,3,2,1,0:T(4,128)(2,1)S(1)} collective-permute-done((bf16[2,2,16,4,128]{4,3,2,1,0:T(4,128)(2,1)S(1)}, bf16[2,2,16,4,128]{4,3,2,1,0:T(4,128)(2,1)S(1)}, u32[]{:S(2)}, u32[]{:S(2)}) %collective-permute-start.9) | collective-permute-done | bytes 65568 | tf_op jit(solution)/shard_map/ppermute | solution.py:165
  222.8 0.1 fusion.4
  222.8 0.6 copy.14
  (10 shorter events, 0.2 us)
Async XLA Ops:
  0.0 27.6 %all-to-all-start = ((bf16[64,4,128]{2,1,0:T(4,128)(2,1)}), bf16[64,4,128]{2,1,0:T(4,128)(2,1)S(1)}, u32[]{:S(2)}, u32[]{:S(2)}) async-start(bf16[64,4,128]{2,1,0:T(4,128)(2,1)} %bitcast.99), calls=%async_computation | async-start | bytes 131072 | tf_op jit(solution)/shard_map/all_to_all | solution.py:12
  30.9 38.1 %all-to-all-start.1 = ((bf16[64,32,128]{2,1,0:T(8,128)(2,1)}), bf16[64,32,128]{2,1,0:T(8,128)(2,1)S(1)}, u32[]{:S(2)}, u32[]{:S(2)}) async-start(bf16[64,32,128]{2,1,0:T(8,128)(2,1)} %pad_maximum_fusion.2), calls=%async_computation.1 | async-start | bytes 1048576 | tf_op jit(solution)/shard_map/all_to_all | solution.py:12
  71.3 12.2 %copy-start.1 = (bf16[2,1,4,2,16,128]{5,4,3,2,1,0:T(8,128)(2,1)S(1)}, bf16[2,1,4,2,16,128]{5,4,3,2,1,0:T(8,128)(2,1)}, u32[]{:S(2)}) copy-start(bf16[2,1,4,2,16,128]{5,4,3,2,1,0:T(8,128)(2,1)} %param.5) | copy-start | bytes 196612
  71.3 120.0 %all-to-all-start.2 = ((bf16[64,48,128]{2,1,0:T(8,128)(2,1)}), bf16[64,48,128]{2,1,0:T(8,128)(2,1)}, u32[]{:S(2)}, u32[]{:S(2)}) async-start(bf16[64,48,128]{2,1,0:T(8,128)(2,1)} %pad_maximum_fusion), calls=%async_computation.2 | async-start | bytes 1572864 | tf_op jit(solution)/shard_map/all_to_all | solution.py:12
  83.5 52.0 %collective-permute-start = (bf16[2,4,2,16,128]{4,3,2,1,0:T(8,128)(2,1)S(1)}, bf16[2,4,2,16,128]{4,3,2,1,0:T(8,128)(2,1)S(1)}, u32[]{:S(2)}, u32[]{:S(2)}) collective-permute-start(bf16[2,4,2,16,128]{4,3,2,1,0:T(8,128)(2,1)S(1)} %bitcast.100), channel_id=1, source_target_pairs={{0,8},{8,16},{16,24},{24,32},{32,40},{40,48},{48,56},{56,64},{64,7... | collective-permute-start | bytes 196616 | tf_op jit(solution)/shard_map/ppermute | solution.py:131
  135.5 16.0 %collective-permute-start.1 = (bf16[32,16,128]{2,1,0:T(8,128)(2,1)S(1)}, bf16[32,16,128]{2,1,0:T(8,128)(2,1)S(1)}, u32[]{:S(2)}, u32[]{:S(2)}) collective-permute-start(bf16[32,16,128]{2,1,0:T(8,128)(2,1)S(1)} %bitcast.97), channel_id=1, source_target_pairs={{0,1},{1,0},{2,3},{3,2},{4,5},{5,4},{6,7},{7,6},{8,9},{9,8},{10,11... | collective-permute-start | bytes 393224 | tf_op jit(solution)/shard_map/ppermute | solution.py:116
  151.6 28.9 %collective-permute-start.4 = (bf16[2,32,16,128]{3,2,1,0:T(8,128)(2,1)S(1)}, bf16[2,32,16,128]{3,2,1,0:T(8,128)(2,1)S(1)}, u32[]{:S(2)}, u32[]{:S(2)}) collective-permute-start(bf16[2,32,16,128]{3,2,1,0:T(8,128)(2,1)S(1)} %pad_maximum_fusion.3.refs_0_), channel_id=1, source_target_pairs={{0,6},{1,7},{2,0},{3,1},{4,2},{5,3},{6,4},{7,5},{8,14},{9,15},{10,... | collective-permute-start | bytes 786440 | tf_op jit(solution)/shard_map/ppermute | solution.py:120
  158.8 15.7 %collective-permute-start.5 = (bf16[32,16,128]{2,1,0:T(8,128)(2,1)S(1)}, bf16[32,16,128]{2,1,0:T(8,128)(2,1)S(1)}, u32[]{:S(2)}, u32[]{:S(2)}) collective-permute-start(bf16[32,16,128]{2,1,0:T(8,128)(2,1)S(1)} %bitcast.95), channel_id=1, source_target_pairs={{0,1},{1,0},{2,3},{3,2},{4,5},{5,4},{6,7},{7,6},{8,9},{9,8},{10,11... | collective-permute-start | bytes 393224 | tf_op jit(solution)/shard_map/ppermute | solution.py:116
  167.2 15.3 %collective-permute-start.3 = (bf16[2,32,16,128]{3,2,1,0:T(8,128)(2,1)S(1)}, bf16[2,32,16,128]{3,2,1,0:T(8,128)(2,1)S(1)}, u32[]{:S(2)}, u32[]{:S(2)}) collective-permute-start(bf16[2,32,16,128]{3,2,1,0:T(8,128)(2,1)S(1)} %pad_maximum_fusion.3.refs_0_), channel_id=1, source_target_pairs={{0,4},{1,5},{2,6},{3,7},{4,0},{5,1},{6,2},{7,3},{8,12},{9,13},{10,... | collective-permute-start | bytes 786440 | tf_op jit(solution)/shard_map/ppermute | solution.py:120
  169.2 13.4 %collective-permute-start.2 = (bf16[2,32,16,128]{3,2,1,0:T(8,128)(2,1)S(1)}, bf16[2,32,16,128]{3,2,1,0:T(8,128)(2,1)S(1)}, u32[]{:S(2)}, u32[]{:S(2)}) collective-permute-start(bf16[2,32,16,128]{3,2,1,0:T(8,128)(2,1)S(1)} %pad_maximum_fusion.3.refs_0_), channel_id=1, source_target_pairs={{0,2},{1,3},{2,4},{3,5},{4,6},{5,7},{6,0},{7,1},{8,10},{9,11},{10,... | collective-permute-start | bytes 786440 | tf_op jit(solution)/shard_map/ppermute | solution.py:120
  174.5 8.3 %collective-permute-start.8 = (bf16[2,32,16,128]{3,2,1,0:T(8,128)(2,1)S(1)}, bf16[2,32,16,128]{3,2,1,0:T(8,128)(2,1)S(1)}, u32[]{:S(2)}, u32[]{:S(2)}) collective-permute-start(bf16[2,32,16,128]{3,2,1,0:T(8,128)(2,1)S(1)} %pad_maximum_fusion.4.refs_4_), channel_id=1, source_target_pairs={{0,6},{1,7},{2,0},{3,1},{4,2},{5,3},{6,4},{7,5},{8,14},{9,15},{10,... | collective-permute-start | bytes 786440 | tf_op jit(solution)/shard_map/ppermute | solution.py:120
  177.5 9.8 %collective-permute-start.7 = (bf16[2,32,16,128]{3,2,1,0:T(8,128)(2,1)S(1)}, bf16[2,32,16,128]{3,2,1,0:T(8,128)(2,1)S(1)}, u32[]{:S(2)}, u32[]{:S(2)}) collective-permute-start(bf16[2,32,16,128]{3,2,1,0:T(8,128)(2,1)S(1)} %pad_maximum_fusion.4.refs_4_), channel_id=1, source_target_pairs={{0,4},{1,5},{2,6},{3,7},{4,0},{5,1},{6,2},{7,3},{8,12},{9,13},{10,... | collective-permute-start | bytes 786440 | tf_op jit(solution)/shard_map/ppermute | solution.py:120
  180.5 9.6 %collective-permute-start.6 = (bf16[2,32,16,128]{3,2,1,0:T(8,128)(2,1)S(1)}, bf16[2,32,16,128]{3,2,1,0:T(8,128)(2,1)S(1)}, u32[]{:S(2)}, u32[]{:S(2)}) collective-permute-start(bf16[2,32,16,128]{3,2,1,0:T(8,128)(2,1)S(1)} %pad_maximum_fusion.4.refs_4_), channel_id=1, source_target_pairs={{0,2},{1,3},{2,4},{3,5},{4,6},{5,7},{6,0},{7,1},{8,10},{9,11},{10,... | collective-permute-start | bytes 786440 | tf_op jit(solution)/shard_map/ppermute | solution.py:120
  192.5 1.0 copy-start
  196.2 11.5 %all-to-all-start.3 = ((bf16[4,2,2,32,512]{4,3,2,1,0:T(8,128)(2,1)}), bf16[4,2,2,32,512]{4,3,2,1,0:T(8,128)(2,1)S(1)}, u32[]{:S(2)}, u32[]{:S(2)}) async-start(bf16[4,2,2,32,512]{4,3,2,1,0:T(8,128)(2,1)} %ladder.1), calls=%async_computation.3 | async-start | bytes 1048576 | tf_op jit(solution)/shard_map/all_to_all | solution.py:159
  207.9 14.9 %collective-permute-start.9 = (bf16[2,2,16,4,128]{4,3,2,1,0:T(4,128)(2,1)S(1)}, bf16[2,2,16,4,128]{4,3,2,1,0:T(4,128)(2,1)S(1)}, u32[]{:S(2)}, u32[]{:S(2)}) collective-permute-start(bf16[2,2,16,4,128]{4,3,2,1,0:T(4,128)(2,1)S(1)} %fusion.3), channel_id=1, source_target_pairs={{0,1},{1,0},{2,3},{3,2},{4,5},{5,4},{6,7},{7,6},{8,9},{9,8},{10,11... | collective-permute-start | bytes 196616 | tf_op jit(solution)/shard_map/ppermute | solution.py:165

commit v2 on v1

v2 whole, which is shorter than its diff:
```python
import jax
import jax.numpy as jnp
from jax import lax
from jax.experimental import pallas as pl
from jax.experimental.pallas import tpu as pltpu
from jax.sharding import PartitionSpec as P

SMEM = pl.BlockSpec(memory_space=pltpu.SMEM)
VMEM = pl.BlockSpec(memory_space=pltpu.VMEM)
HBM = pl.BlockSpec(memory_space=pltpu.HBM)


def exchange(value, axis):
    return lax.all_to_all(value, axis, split_axis=0, concat_axis=0, tiled=True)


def params(mebibytes):
    return pltpu.CompilerParams(vmem_limit_bytes=mebibytes * 1024 * 1024)


def wide(value):
    return value.astype(jnp.float32)


def tables(kminus_ref, rows_ref, shift_ref, row):
    return kminus_ref[rows_ref[row], shift_ref[0]]


def mirror_kernel(kminus_ref, rows_ref, shift_ref, row_ref, spread_ref, out_ref):
    target = tables(kminus_ref, rows_ref, shift_ref, row_ref[0])
    before = wide(spread_ref[kminus_ref[target, 63]])[24:28]
    for k in range(64):
        piece = wide(spread_ref[kminus_ref[target, k]])[24:28]
        value = jnp.concatenate([piece, before], 0).astype(jnp.bfloat16)
        out_ref[k] = value
        out_ref[64 + k] = value
        before = piece


def mirror_pieces(lookup, row, spread):
    return pl.pallas_call(
        mirror_kernel,
        out_shape=jax.ShapeDtypeStruct((128, 8, 128), jnp.bfloat16),
        in_specs=[SMEM] * 4 + [VMEM],
        out_specs=VMEM,
        compiler_params=params(16),
        cost_estimate=pl.CostEstimate(flops=0, bytes_accessed=1000000, transcendentals=0),
        name="mirror_pieces",
    )(*lookup, row, spread)


def factor_kernel(kminus_ref, rows_ref, shift_ref, spread_ref, out_ref):
    first = tables(kminus_ref, rows_ref, shift_ref, 0)
    second = tables(kminus_ref, rows_ref, shift_ref, 1)
    for k in range(64):
        block = jnp.concatenate(
            [
                wide(spread_ref[kminus_ref[first, k]])[0:24],
                wide(spread_ref[kminus_ref[second, k]])[0:24],
            ],
            0,
        )
        out_ref[k] = block.astype(jnp.bfloat16)


def factor_pieces(lookup, spread):
    return pl.pallas_call(
        factor_kernel,
        out_shape=jax.ShapeDtypeStruct((64, 48, 128), jnp.bfloat16),
        in_specs=[SMEM] * 3 + [VMEM],
        out_specs=VMEM,
        compiler_params=params(16),
        cost_estimate=pl.CostEstimate(flops=0, bytes_accessed=1300000, transcendentals=0),
        name="factor_pieces",
    )(*lookup, spread)


def tilde_kernel(place_ref, own_ref, *refs):
    turns = refs[0:4]
    out_ref, left_ref, blocks, arrived = refs[4:8]
    copies = []
    for turn in range(4):
        for high in range(2):
            start = pl.multiple_of(place_ref[turn] + high * 16, 16)
            copies.append(
                pltpu.make_async_copy(
                    turns[turn].at[:, high],
                    blocks.at[:, :, pl.ds(start, 16), :],
                    arrived.at[turn * 2 + high],
                )
            )
    for copy in copies:
        copy.start()
    for step in range(2):
        for lane in range(3):
            at = (step * 3 + lane) * 256
            left_ref[:, at : at + 256] = complex_matrix(
                own_ref[step, 0, lane], own_ref[step, 1, lane]
            )
    for copy in copies:
        copy.wait()
    for step in range(2):
        for row in range(2):
            for occ in range(4):
                for part in range(2):
                    block = (row * 4 + occ) * 2 + part
                    flipped = jnp.transpose(wide(blocks[2 + step, block]))
                    value = 2.0 * wide(blocks[step, block]) - flipped
                    out_ref[
                        row, step, occ * 128 : (occ + 1) * 128, part * 128 : (part + 1) * 128
                    ] = value.astype(jnp.bfloat16)


def spin_adapted(place, own, turns):
    return pl.pallas_call(
        tilde_kernel,
        out_shape=[
            jax.ShapeDtypeStruct((2, 2, 512, 256), jnp.bfloat16),
            jax.ShapeDtypeStruct((256, 1536), jnp.bfloat16),
        ],
        in_specs=[SMEM, VMEM] + [HBM] * 4,
        out_specs=[VMEM, VMEM],
        scratch_shapes=[
            pltpu.VMEM((4, 16, 128, 128), jnp.bfloat16),
            pltpu.SemaphoreType.DMA((8,)),
        ],
        compiler_params=params(12),
        cost_estimate=pl.CostEstimate(flops=2000000, bytes_accessed=3200000, transcendentals=0),
        name="spin_adapted",
    )(place, own, *turns)


def complex_matrix(real, imag):
    return jnp.concatenate(
        [jnp.concatenate([real, -imag], 1), jnp.concatenate([imag, real], 1)], 0
    )


def ladder_kernel(tilde_ref, left_ref, other_ref, out_ref, tilde, left, other, right, inner, here):
    copies = [
        pltpu.make_async_copy(other_ref, other, here.at[0]),
        pltpu.make_async_copy(tilde_ref, tilde, here.at[1]),
        pltpu.make_async_copy(left_ref, left, here.at[2]),
    ]
    for copy in copies:
        copy.start()
    for copy in copies:
        copy.wait()
    for row in range(2):
        factor = jnp.concatenate(
            [wide(other[m])[row * 24 : (row + 1) * 24] for m in range(64)], 0
        ).astype(jnp.bfloat16)
        for step in range(2):
            for lane in range(3):
                real = (step * 6 + lane) * 128
                imag = real + 384
                right[lane * 256 : (lane + 1) * 256, :] = complex_matrix(
                    factor[real : real + 128], factor[imag : imag + 128]
                )
            product = lax.dot_general(
                tilde[row, step],
                right[...],
                (((1,), (1,)), ((), ())),
                preferred_element_type=jnp.float32,
            ).astype(jnp.bfloat16)
            for lane in range(3):
                for part in range(2):
                    at = (step * 3 + lane) * 256 + part * 128
                    column = lane * 256 + part * 128
                    for occ in range(4):
                        inner[at : at + 128, occ * 128 : (occ + 1) * 128] = product[
                            occ * 128 : (occ + 1) * 128, column : column + 128
                        ]
        total = jnp.dot(left[...], inner[...], preferred_element_type=jnp.float32)
        total = total.astype(jnp.bfloat16)
        for occ in range(4):
            for part in range(2):
                for place in range(4):
                    at = part * 128 + place * 32
                    out_ref[place, row, occ, part] = total[
                        at : at + 32, occ * 128 : (occ + 1) * 128
                    ]


def ladder(tilde, left, other):
    return pl.pallas_call(
        ladder_kernel,
        out_shape=jax.ShapeDtypeStruct((4, 2, 4, 2, 32, 128), jnp.bfloat16),
        in_specs=[HBM] * 3,
        out_specs=VMEM,
        scratch_shapes=[
            pltpu.VMEM((2, 2, 512, 256), jnp.bfloat16),
            pltpu.VMEM((256, 1536), jnp.bfloat16),
            pltpu.VMEM((64, 48, 128), jnp.bfloat16),
            pltpu.VMEM((768, 256), jnp.bfloat16),
            pltpu.VMEM((1536, 512), jnp.bfloat16),
            pltpu.SemaphoreType.DMA((3,)),
        ],
        compiler_params=params(12),
        cost_estimate=pl.CostEstimate(
            flops=1610612736, bytes_accessed=2900000, transcendentals=0
        ),
        name="ladder",
    )(tilde, left, other)


def turned(value):
    return [value] + [
        lax.ppermute(value, "vert", [(v, (v + 2 * turn) % 8) for v in range(8)])
        for turn in range(1, 4)
    ]


def swapped(value):
    return lax.ppermute(value, "vert", [(v, v ^ 1) for v in range(8)])


def ahead(value):
    return lax.ppermute(value, "ka", [(k, (k + 1) % 64) for k in range(64)])


def per_device(amplitudes, factors, kminus, kj_rows, kshift):
    spot = lax.axis_index("ka")
    vert = lax.axis_index("vert")
    high = lax.rem(vert, 2)
    level = lax.div(vert, 2)
    lookup = (kminus, kj_rows, kshift)
    row = lax.div(spot, 32).astype(jnp.int32).reshape(1)
    place = jnp.stack([lax.rem(level + 4 - turn, 4) * 32 for turn in range(4)]).astype(jnp.int32)

    shard = amplitudes[:, 0]
    spread = exchange(
        jnp.concatenate([factors[:, 0].reshape(64, 24, 128), shard.reshape(64, 4, 128)], 1), "ka"
    )
    behind = ahead(shard)
    other_half = swapped(shard)
    spread, behind, other_half = lax.optimization_barrier((spread, behind, other_half))
    here = jnp.stack([shard, behind]).reshape(2, 16, 16, 128)
    there = jnp.stack([other_half, ahead(other_half)]).reshape(2, 16, 16, 128)
    own = jnp.where(
        high == 0, jnp.stack([here, there], axis=1), jnp.stack([there, here], axis=1)
    )
    pairs = [[k * 8 + 2 * y + h for h in range(2) for k in range(64)] for y in range(4)]
    mirror = lax.all_to_all(
        mirror_pieces(lookup, row, spread),
        ("ka", "vert"),
        split_axis=0,
        concat_axis=0,
        tiled=True,
        axis_index_groups=pairs,
    )
    chosen = factor_pieces(lookup, spread)
    mirror, own, chosen = lax.optimization_barrier((mirror, own, chosen))

    other = exchange(chosen, "ka")
    mirror = jnp.transpose(mirror.reshape(2, 64, 2, 4, 128), (2, 0, 1, 3, 4))
    blocks = turned(jnp.concatenate([own, mirror.reshape(2, 2, 16, 16, 128)]))

    tilde, left = spin_adapted(place, factors[:, 0], blocks)
    partial = ladder(tilde, left, other)

    groups = [[0, 2, 4, 6], [1, 3, 5, 7]]
    pieces = lax.all_to_all(
        partial, "vert", split_axis=0, concat_axis=0, tiled=True, axis_index_groups=groups
    )
    total = jnp.sum(pieces.astype(jnp.float32), 0).reshape(2, 4, 2, 2, 16, 128)
    keep = jnp.where(high == 0, total[:, :, :, 0], total[:, :, :, 1])
    give = jnp.where(high == 0, total[:, :, :, 1], total[:, :, :, 0]).astype(jnp.bfloat16)
    taken = swapped(give)
    total = (keep + taken.astype(jnp.float32)).astype(jnp.bfloat16)
    return total[:, None]


def solution(mesh):
    in_specs = (
        P(None, "ka", None, None, "vert", None),
        P(None, "ka", None, "vert", None, None),
        P(),
        P(),
        P(),
    )
    out_specs = P(None, "ka", None, None, "vert", None)
    return jax.shard_map(
        per_device, mesh=mesh, in_specs=in_specs, out_specs=out_specs, check_vma=False
    )
```

time: 224 us -> 173 us (0.77)
  the two profiles are of different devices: /device:TPU:128 before, /device:TPU:4 now
where the time goes in v2:
time: 173 us
  waiting for transfers between devices  75.1 us (43%)
  starting transfers between devices  68 us (39%)
  blocking collectives  14 us (8%)
  Pallas kernels  7.57 us (4%)
  local copies, waits for them, and re-layouts  4.34 us (3%)
  other arithmetic  2.79 us (2%)
    all_to_all x2, starting transfers between devices, exchange(): return lax.all_to_all(value, axis, split_axis=0, concat_axis=0, tiled=True)  23.2 us
    ppermute x3, waiting for transfers between devices, turned(): lax.ppermute(value, 'vert', [(v, (v + 2 * turn) % 8) for v in range(8)])  22.8 us
    all_to_all x2, waiting for transfers between devices, exchange(): return lax.all_to_all(value, axis, split_axis=0, concat_axis=0, tiled=True)  19.2 us
    ppermute x2, starting transfers between devices, swapped(): return lax.ppermute(value, 'vert', [(v, v ^ 1) for v in range(8)])  18 us
    ppermute x2, waiting for transfers between devices, swapped(): return lax.ppermute(value, 'vert', [(v, v ^ 1) for v in range(8)])  16.4 us
    all_to_all x1, waiting for transfers between devices, per_device(): lax.all_to_all(mirror_pieces(lookup, row, spread), ('ka', 'vert'), split_...  15.3 us
    all_to_all x1, blocking collectives, per_device(): lax.all_to_all(partial, 'vert', split_axis=0, concat_axis=0, tiled=True,...  14 us
    all_to_all x1, starting transfers between devices, per_device(): lax.all_to_all(mirror_pieces(lookup, row, spread), ('ka', 'vert'), split_...  12.4 us
  transfers between devices with their start and end apart: 10, of which 8 were waited for; matrix products, arithmetic and copies ran while one was open for 0% of the time, Pallas kernels for 2%

profile of v2, /device:TPU:4, one launch (start us, length us, event | category | flops | bytes accessed | tf_op | source)
XLA Modules:
  0.0 172.6 jit_solution(10980357808253343155)
XLA Ops:
  0.0 1.9 %pad_maximum_fusion = bf16[64,28,128]{2,1,0:T(8,128)(2,1)} fusion(bf16[64,4,128]{2,1,0:T(4,128)(2,1)} %bitcast.58, bf16[64,24,128]{2,1,0:T(8,128)(2,1)} %bitcast.52), kind=kLoop, calls=%fused_computation.1 | loop fusion | flops 917504 | bytes 917504 | tf_op jit(solution)/shard_map/concatenate | solution.py:233
  1.9 0.0 copy-start.7
  1.9 0.0 copy-start.1
  1.9 16.2 %all-to-all-start = ((bf16[64,28,128]{2,1,0:T(8,128)(2,1)}), bf16[64,28,128]{2,1,0:T(8,128)(2,1)S(1)}, u32[]{:S(2)}, u32[]{:S(2)}) async-start(bf16[64,28,128]{2,1,0:T(8,128)(2,1)} %pad_maximum_fusion), calls=%async_computation | async-start | bytes 1048576 | tf_op jit(solution)/shard_map/all_to_all | solution.py:14
  18.1 0.0 copy-done.7
  18.1 8.2 %collective-permute-start.1 = (bf16[2,4,2,16,128]{4,3,2,1,0:T(8,128)(2,1)S(1)}, bf16[2,4,2,16,128]{4,3,2,1,0:T(8,128)(2,1)S(1)}, u32[]{:S(2)}, u32[]{:S(2)}) collective-permute-start(bf16[2,4,2,16,128]{4,3,2,1,0:T(8,128)(2,1)S(1)} %bitcast.59), channel_id=1, source_target_pairs={{0,1},{1,0},{2,3},{3,2},{4,5},{5,4},{6,7},{7,6},{8,9},{9,8},{10,11... | collective-permute-start | bytes 196616 | tf_op jit(solution)/shard_map/ppermute | solution.py:215
  26.3 1.9 %collective-permute-start = (bf16[2,4,2,16,128]{4,3,2,1,0:T(8,128)(2,1)S(1)}, bf16[2,4,2,16,128]{4,3,2,1,0:T(8,128)(2,1)S(1)}, u32[]{:S(2)}, u32[]{:S(2)}) collective-permute-start(bf16[2,4,2,16,128]{4,3,2,1,0:T(8,128)(2,1)S(1)} %bitcast.60), channel_id=1, source_target_pairs={{0,8},{8,16},{16,24},{24,32},{32,40},{40,48},{48,56},{56,64},{64,7... | collective-permute-start | bytes 196616 | tf_op jit(solution)/shard_map/ppermute | solution.py:219
  28.9 0.0 copy-start.2
  28.9 7.6 %collective-permute-done.1 = bf16[2,4,2,16,128]{4,3,2,1,0:T(8,128)(2,1)S(1)} collective-permute-done((bf16[2,4,2,16,128]{4,3,2,1,0:T(8,128)(2,1)S(1)}, bf16[2,4,2,16,128]{4,3,2,1,0:T(8,128)(2,1)S(1)}, u32[]{:S(2)}, u32[]{:S(2)}) %collective-permute-start.1) | collective-permute-done | bytes 65568 | tf_op jit(solution)/shard_map/ppermute | solution.py:215
  36.5 0.0 collective-permute-done
  36.5 16.0 %all-to-all-done.spread_ref = bf16[64,28,128]{2,1,0:T(8,128)(2,1)S(1)} async-done(((bf16[64,28,128]{2,1,0:T(8,128)(2,1)}), bf16[64,28,128]{2,1,0:T(8,128)(2,1)S(1)}, u32[]{:S(2)}, u32[]{:S(2)}) %all-to-all-start) | async-done | bytes 458784 | tf_op jit(solution)/shard_map/all_to_all | solution.py:14
  52.5 0.0 copy-done.1
  52.5 0.0 copy-done.2
  52.5 1.9 %mirror_pieces.1 = bf16[128,8,128]{2,1,0:T(8,128)(2,1)} custom-call(s32[64,64]{1,0:T(8,128)S(1)} %copy-done.1, s32[2]{0:T(128)S(1)} %copy-done.2, s32[1]{0:T(128)S(6)} %copy.14.shift_ref, s32[1]{0:T(128)} %bitcast.5.row_ref, bf16[64,28,128]{2,1,0:T(8,128)(2,1)S(1)} %all-to-all-done.spread_ref), custom_call_target="tpu_custom_call" | custom-call | bytes 1000000 | tf_op jit(solution)/shard_map/mirror_pieces/pallas_call | solution.py:41
  54.4 12.4 %all-to-all-start.1 = ((bf16[128,8,128]{2,1,0:T(8,128)(2,1)}), bf16[128,8,128]{2,1,0:T(8,128)(2,1)S(1)}, u32[]{:S(2)}, u32[]{:S(2)}) async-start(bf16[128,8,128]{2,1,0:T(8,128)(2,1)} %mirror_pieces.1), calls=%async_computation.1 | async-start | bytes 524288 | tf_op jit(solution)/shard_map/all_to_all | solution.py:244
  66.8 2.1 %collective-permute-start.2 = (bf16[2,4,2,16,128]{4,3,2,1,0:T(8,128)(2,1)S(1)}, bf16[2,4,2,16,128]{4,3,2,1,0:T(8,128)(2,1)S(1)}, u32[]{:S(2)}, u32[]{:S(2)}) collective-permute-start(bf16[2,4,2,16,128]{4,3,2,1,0:T(8,128)(2,1)S(1)} %collective-permute-done.1), channel_id=1, source_target_pairs={{0,8},{8,16},{16,24},{24,32},{32,40},{40,48},{48,56},{56,64},{64,7... | collective-permute-start | bytes 196616 | tf_op jit(solution)/shard_map/ppermute | solution.py:219
  68.8 2.2 %factor_pieces.1 = bf16[64,48,128]{2,1,0:T(8,128)(2,1)} custom-call(s32[64,64]{1,0:T(8,128)S(1)} %copy-done.1, s32[2]{0:T(128)S(1)} %copy-done.2, s32[1]{0:T(128)S(6)} %copy.14.shift_ref, bf16[64,28,128]{2,1,0:T(8,128)(2,1)S(1)} %all-to-all-done.spread_ref), custom_call_target="tpu_custom_call" | custom-call | bytes 1300000 | tf_op jit(solution)/shard_map/factor_pieces/pallas_call | solution.py:67
  71.1 1.4 collective-permute-done.2
  72.5 15.3 %all-to-all-done.1 = bf16[128,8,128]{2,1,0:T(8,128)(2,1)S(1)} async-done(((bf16[128,8,128]{2,1,0:T(8,128)(2,1)}), bf16[128,8,128]{2,1,0:T(8,128)(2,1)S(1)}, u32[]{:S(2)}, u32[]{:S(2)}) %all-to-all-start.1) | async-done | bytes 262176 | tf_op jit(solution)/shard_map/all_to_all | solution.py:244
  87.8 7.0 %all-to-all-start.2 = ((bf16[64,48,128]{2,1,0:T(8,128)(2,1)}), bf16[64,48,128]{2,1,0:T(8,128)(2,1)S(1)}, u32[]{:S(2)}, u32[]{:S(2)}) async-start(bf16[64,48,128]{2,1,0:T(8,128)(2,1)} %factor_pieces.1), calls=%async_computation.2 | async-start | bytes 1572864 | tf_op jit(solution)/shard_map/all_to_all | solution.py:14
  94.9 0.1 copy.7
  95.0 0.0 copy-start
  95.0 5.1 %collective-permute-start.5 = (bf16[4,2,16,16,128]{4,3,2,1,0:T(8,128)(2,1)S(1)}, bf16[4,2,16,16,128]{4,3,2,1,0:T(8,128)(2,1)S(1)}, u32[]{:S(2)}, u32[]{:S(2)}) collective-permute-start(bf16[4,2,16,16,128]{4,3,2,1,0:T(8,128)(2,1)S(1)} %pad_maximum_fusion.1.refs_0_), channel_id=1, source_target_pairs={{0,6},{1,7},{2,0},{3,1},{4,2},{5,3},{6,4},{7,5},{8,14},{9,15},{10,... | collective-permute-start | bytes 1572872 | tf_op jit(solution)/shard_map/ppermute | solution.py:209
  100.1 2.5 %collective-permute-start.4 = (bf16[4,2,16,16,128]{4,3,2,1,0:T(8,128)(2,1)S(1)}, bf16[4,2,16,16,128]{4,3,2,1,0:T(8,128)(2,1)S(1)}, u32[]{:S(2)}, u32[]{:S(2)}) collective-permute-start(bf16[4,2,16,16,128]{4,3,2,1,0:T(8,128)(2,1)S(1)} %pad_maximum_fusion.1.refs_0_), channel_id=1, source_target_pairs={{0,4},{1,5},{2,6},{3,7},{4,0},{5,1},{6,2},{7,3},{8,12},{9,13},{10,... | collective-permute-start | bytes 1572872 | tf_op jit(solution)/shard_map/ppermute | solution.py:209
  102.7 2.9 %collective-permute-start.3 = (bf16[4,2,16,16,128]{4,3,2,1,0:T(8,128)(2,1)S(1)}, bf16[4,2,16,16,128]{4,3,2,1,0:T(8,128)(2,1)S(1)}, u32[]{:S(2)}, u32[]{:S(2)}) collective-permute-start(bf16[4,2,16,16,128]{4,3,2,1,0:T(8,128)(2,1)S(1)} %pad_maximum_fusion.1.refs_0_), channel_id=1, source_target_pairs={{0,2},{1,3},{2,4},{3,5},{4,6},{5,7},{6,0},{7,1},{8,10},{9,11},{10,... | collective-permute-start | bytes 1572872 | tf_op jit(solution)/shard_map/ppermute | solution.py:209
  105.6 0.1 pad_add_fusion.place_ref
  105.7 17.2 %collective-permute-done.5.refs_3_ = bf16[4,2,16,16,128]{4,3,2,1,0:T(8,128)(2,1)S(1)} collective-permute-done((bf16[4,2,16,16,128]{4,3,2,1,0:T(8,128)(2,1)S(1)}, bf16[4,2,16,16,128]{4,3,2,1,0:T(8,128)(2,1)S(1)}, u32[]{:S(2)}, u32[]{:S(2)}) %collective-permute-start.5) | collective-permute-done | bytes 524320 | tf_op jit(solution)/shard_map/ppermute | solution.py:209
  122.8 0.0 collective-permute-done.4.refs_2_
  122.8 5.6 %collective-permute-done.3.refs_1_ = bf16[4,2,16,16,128]{4,3,2,1,0:T(8,128)(2,1)S(1)} collective-permute-done((bf16[4,2,16,16,128]{4,3,2,1,0:T(8,128)(2,1)S(1)}, bf16[4,2,16,16,128]{4,3,2,1,0:T(8,128)(2,1)S(1)}, u32[]{:S(2)}, u32[]{:S(2)}) %collective-permute-start.3) | collective-permute-done | bytes 524320 | tf_op jit(solution)/shard_map/ppermute | solution.py:209
  128.4 0.0 copy-done
  128.4 1.4 spin_adapted.1
  129.9 0.0 copy-start.3
  129.9 1.0 copy-done.3
  130.9 0.0 copy-start.5
  130.9 0.9 copy-done.5
  131.8 3.1 %all-to-all-done.2.other_ref = bf16[64,48,128]{2,1,0:T(8,128)(2,1)S(1)} async-done(((bf16[64,48,128]{2,1,0:T(8,128)(2,1)}), bf16[64,48,128]{2,1,0:T(8,128)(2,1)S(1)}, u32[]{:S(2)}, u32[]{:S(2)}) %all-to-all-start.2) | async-done | bytes 786464 | tf_op jit(solution)/shard_map/all_to_all | solution.py:14
  134.9 0.0 copy-start.4
  134.9 1.2 copy-done.4
  136.1 0.0 copy-start.6
  136.1 1.1 copy-done.6
  137.3 2.0 %ladder.1 = bf16[4,2,4,2,32,128]{5,4,3,2,1,0:T(8,128)(2,1)S(1)} custom-call(bf16[2,2,512,256]{3,2,1,0:T(8,128)(2,1)S(1)} %copy-done.4, bf16[256,1536]{1,0:T(8,128)(2,1)S(1)} %copy-done.6, bf16[64,48,128]{2,1,0:T(8,128)(2,1)S(1)} %all-to-all-done.2.other_ref), custom_call_target="tpu_custom_call" | custom-call | flops 1610612736 | bytes 2900000 | tf_op jit(solution)/shard_map/ladder/pallas_call | solution.py:186
  139.3 14.0 %all_to_all.20 = bf16[4,2,4,2,32,128]{5,4,3,2,1,0:T(8,128)(2,1)S(1)} all-to-all(bf16[4,2,4,2,32,128]{5,4,3,2,1,0:T(8,128)(2,1)S(1)} %ladder.1), channel_id=1, replica_groups={{0,2,4,6},{1,3,5,7},{8,10,12,14},{9,11,13,15},{16,18,20,22},{17,19,21,2..., dimensions={0} | all-to-all | bytes 1048576 | tf_op jit(solution)/shard_map/all_to_all | solution.py:263
  153.3 0.1 convert_reduce_fusion
  153.4 9.8 %collective-permute-start.6 = (bf16[2,4,2,16,128]{4,3,2,1,0:T(8,128)(2,1)S(1)}, bf16[2,4,2,16,128]{4,3,2,1,0:T(8,128)(2,1)S(1)}, u32[]{:S(2)}, u32[]{:S(2)}) collective-permute-start(bf16[2,4,2,16,128]{4,3,2,1,0:T(8,128)(2,1)S(1)} %fusion.3), channel_id=1, source_target_pairs={{0,1},{1,0},{2,3},{3,2},{4,5},{5,4},{6,7},{7,6},{8,9},{9,8},{10,11... | collective-permute-start | bytes 196616 | tf_op jit(solution)/shard_map/ppermute | solution.py:215
  163.1 8.8 %collective-permute-done.6 = bf16[2,4,2,16,128]{4,3,2,1,0:T(8,128)(2,1)S(1)} collective-permute-done((bf16[2,4,2,16,128]{4,3,2,1,0:T(8,128)(2,1)S(1)}, bf16[2,4,2,16,128]{4,3,2,1,0:T(8,128)(2,1)S(1)}, u32[]{:S(2)}, u32[]{:S(2)}) %collective-permute-start.6) | collective-permute-done | bytes 65568 | tf_op jit(solution)/shard_map/ppermute | solution.py:215
  172.0 0.7 fusion.4
  (3 shorter events, 0.1 us)
Async XLA Ops:
  1.9 16.2 %copy-start.7 = (bf16[2,1,4,2,16,128]{5,4,3,2,1,0:T(8,128)(2,1)S(1)}, bf16[2,1,4,2,16,128]{5,4,3,2,1,0:T(8,128)(2,1)}, u32[]{:S(2)}) copy-start(bf16[2,1,4,2,16,128]{5,4,3,2,1,0:T(8,128)(2,1)} %param.5) | copy-start | bytes 196612
  1.9 50.6 %copy-start.1 = (s32[64,64]{1,0:T(8,128)S(1)}, s32[64,64]{1,0:T(8,128)}, u32[]{:S(2)}) copy-start(s32[64,64]{1,0:T(8,128)} %kminus_ref.3) | copy-start | bytes 49156
  1.9 50.6 %all-to-all-start = ((bf16[64,28,128]{2,1,0:T(8,128)(2,1)}), bf16[64,28,128]{2,1,0:T(8,128)(2,1)S(1)}, u32[]{:S(2)}, u32[]{:S(2)}) async-start(bf16[64,28,128]{2,1,0:T(8,128)(2,1)} %pad_maximum_fusion), calls=%async_computation | async-start | bytes 1048576 | tf_op jit(solution)/shard_map/all_to_all | solution.py:14
  18.1 18.4 %collective-permute-start.1 = (bf16[2,4,2,16,128]{4,3,2,1,0:T(8,128)(2,1)S(1)}, bf16[2,4,2,16,128]{4,3,2,1,0:T(8,128)(2,1)S(1)}, u32[]{:S(2)}, u32[]{:S(2)}) collective-permute-start(bf16[2,4,2,16,128]{4,3,2,1,0:T(8,128)(2,1)S(1)} %bitcast.59), channel_id=1, source_target_pairs={{0,1},{1,0},{2,3},{3,2},{4,5},{5,4},{6,7},{7,6},{8,9},{9,8},{10,11... | collective-permute-start | bytes 196616 | tf_op jit(solution)/shard_map/ppermute | solution.py:215
  26.3 10.2 %collective-permute-start = (bf16[2,4,2,16,128]{4,3,2,1,0:T(8,128)(2,1)S(1)}, bf16[2,4,2,16,128]{4,3,2,1,0:T(8,128)(2,1)S(1)}, u32[]{:S(2)}, u32[]{:S(2)}) collective-permute-start(bf16[2,4,2,16,128]{4,3,2,1,0:T(8,128)(2,1)S(1)} %bitcast.60), channel_id=1, source_target_pairs={{0,8},{8,16},{16,24},{24,32},{32,40},{40,48},{48,56},{56,64},{64,7... | collective-permute-start | bytes 196616 | tf_op jit(solution)/shard_map/ppermute | solution.py:219
  28.9 23.6 %copy-start.2 = (s32[2]{0:T(128)S(1)}, s32[2]{0:T(128)}, u32[]{:S(2)}) copy-start(s32[2]{0:T(128)} %rows_ref.3) | copy-start | bytes 28
  54.4 33.5 %all-to-all-start.1 = ((bf16[128,8,128]{2,1,0:T(8,128)(2,1)}), bf16[128,8,128]{2,1,0:T(8,128)(2,1)S(1)}, u32[]{:S(2)}, u32[]{:S(2)}) async-start(bf16[128,8,128]{2,1,0:T(8,128)(2,1)} %mirror_pieces.1), calls=%async_computation.1 | async-start | bytes 524288 | tf_op jit(solution)/shard_map/all_to_all | solution.py:244
  66.8 5.7 %collective-permute-start.2 = (bf16[2,4,2,16,128]{4,3,2,1,0:T(8,128)(2,1)S(1)}, bf16[2,4,2,16,128]{4,3,2,1,0:T(8,128)(2,1)S(1)}, u32[]{:S(2)}, u32[]{:S(2)}) collective-permute-start(bf16[2,4,2,16,128]{4,3,2,1,0:T(8,128)(2,1)S(1)} %collective-permute-done.1), channel_id=1, source_target_pairs={{0,8},{8,16},{16,24},{24,32},{32,40},{40,48},{48,56},{56,64},{64,7... | collective-permute-start | bytes 196616 | tf_op jit(solution)/shard_map/ppermute | solution.py:219
  87.8 47.1 %all-to-all-start.2 = ((bf16[64,48,128]{2,1,0:T(8,128)(2,1)}), bf16[64,48,128]{2,1,0:T(8,128)(2,1)S(1)}, u32[]{:S(2)}, u32[]{:S(2)}) async-start(bf16[64,48,128]{2,1,0:T(8,128)(2,1)} %factor_pieces.1), calls=%async_computation.2 | async-start | bytes 1572864 | tf_op jit(solution)/shard_map/all_to_all | solution.py:14
  95.0 33.5 %copy-start = (bf16[2,1,2,3,128,128]{5,4,3,2,1,0:T(8,128)(2,1)S(1)}, bf16[2,1,2,3,128,128]{5,4,3,2,1,0:T(8,128)(2,1)}, u32[]{:S(2)}) copy-start(bf16[2,1,2,3,128,128]{5,4,3,2,1,0:T(8,128)(2,1)} %param.6) | copy-start | bytes 1179652
  95.0 27.8 %collective-permute-start.5 = (bf16[4,2,16,16,128]{4,3,2,1,0:T(8,128)(2,1)S(1)}, bf16[4,2,16,16,128]{4,3,2,1,0:T(8,128)(2,1)S(1)}, u32[]{:S(2)}, u32[]{:S(2)}) collective-permute-start(bf16[4,2,16,16,128]{4,3,2,1,0:T(8,128)(2,1)S(1)} %pad_maximum_fusion.1.refs_0_), channel_id=1, source_target_pairs={{0,6},{1,7},{2,0},{3,1},{4,2},{5,3},{6,4},{7,5},{8,14},{9,15},{10,... | collective-permute-start | bytes 1572872 | tf_op jit(solution)/shard_map/ppermute | solution.py:209
  100.1 22.7 %collective-permute-start.4 = (bf16[4,2,16,16,128]{4,3,2,1,0:T(8,128)(2,1)S(1)}, bf16[4,2,16,16,128]{4,3,2,1,0:T(8,128)(2,1)S(1)}, u32[]{:S(2)}, u32[]{:S(2)}) collective-permute-start(bf16[4,2,16,16,128]{4,3,2,1,0:T(8,128)(2,1)S(1)} %pad_maximum_fusion.1.refs_0_), channel_id=1, source_target_pairs={{0,4},{1,5},{2,6},{3,7},{4,0},{5,1},{6,2},{7,3},{8,12},{9,13},{10,... | collective-permute-start | bytes 1572872 | tf_op jit(solution)/shard_map/ppermute | solution.py:209
  102.7 25.8 %collective-permute-start.3 = (bf16[4,2,16,16,128]{4,3,2,1,0:T(8,128)(2,1)S(1)}, bf16[4,2,16,16,128]{4,3,2,1,0:T(8,128)(2,1)S(1)}, u32[]{:S(2)}, u32[]{:S(2)}) collective-permute-start(bf16[4,2,16,16,128]{4,3,2,1,0:T(8,128)(2,1)S(1)} %pad_maximum_fusion.1.refs_0_), channel_id=1, source_target_pairs={{0,2},{1,3},{2,4},{3,5},{4,6},{5,7},{6,0},{7,1},{8,10},{9,11},{10,... | collective-permute-start | bytes 1572872 | tf_op jit(solution)/shard_map/ppermute | solution.py:209
  129.9 1.0 copy-start.3
  130.9 0.9 copy-start.5
  134.9 1.2 copy-start.4
  136.1 1.1 copy-start.6
  153.4 18.6 %collective-permute-start.6 = (bf16[2,4,2,16,128]{4,3,2,1,0:T(8,128)(2,1)S(1)}, bf16[2,4,2,16,128]{4,3,2,1,0:T(8,128)(2,1)S(1)}, u32[]{:S(2)}, u32[]{:S(2)}) collective-permute-start(bf16[2,4,2,16,128]{4,3,2,1,0:T(8,128)(2,1)S(1)} %fusion.3), channel_id=1, source_target_pairs={{0,1},{1,0},{2,3},{3,2},{4,5},{5,4},{6,7},{7,6},{8,9},{9,8},{10,11... | collective-permute-start | bytes 196616 | tf_op jit(solution)/shard_map/ppermute | solution.py:215

commit v3 on v2

v3 whole, which is shorter than its diff:
```python
import jax
import jax.numpy as jnp
from jax import lax
from jax.experimental import pallas as pl
from jax.experimental.pallas import tpu as pltpu
from jax.sharding import PartitionSpec as P

SMEM = pl.BlockSpec(memory_space=pltpu.SMEM)
VMEM = pl.BlockSpec(memory_space=pltpu.VMEM)
ANY = pl.BlockSpec(memory_space=pl.ANY)


def params(mebibytes):
    return pltpu.CompilerParams(vmem_limit_bytes=mebibytes * 1024 * 1024)


def wide(value):
    return value.astype(jnp.float32)


def exchange(value):
    return lax.all_to_all(value, "ka", split_axis=0, concat_axis=0, tiled=True)


def exchange_both(value):
    groups = [[k * 8 + 2 * y + h for h in range(2) for k in range(64)] for y in range(4)]
    return lax.all_to_all(
        value, ("ka", "vert"), split_axis=0, concat_axis=0, tiled=True, axis_index_groups=groups
    )


def mirror_kernel(kminus_ref, rows_ref, shift_ref, row_ref, spread_ref, out_ref):
    target = kminus_ref[rows_ref[row_ref[0]], shift_ref[0]]
    before = spread_ref[kminus_ref[target, 63], 6]
    for k in range(64):
        piece = spread_ref[kminus_ref[target, k], 6]
        for high in range(2):
            out_ref[high * 64 + k, 0] = piece
            out_ref[high * 64 + k, 1] = before
        before = piece


def mirror_pieces(lookup, row, spread):
    return pl.pallas_call(
        mirror_kernel,
        out_shape=jax.ShapeDtypeStruct((128, 2, 4, 128), jnp.bfloat16),
        in_specs=[SMEM] * 4 + [VMEM],
        out_specs=VMEM,
        compiler_params=params(12),
        cost_estimate=pl.CostEstimate(flops=0, bytes_accessed=700000, transcendentals=0),
        name="mirror_pieces",
    )(*lookup, row, spread)


def factor_kernel(kminus_ref, rows_ref, shift_ref, spread_ref, out_ref):
    for row in range(2):
        target = kminus_ref[rows_ref[row], shift_ref[0]]
        for k in range(64):
            out_ref[k, row * 6 : row * 6 + 6] = spread_ref[kminus_ref[target, k], 0:6]


def factor_pieces(lookup, spread):
    return pl.pallas_call(
        factor_kernel,
        out_shape=jax.ShapeDtypeStruct((64, 12, 4, 128), jnp.bfloat16),
        in_specs=[SMEM] * 3 + [VMEM],
        out_specs=VMEM,
        compiler_params=params(12),
        cost_estimate=pl.CostEstimate(flops=0, bytes_accessed=1300000, transcendentals=0),
        name="factor_pieces",
    )(*lookup, spread)


def complex_matrix(real, imag):
    return jnp.concatenate(
        [jnp.concatenate([real, -imag], 1), jnp.concatenate([imag, real], 1)], 0
    )


def ladder_kernel(place_ref, *refs):
    turns = refs[0:4]
    factor_ref, other_ref, out_ref, blocks, left, right, inner, arrived = refs[4:12]
    copies = []
    for turn in range(4):
        for high in range(2):
            start = pl.multiple_of(place_ref[turn] + high * 16, 16)
            copies.append(
                pltpu.make_async_copy(
                    turns[turn].at[:, high],
                    blocks.at[:, :, pl.ds(start, 16), :],
                    arrived.at[turn * 2 + high],
                )
            )
    for copy in copies:
        copy.start()
    for step in range(2):
        for lane in range(3):
            at = (step * 3 + lane) * 256
            left[:, at : at + 256] = complex_matrix(
                factor_ref[step, 0, lane], factor_ref[step, 1, lane]
            )
    for copy in copies:
        copy.wait()
    for row in range(2):
        other = jnp.concatenate(
            [wide(other_ref[m])[row * 24 : (row + 1) * 24] for m in range(64)], 0
        ).astype(jnp.bfloat16)
        for step in range(2):
            for lane in range(3):
                real = (step * 6 + lane) * 128
                imag = real + 384
                right[lane * 256 : (lane + 1) * 256, :] = complex_matrix(
                    other[real : real + 128], other[imag : imag + 128]
                )
            tilde = []
            for occ in range(4):
                parts = []
                for part in range(2):
                    block = (row * 4 + occ) * 2 + part
                    flipped = jnp.transpose(wide(blocks[2 + step, block]))
                    value = 2.0 * wide(blocks[step, block]) - flipped
                    parts.append(value.astype(jnp.bfloat16))
                tilde.append(jnp.concatenate(parts, 1))
            product = lax.dot_general(
                jnp.concatenate(tilde, 0),
                right[...],
                (((1,), (1,)), ((), ())),
                preferred_element_type=jnp.float32,
            ).astype(jnp.bfloat16)
            for lane in range(3):
                for part in range(2):
                    at = (step * 3 + lane) * 256 + part * 128
                    column = lane * 256 + part * 128
                    for occ in range(4):
                        inner[at : at + 128, occ * 128 : (occ + 1) * 128] = product[
                            occ * 128 : (occ + 1) * 128, column : column + 128
                        ]
        total = jnp.dot(left[...], inner[...], preferred_element_type=jnp.float32)
        total = total.astype(jnp.bfloat16)
        for occ in range(4):
            for part in range(2):
                for place in range(4):
                    at = part * 128 + place * 32
                    out_ref[place, row, occ, part] = total[
                        at : at + 32, occ * 128 : (occ + 1) * 128
                    ]


def ladder(place, turns, factor, other):
    return pl.pallas_call(
        ladder_kernel,
        out_shape=jax.ShapeDtypeStruct((4, 2, 4, 2, 32, 128), jnp.bfloat16),
        in_specs=[SMEM] + [ANY] * 4 + [VMEM, VMEM],
        out_specs=VMEM,
        scratch_shapes=[
            pltpu.VMEM((4, 16, 128, 128), jnp.bfloat16),
            pltpu.VMEM((256, 1536), jnp.bfloat16),
            pltpu.VMEM((768, 256), jnp.bfloat16),
            pltpu.VMEM((1536, 512), jnp.bfloat16),
            pltpu.SemaphoreType.DMA((8,)),
        ],
        compiler_params=params(16),
        cost_estimate=pl.CostEstimate(
            flops=1610612736, bytes_accessed=4000000, transcendentals=0
        ),
        name="ladder",
    )(place, *turns, factor, other)


def turned(value):
    return [value] + [
        lax.ppermute(value, "vert", [(v, (v + 2 * turn) % 8) for v in range(8)])
        for turn in range(1, 4)
    ]


def swapped(value):
    return lax.ppermute(value, "vert", [(v, v ^ 1) for v in range(8)])


def ahead(value):
    return lax.ppermute(value, "ka", [(k, (k + 1) % 64) for k in range(64)])


def per_device(amplitudes, factors, kminus, kj_rows, kshift):
    vert = lax.axis_index("vert")
    high = lax.rem(vert, 2)
    level = lax.div(vert, 2)
    lookup = (kminus, kj_rows, kshift)
    place = jnp.stack([lax.rem(level + 4 - turn, 4) * 32 for turn in range(4)]).astype(jnp.int32)

    row = lax.div(lax.axis_index("ka"), 32).astype(jnp.int32).reshape(1)

    shard = amplitudes[:, 0]
    spread = exchange(
        jnp.concatenate([factors[:, 0].reshape(64, 6, 4, 128), shard.reshape(64, 1, 4, 128)], 1)
    )
    behind = ahead(shard)
    other_half = swapped(shard)
    spread, behind, other_half = lax.optimization_barrier((spread, behind, other_half))

    mirror = exchange_both(mirror_pieces(lookup, row, spread))
    here = jnp.stack([shard, behind]).reshape(2, 16, 16, 128)
    there = jnp.stack([other_half, ahead(other_half)]).reshape(2, 16, 16, 128)
    own = jnp.where(
        high == 0, jnp.stack([here, there], axis=1), jnp.stack([there, here], axis=1)
    )
    chosen = factor_pieces(lookup, spread)
    mirror, own, chosen = lax.optimization_barrier((mirror, own, chosen))

    other = exchange(chosen.reshape(64, 48, 128))
    mirror = jnp.transpose(mirror.reshape(2, 64, 2, 4, 128), (2, 0, 1, 3, 4))
    turns = turned(jnp.concatenate([own, mirror.reshape(2, 2, 16, 16, 128)]))
    partial = ladder(place, turns, factors[:, 0], other)

    groups = [[0, 2, 4, 6], [1, 3, 5, 7]]
    pieces = lax.all_to_all(
        partial, "vert", split_axis=0, concat_axis=0, tiled=True, axis_index_groups=groups
    )
    total = jnp.sum(pieces.astype(jnp.float32), 0).reshape(2, 4, 2, 2, 16, 128)
    keep = jnp.where(high == 0, total[:, :, :, 0], total[:, :, :, 1])
    give = jnp.where(high == 0, total[:, :, :, 1], total[:, :, :, 0]).astype(jnp.bfloat16)
    taken = swapped(give)
    total = (keep + taken.astype(jnp.float32)).astype(jnp.bfloat16)
    return total[:, None]


def solution(mesh):
    in_specs = (
        P(None, "ka", None, None, "vert", None),
        P(None, "ka", None, "vert", None, None),
        P(),
        P(),
        P(),
    )
    out_specs = P(None, "ka", None, None, "vert", None)
    return jax.shard_map(
        per_device, mesh=mesh, in_specs=in_specs, out_specs=out_specs, check_vma=False
    )
```

time: 173 us -> 167 us (0.965)
  local copies, waits for them, and re-layouts: 4.34 us -> 0.11 us
    unnamed x16 -> x8, local copies, waits for them, and re-layouts: 4.25 us -> 0.02 us
    ppermute x2, waiting for transfers between devices: 16.4 us -> 13.3 us  [swapped(): return lax.ppermute(value, 'vert', [(v, v ^ 1) for v in range(8)])]
    all_to_all x3, waiting for transfers between devices: 34.5 us -> 36.2 us  [the longest x2 20.9 us: exchange(): return lax.all_to_all(value, 'ka', split_axis=0, concat_axis=0, tiled=True)]
    pallas_call x3 -> x2, Pallas kernels: 5.53 us -> 4.04 us  [the longest x1 2.15 us: factor_pieces(): pl.pallas_call(factor_kernel, out_shape=jax.ShapeDtypeStruct((64, 12, 4,...]
  transfers between devices with their start and end apart: 10 -> 10, of which waited for: 8 -> 8; matrix products, arithmetic and copies ran while one was open for 0% -> 0% of each run, Pallas kernels for 2% -> 1%
where the time goes in v3:
time: 167 us
  waiting for transfers between devices  73.8 us (44%)
  starting transfers between devices  68 us (41%)
  blocking collectives  14 us (8%)
  Pallas kernels  6.87 us (4%)
  other arithmetic  3.01 us (2%)
    all_to_all x2, starting transfers between devices, exchange(): return lax.all_to_all(value, 'ka', split_axis=0, concat_axis=0, tiled=True)  23.2 us
    ppermute x3, waiting for transfers between devices, turned(): lax.ppermute(value, 'vert', [(v, (v + 2 * turn) % 8) for v in range(8)])  22.8 us
    all_to_all x2, waiting for transfers between devices, exchange(): return lax.all_to_all(value, 'ka', split_axis=0, concat_axis=0, tiled=True)  20.9 us
    ppermute x2, starting transfers between devices, swapped(): return lax.ppermute(value, 'vert', [(v, v ^ 1) for v in range(8)])  18 us
    all_to_all x1, waiting for transfers between devices, exchange_both(): lax.all_to_all(value, ('ka', 'vert'), split_axis=0, concat_axis=0, tiled=...  15.3 us
    all_to_all x1, blocking collectives, per_device(): lax.all_to_all(partial, 'vert', split_axis=0, concat_axis=0, tiled=True,...  14 us
    ppermute x2, waiting for transfers between devices, swapped(): return lax.ppermute(value, 'vert', [(v, v ^ 1) for v in range(8)])  13.3 us
    all_to_all x1, starting transfers between devices, exchange_both(): lax.all_to_all(value, ('ka', 'vert'), split_axis=0, concat_axis=0, tiled=...  12.4 us
  transfers between devices with their start and end apart: 10, of which 8 were waited for; matrix products, arithmetic and copies ran while one was open for 0% of the time, Pallas kernels for 1%

profile of v3, /device:TPU:4, one launch (start us, length us, event | category | flops | bytes accessed | tf_op | source)
XLA Modules:
  0.0 166.7 jit_solution(19676788748776330)
XLA Ops:
  0.0 2.1 %pad_maximum_fusion.1 = bf16[64,7,4,128]{3,2,1,0:T(4,128)(2,1)} fusion(bf16[64,1,4,128]{3,2,1,0:T(4,128)(2,1)} %bitcast.59, bf16[64,6,4,128]{3,2,1,0:T(4,128)(2,1)} %bitcast.53), kind=kLoop, calls=%fused_computation.2 | loop fusion | flops 229376 | bytes 917504 | tf_op jit(solution)/shard_map/concatenate | solution.py:196
  2.1 0.0 copy-start.3
  2.1 0.0 copy-start.1
  2.1 16.2 %all-to-all-start = ((bf16[64,7,4,128]{3,2,1,0:T(4,128)(2,1)}), bf16[64,7,4,128]{3,2,1,0:T(4,128)(2,1)S(1)}, u32[]{:S(2)}, u32[]{:S(2)}) async-start(bf16[64,7,4,128]{3,2,1,0:T(4,128)(2,1)} %pad_maximum_fusion.1), calls=%async_computation | async-start | bytes 917504 | tf_op jit(solution)/shard_map/all_to_all | solution.py:22
  18.3 0.0 copy-done.3
  18.3 8.2 %collective-permute-start.1 = (bf16[2,4,2,16,128]{4,3,2,1,0:T(8,128)(2,1)S(1)}, bf16[2,4,2,16,128]{4,3,2,1,0:T(8,128)(2,1)S(1)}, u32[]{:S(2)}, u32[]{:S(2)}) collective-permute-start(bf16[2,4,2,16,128]{4,3,2,1,0:T(8,128)(2,1)S(1)} %bitcast.60), channel_id=1, source_target_pairs={{0,1},{1,0},{2,3},{3,2},{4,5},{5,4},{6,7},{7,6},{8,9},{9,8},{10,11... | collective-permute-start | bytes 196616 | tf_op jit(solution)/shard_map/ppermute | solution.py:178
  26.5 1.9 %collective-permute-start = (bf16[2,4,2,16,128]{4,3,2,1,0:T(8,128)(2,1)S(1)}, bf16[2,4,2,16,128]{4,3,2,1,0:T(8,128)(2,1)S(1)}, u32[]{:S(2)}, u32[]{:S(2)}) collective-permute-start(bf16[2,4,2,16,128]{4,3,2,1,0:T(8,128)(2,1)S(1)} %bitcast.61), channel_id=1, source_target_pairs={{0,8},{8,16},{16,24},{24,32},{32,40},{40,48},{48,56},{56,64},{64,7... | collective-permute-start | bytes 196616 | tf_op jit(solution)/shard_map/ppermute | solution.py:182
  29.1 0.0 copy-start.2
  29.1 6.3 %collective-permute-done.1 = bf16[2,4,2,16,128]{4,3,2,1,0:T(8,128)(2,1)S(1)} collective-permute-done((bf16[2,4,2,16,128]{4,3,2,1,0:T(8,128)(2,1)S(1)}, bf16[2,4,2,16,128]{4,3,2,1,0:T(8,128)(2,1)S(1)}, u32[]{:S(2)}, u32[]{:S(2)}) %collective-permute-start.1) | collective-permute-done | bytes 65568 | tf_op jit(solution)/shard_map/ppermute | solution.py:178
  35.5 0.0 collective-permute-done
  35.5 14.4 %all-to-all-done.spread_ref = bf16[64,7,4,128]{3,2,1,0:T(4,128)(2,1)S(1)} async-done(((bf16[64,7,4,128]{3,2,1,0:T(4,128)(2,1)}), bf16[64,7,4,128]{3,2,1,0:T(4,128)(2,1)S(1)}, u32[]{:S(2)}, u32[]{:S(2)}) %all-to-all-start) | async-done | bytes 458784 | tf_op jit(solution)/shard_map/all_to_all | solution.py:22
  49.9 0.0 copy-done.1
  49.9 0.0 copy-done.2
  49.9 1.9 %mirror_pieces.1 = bf16[128,2,4,128]{3,2,1,0:T(4,128)(2,1)} custom-call(s32[64,64]{1,0:T(8,128)S(1)} %copy-done.1, s32[2]{0:T(128)S(1)} %copy-done.2, s32[1]{0:T(128)S(6)} %copy.14.shift_ref, s32[1]{0:T(128)} %bitcast.4.row_ref, bf16[64,7,4,128]{3,2,1,0:T(4,128)(2,1)S(1)} %all-to-all-done.spread_ref), custom_call_target="tpu_custom_call" | custom-call | bytes 700000 | tf_op jit(solution)/shard_map/mirror_pieces/pallas_call | solution.py:44
  51.8 12.4 %all-to-all-start.1 = ((bf16[128,2,4,128]{3,2,1,0:T(4,128)(2,1)}), bf16[128,2,4,128]{3,2,1,0:T(4,128)(2,1)S(1)}, u32[]{:S(2)}, u32[]{:S(2)}) async-start(bf16[128,2,4,128]{3,2,1,0:T(4,128)(2,1)} %mirror_pieces.1), calls=%async_computation.1 | async-start | bytes 524288 | tf_op jit(solution)/shard_map/all_to_all | solution.py:27
  64.2 2.1 %collective-permute-start.2 = (bf16[2,4,2,16,128]{4,3,2,1,0:T(8,128)(2,1)S(1)}, bf16[2,4,2,16,128]{4,3,2,1,0:T(8,128)(2,1)S(1)}, u32[]{:S(2)}, u32[]{:S(2)}) collective-permute-start(bf16[2,4,2,16,128]{4,3,2,1,0:T(8,128)(2,1)S(1)} %collective-permute-done.1), channel_id=1, source_target_pairs={{0,8},{8,16},{16,24},{24,32},{32,40},{40,48},{48,56},{56,64},{64,7... | collective-permute-start | bytes 196616 | tf_op jit(solution)/shard_map/ppermute | solution.py:182
  66.3 2.1 %factor_pieces.1 = bf16[64,12,4,128]{3,2,1,0:T(4,128)(2,1)} custom-call(s32[64,64]{1,0:T(8,128)S(1)} %copy-done.1, s32[2]{0:T(128)S(1)} %copy-done.2, s32[1]{0:T(128)S(6)} %copy.14.shift_ref, bf16[64,7,4,128]{3,2,1,0:T(4,128)(2,1)S(1)} %all-to-all-done.spread_ref), custom_call_target="tpu_custom_call" | custom-call | bytes 1300000 | tf_op jit(solution)/shard_map/factor_pieces/pallas_call | solution.py:63
  68.5 1.5 collective-permute-done.2
  70.0 15.3 %all-to-all-done.1 = bf16[128,2,4,128]{3,2,1,0:T(4,128)(2,1)S(1)} async-done(((bf16[128,2,4,128]{3,2,1,0:T(4,128)(2,1)}), bf16[128,2,4,128]{3,2,1,0:T(4,128)(2,1)S(1)}, u32[]{:S(2)}, u32[]{:S(2)}) %all-to-all-start.1) | async-done | bytes 262176 | tf_op jit(solution)/shard_map/all_to_all | solution.py:27
  85.3 7.0 %all-to-all-start.2 = ((bf16[64,48,128]{2,1,0:T(8,128)(2,1)}), bf16[64,48,128]{2,1,0:T(8,128)(2,1)S(1)}, u32[]{:S(2)}, u32[]{:S(2)}) async-start(bf16[64,48,128]{2,1,0:T(8,128)(2,1)} %bitcast.16), calls=%async_computation.2 | async-start | bytes 1572864 | tf_op jit(solution)/shard_map/all_to_all | solution.py:22
  92.4 0.1 copy.7
  92.5 0.0 copy-start
  92.5 5.1 %collective-permute-start.5 = (bf16[4,2,16,16,128]{4,3,2,1,0:T(8,128)(2,1)S(1)}, bf16[4,2,16,16,128]{4,3,2,1,0:T(8,128)(2,1)S(1)}, u32[]{:S(2)}, u32[]{:S(2)}) collective-permute-start(bf16[4,2,16,16,128]{4,3,2,1,0:T(8,128)(2,1)S(1)} %pad_maximum_fusion.refs_0_), channel_id=1, source_target_pairs={{0,6},{1,7},{2,0},{3,1},{4,2},{5,3},{6,4},{7,5},{8,14},{9,15},{10,... | collective-permute-start | bytes 1572872 | tf_op jit(solution)/shard_map/ppermute | solution.py:172
  97.6 2.5 %collective-permute-start.4 = (bf16[4,2,16,16,128]{4,3,2,1,0:T(8,128)(2,1)S(1)}, bf16[4,2,16,16,128]{4,3,2,1,0:T(8,128)(2,1)S(1)}, u32[]{:S(2)}, u32[]{:S(2)}) collective-permute-start(bf16[4,2,16,16,128]{4,3,2,1,0:T(8,128)(2,1)S(1)} %pad_maximum_fusion.refs_0_), channel_id=1, source_target_pairs={{0,4},{1,5},{2,6},{3,7},{4,0},{5,1},{6,2},{7,3},{8,12},{9,13},{10,... | collective-permute-start | bytes 1572872 | tf_op jit(solution)/shard_map/ppermute | solution.py:172
  100.1 2.9 %collective-permute-start.3 = (bf16[4,2,16,16,128]{4,3,2,1,0:T(8,128)(2,1)S(1)}, bf16[4,2,16,16,128]{4,3,2,1,0:T(8,128)(2,1)S(1)}, u32[]{:S(2)}, u32[]{:S(2)}) collective-permute-start(bf16[4,2,16,16,128]{4,3,2,1,0:T(8,128)(2,1)S(1)} %pad_maximum_fusion.refs_0_), channel_id=1, source_target_pairs={{0,2},{1,3},{2,4},{3,5},{4,6},{5,7},{6,0},{7,1},{8,10},{9,11},{10,... | collective-permute-start | bytes 1572872 | tf_op jit(solution)/shard_map/ppermute | solution.py:172
  103.1 0.1 pad_add_fusion.place_ref
  103.1 17.2 %collective-permute-done.5.refs_3_ = bf16[4,2,16,16,128]{4,3,2,1,0:T(8,128)(2,1)S(1)} collective-permute-done((bf16[4,2,16,16,128]{4,3,2,1,0:T(8,128)(2,1)S(1)}, bf16[4,2,16,16,128]{4,3,2,1,0:T(8,128)(2,1)S(1)}, u32[]{:S(2)}, u32[]{:S(2)}) %collective-permute-start.5) | collective-permute-done | bytes 524320 | tf_op jit(solution)/shard_map/ppermute | solution.py:172
  120.3 0.0 collective-permute-done.4.refs_2_
  120.3 5.6 %collective-permute-done.3.refs_1_ = bf16[4,2,16,16,128]{4,3,2,1,0:T(8,128)(2,1)S(1)} collective-permute-done((bf16[4,2,16,16,128]{4,3,2,1,0:T(8,128)(2,1)S(1)}, bf16[4,2,16,16,128]{4,3,2,1,0:T(8,128)(2,1)S(1)}, u32[]{:S(2)}, u32[]{:S(2)}) %collective-permute-start.3) | collective-permute-done | bytes 524320 | tf_op jit(solution)/shard_map/ppermute | solution.py:172
  125.9 6.5 %all-to-all-done.2.refs_5_ = bf16[64,48,128]{2,1,0:T(8,128)(2,1)S(1)} async-done(((bf16[64,48,128]{2,1,0:T(8,128)(2,1)}), bf16[64,48,128]{2,1,0:T(8,128)(2,1)S(1)}, u32[]{:S(2)}, u32[]{:S(2)}) %all-to-all-start.2) | async-done | bytes 786464 | tf_op jit(solution)/shard_map/all_to_all | solution.py:22
  132.4 0.0 copy-done
  132.4 2.8 %ladder.1 = bf16[4,2,4,2,32,128]{5,4,3,2,1,0:T(8,128)(2,1)S(1)} custom-call(s32[4]{0:T(128)S(1)} %pad_add_fusion.place_ref, bf16[4,2,16,16,128]{4,3,2,1,0:T(8,128)(2,1)S(1)} %pad_maximum_fusion.refs_0_, bf16[4,2,16,16,128]{4,3,2,1,0:T(8,128)(2,1)S(1)} %collective-permute-done.3.refs_1_, bf16[4,2,16,16,128]{4,3,2,1,0:T(8,128)(2,1)S(1)} %collective-permute-done.4.refs_2_, ...), custom_call_target="tpu_custom_call" | custom-call | flops 1610612736 | bytes 4000000 | tf_op jit(solution)/shard_map/ladder/pallas_call | solution.py:150
  135.2 14.0 %all_to_all.20 = bf16[4,2,4,2,32,128]{5,4,3,2,1,0:T(8,128)(2,1)S(1)} all-to-all(bf16[4,2,4,2,32,128]{5,4,3,2,1,0:T(8,128)(2,1)S(1)} %ladder.1), channel_id=1, replica_groups={{0,2,4,6},{1,3,5,7},{8,10,12,14},{9,11,13,15},{16,18,20,22},{17,19,21,2..., dimensions={0} | all-to-all | bytes 1048576 | tf_op jit(solution)/shard_map/all_to_all | solution.py:217
  149.2 0.1 convert_reduce_fusion
  149.3 9.7 %collective-permute-start.6 = (bf16[2,4,2,16,128]{4,3,2,1,0:T(8,128)(2,1)S(1)}, bf16[2,4,2,16,128]{4,3,2,1,0:T(8,128)(2,1)S(1)}, u32[]{:S(2)}, u32[]{:S(2)}) collective-permute-start(bf16[2,4,2,16,128]{4,3,2,1,0:T(8,128)(2,1)S(1)} %fusion.3), channel_id=1, source_target_pairs={{0,1},{1,0},{2,3},{3,2},{4,5},{5,4},{6,7},{7,6},{8,9},{9,8},{10,11... | collective-permute-start | bytes 196616 | tf_op jit(solution)/shard_map/ppermute | solution.py:178
  159.1 7.0 %collective-permute-done.6 = bf16[2,4,2,16,128]{4,3,2,1,0:T(8,128)(2,1)S(1)} collective-permute-done((bf16[2,4,2,16,128]{4,3,2,1,0:T(8,128)(2,1)S(1)}, bf16[2,4,2,16,128]{4,3,2,1,0:T(8,128)(2,1)S(1)}, u32[]{:S(2)}, u32[]{:S(2)}) %collective-permute-start.6) | collective-permute-done | bytes 65568 | tf_op jit(solution)/shard_map/ppermute | solution.py:178
  166.0 0.7 fusion.4
  (3 shorter events, 0.1 us)
Async XLA Ops:
  2.1 16.2 %copy-start.3 = (bf16[2,1,4,2,16,128]{5,4,3,2,1,0:T(8,128)(2,1)S(1)}, bf16[2,1,4,2,16,128]{5,4,3,2,1,0:T(8,128)(2,1)}, u32[]{:S(2)}) copy-start(bf16[2,1,4,2,16,128]{5,4,3,2,1,0:T(8,128)(2,1)} %param.5) | copy-start | bytes 196612
  2.1 47.8 %copy-start.1 = (s32[64,64]{1,0:T(8,128)S(1)}, s32[64,64]{1,0:T(8,128)}, u32[]{:S(2)}) copy-start(s32[64,64]{1,0:T(8,128)} %kminus_ref.3) | copy-start | bytes 49156
  2.1 47.8 %all-to-all-start = ((bf16[64,7,4,128]{3,2,1,0:T(4,128)(2,1)}), bf16[64,7,4,128]{3,2,1,0:T(4,128)(2,1)S(1)}, u32[]{:S(2)}, u32[]{:S(2)}) async-start(bf16[64,7,4,128]{3,2,1,0:T(4,128)(2,1)} %pad_maximum_fusion.1), calls=%async_computation | async-start | bytes 917504 | tf_op jit(solution)/shard_map/all_to_all | solution.py:22
  18.3 17.2 %collective-permute-start.1 = (bf16[2,4,2,16,128]{4,3,2,1,0:T(8,128)(2,1)S(1)}, bf16[2,4,2,16,128]{4,3,2,1,0:T(8,128)(2,1)S(1)}, u32[]{:S(2)}, u32[]{:S(2)}) collective-permute-start(bf16[2,4,2,16,128]{4,3,2,1,0:T(8,128)(2,1)S(1)} %bitcast.60), channel_id=1, source_target_pairs={{0,1},{1,0},{2,3},{3,2},{4,5},{5,4},{6,7},{7,6},{8,9},{9,8},{10,11... | collective-permute-start | bytes 196616 | tf_op jit(solution)/shard_map/ppermute | solution.py:178
  26.5 8.9 %collective-permute-start = (bf16[2,4,2,16,128]{4,3,2,1,0:T(8,128)(2,1)S(1)}, bf16[2,4,2,16,128]{4,3,2,1,0:T(8,128)(2,1)S(1)}, u32[]{:S(2)}, u32[]{:S(2)}) collective-permute-start(bf16[2,4,2,16,128]{4,3,2,1,0:T(8,128)(2,1)S(1)} %bitcast.61), channel_id=1, source_target_pairs={{0,8},{8,16},{16,24},{24,32},{32,40},{40,48},{48,56},{56,64},{64,7... | collective-permute-start | bytes 196616 | tf_op jit(solution)/shard_map/ppermute | solution.py:182
  29.1 20.8 %copy-start.2 = (s32[2]{0:T(128)S(1)}, s32[2]{0:T(128)}, u32[]{:S(2)}) copy-start(s32[2]{0:T(128)} %rows_ref.3) | copy-start | bytes 28
  51.8 33.5 %all-to-all-start.1 = ((bf16[128,2,4,128]{3,2,1,0:T(4,128)(2,1)}), bf16[128,2,4,128]{3,2,1,0:T(4,128)(2,1)S(1)}, u32[]{:S(2)}, u32[]{:S(2)}) async-start(bf16[128,2,4,128]{3,2,1,0:T(4,128)(2,1)} %mirror_pieces.1), calls=%async_computation.1 | async-start | bytes 524288 | tf_op jit(solution)/shard_map/all_to_all | solution.py:27
  64.2 5.7 %collective-permute-start.2 = (bf16[2,4,2,16,128]{4,3,2,1,0:T(8,128)(2,1)S(1)}, bf16[2,4,2,16,128]{4,3,2,1,0:T(8,128)(2,1)S(1)}, u32[]{:S(2)}, u32[]{:S(2)}) collective-permute-start(bf16[2,4,2,16,128]{4,3,2,1,0:T(8,128)(2,1)S(1)} %collective-permute-done.1), channel_id=1, source_target_pairs={{0,8},{8,16},{16,24},{24,32},{32,40},{40,48},{48,56},{56,64},{64,7... | collective-permute-start | bytes 196616 | tf_op jit(solution)/shard_map/ppermute | solution.py:182
  85.3 47.1 %all-to-all-start.2 = ((bf16[64,48,128]{2,1,0:T(8,128)(2,1)}), bf16[64,48,128]{2,1,0:T(8,128)(2,1)S(1)}, u32[]{:S(2)}, u32[]{:S(2)}) async-start(bf16[64,48,128]{2,1,0:T(8,128)(2,1)} %bitcast.16), calls=%async_computation.2 | async-start | bytes 1572864 | tf_op jit(solution)/shard_map/all_to_all | solution.py:22
  92.5 39.9 %copy-start = (bf16[2,1,2,3,128,128]{5,4,3,2,1,0:T(8,128)(2,1)S(1)}, bf16[2,1,2,3,128,128]{5,4,3,2,1,0:T(8,128)(2,1)}, u32[]{:S(2)}) copy-start(bf16[2,1,2,3,128,128]{5,4,3,2,1,0:T(8,128)(2,1)} %param.6) | copy-start | bytes 1179652
  92.5 27.8 %collective-permute-start.5 = (bf16[4,2,16,16,128]{4,3,2,1,0:T(8,128)(2,1)S(1)}, bf16[4,2,16,16,128]{4,3,2,1,0:T(8,128)(2,1)S(1)}, u32[]{:S(2)}, u32[]{:S(2)}) collective-permute-start(bf16[4,2,16,16,128]{4,3,2,1,0:T(8,128)(2,1)S(1)} %pad_maximum_fusion.refs_0_), channel_id=1, source_target_pairs={{0,6},{1,7},{2,0},{3,1},{4,2},{5,3},{6,4},{7,5},{8,14},{9,15},{10,... | collective-permute-start | bytes 1572872 | tf_op jit(solution)/shard_map/ppermute | solution.py:172
  97.6 22.7 %collective-permute-start.4 = (bf16[4,2,16,16,128]{4,3,2,1,0:T(8,128)(2,1)S(1)}, bf16[4,2,16,16,128]{4,3,2,1,0:T(8,128)(2,1)S(1)}, u32[]{:S(2)}, u32[]{:S(2)}) collective-permute-start(bf16[4,2,16,16,128]{4,3,2,1,0:T(8,128)(2,1)S(1)} %pad_maximum_fusion.refs_0_), channel_id=1, source_target_pairs={{0,4},{1,5},{2,6},{3,7},{4,0},{5,1},{6,2},{7,3},{8,12},{9,13},{10,... | collective-permute-start | bytes 1572872 | tf_op jit(solution)/shard_map/ppermute | solution.py:172
  100.1 25.8 %collective-permute-start.3 = (bf16[4,2,16,16,128]{4,3,2,1,0:T(8,128)(2,1)S(1)}, bf16[4,2,16,16,128]{4,3,2,1,0:T(8,128)(2,1)S(1)}, u32[]{:S(2)}, u32[]{:S(2)}) collective-permute-start(bf16[4,2,16,16,128]{4,3,2,1,0:T(8,128)(2,1)S(1)} %pad_maximum_fusion.refs_0_), channel_id=1, source_target_pairs={{0,2},{1,3},{2,4},{3,5},{4,6},{5,7},{6,0},{7,1},{8,10},{9,11},{10,... | collective-permute-start | bytes 1572872 | tf_op jit(solution)/shard_map/ppermute | solution.py:172
  149.3 16.7 %collective-permute-start.6 = (bf16[2,4,2,16,128]{4,3,2,1,0:T(8,128)(2,1)S(1)}, bf16[2,4,2,16,128]{4,3,2,1,0:T(8,128)(2,1)S(1)}, u32[]{:S(2)}, u32[]{:S(2)}) collective-permute-start(bf16[2,4,2,16,128]{4,3,2,1,0:T(8,128)(2,1)S(1)} %fusion.3), channel_id=1, source_target_pairs={{0,1},{1,0},{2,3},{3,2},{4,5},{5,4},{6,7},{7,6},{8,9},{9,8},{10,11... | collective-permute-start | bytes 196616 | tf_op jit(solution)/shard_map/ppermute | solution.py:178

commit v4 on v3

--- a/solution.py
+++ b/solution.py
@@ -29,21 +29,42 @@
     )
 
 
+def join_kernel(now_ref, before_ref, out_ref, done):
+    copies = [
+        pltpu.make_async_copy(ref, out_ref.at[:, step], done.at[step])
+        for step, ref in enumerate((now_ref, before_ref))
+    ]
+    for copy in copies:
+        copy.start()
+    for copy in copies:
+        copy.wait()
+
+
+def joined(now, before):
+    return pl.pallas_call(
+        join_kernel,
+        out_shape=jax.ShapeDtypeStruct((2, 2, 2, 16, 16, 128), jnp.bfloat16),
+        in_specs=[ANY, ANY],
+        out_specs=VMEM,
+        scratch_shapes=[pltpu.SemaphoreType.DMA((2,))],
+        compiler_params=params(8),
+        cost_estimate=pl.CostEstimate(flops=115000000000, bytes_accessed=1000000, transcendentals=0),
+        name="joined",
+    )(now, before)
+
+
 def mirror_kernel(kminus_ref, rows_ref, shift_ref, row_ref, spread_ref, out_ref):
     target = kminus_ref[rows_ref[row_ref[0]], shift_ref[0]]
-    before = spread_ref[kminus_ref[target, 63], 6]
     for k in range(64):
         piece = spread_ref[kminus_ref[target, k], 6]
-        for high in range(2):
-            out_ref[high * 64 + k, 0] = piece
-            out_ref[high * 64 + k, 1] = before
-        before = piece
+        out_ref[k] = piece
+        out_ref[64 + k] = piece
 
 
 def mirror_pieces(lookup, row, spread):
     return pl.pallas_call(
         mirror_kernel,
-        out_shape=jax.ShapeDtypeStruct((128, 2, 4, 128), jnp.bfloat16),
+        out_shape=jax.ShapeDtypeStruct((128, 4, 128), jnp.bfloat16),
         in_specs=[SMEM] * 4 + [VMEM],
         out_specs=VMEM,
         compiler_params=params(12),
@@ -179,7 +200,10 @@
 
 
 def ahead(value):
-    return lax.ppermute(value, "ka", [(k, (k + 1) % 64) for k in range(64)])
+    pairs = [
+        (k * 8 + v, (k + 1) * 8 + v if k < 63 else v ^ 1) for k in range(64) for v in range(8)
+    ]
+    return lax.ppermute(value, ("ka", "vert"), pairs)
 
 
 def per_device(amplitudes, factors, kminus, kj_rows, kshift):
@@ -195,22 +219,19 @@
     spread = exchange(
         jnp.concatenate([factors[:, 0].reshape(64, 6, 4, 128), shard.reshape(64, 1, 4, 128)], 1)
     )
-    behind = ahead(shard)
     other_half = swapped(shard)
-    spread, behind, other_half = lax.optimization_barrier((spread, behind, other_half))
+    spread, other_half = lax.optimization_barrier((spread, other_half))
 
     mirror = exchange_both(mirror_pieces(lookup, row, spread))
-    here = jnp.stack([shard, behind]).reshape(2, 16, 16, 128)
-    there = jnp.stack([other_half, ahead(other_half)]).reshape(2, 16, 16, 128)
     own = jnp.where(
-        high == 0, jnp.stack([here, there], axis=1), jnp.stack([there, here], axis=1)
+        high == 0, jnp.stack([shard, other_half]), jnp.stack([other_half, shard])
     )
     chosen = factor_pieces(lookup, spread)
     mirror, own, chosen = lax.optimization_barrier((mirror, own, chosen))
 
     other = exchange(chosen.reshape(64, 48, 128))
-    mirror = jnp.transpose(mirror.reshape(2, 64, 2, 4, 128), (2, 0, 1, 3, 4))
-    turns = turned(jnp.concatenate([own, mirror.reshape(2, 2, 16, 16, 128)]))
+    now = jnp.stack([own.reshape(2, 16, 16, 128), mirror.reshape(2, 16, 16, 128)])
+    turns = turned(joined(now, ahead(now)).reshape(4, 2, 16, 16, 128))
     partial = ladder(place, turns, factors[:, 0], other)
 
     groups = [[0, 2, 4, 6], [1, 3, 5, 7]]

time: 167 us -> 165 us (0.988)
  the two profiles are of different devices: /device:TPU:4 before, /device:TPU:6 now
where the time goes in v4:
time: 165 us; the launch traced here: 164 us
  waiting for transfers between devices  74.6 us (45%)
  starting transfers between devices  65.8 us (40%)
  blocking collectives  13.3 us (8%)
  Pallas kernels  6.84 us (4%)
  other arithmetic  2.98 us (2%)
    all_to_all x2, starting transfers between devices, exchange(): return lax.all_to_all(value, 'ka', split_axis=0, concat_axis=0, tiled=True)  24.1 us
    ppermute x3, waiting for transfers between devices, turned(): lax.ppermute(value, 'vert', [(v, (v + 2 * turn) % 8) for v in range(8)])  22.8 us
    all_to_all x2, waiting for transfers between devices, exchange(): return lax.all_to_all(value, 'ka', split_axis=0, concat_axis=0, tiled=True)  21 us
    ppermute x2, starting transfers between devices, swapped(): return lax.ppermute(value, 'vert', [(v, v ^ 1) for v in range(8)])  17.3 us
    ppermute x2, waiting for transfers between devices, swapped(): return lax.ppermute(value, 'vert', [(v, v ^ 1) for v in range(8)])  16.8 us
    all_to_all x1, waiting for transfers between devices, exchange_both(): lax.all_to_all(value, ('ka', 'vert'), split_axis=0, concat_axis=0, tiled=...  14 us
    all_to_all x1, blocking collectives, per_device(): lax.all_to_all(partial, 'vert', split_axis=0, concat_axis=0, tiled=True,...  13.3 us
    all_to_all x1, starting transfers between devices, exchange_both(): lax.all_to_all(value, ('ka', 'vert'), split_axis=0, concat_axis=0, tiled=...  11.9 us
  transfers between devices with their start and end apart: 9, of which 7 were waited for; matrix products, arithmetic and copies ran while one was open for 0% of the time, Pallas kernels for 1%

profile of v4, /device:TPU:6, one launch (start us, length us, event | category | flops | bytes accessed | tf_op | source)
XLA Modules:
  0.0 164.3 jit_solution(1365997279200396418)
XLA Ops:
  0.0 2.1 %pad_maximum_fusion = bf16[64,7,4,128]{3,2,1,0:T(4,128)(2,1)} fusion(bf16[64,1,4,128]{3,2,1,0:T(4,128)(2,1)} %bitcast.60, bf16[64,6,4,128]{3,2,1,0:T(4,128)(2,1)} %bitcast.50), kind=kLoop, calls=%fused_computation.1 | loop fusion | flops 229376 | bytes 917504 | tf_op jit(solution)/shard_map/concatenate | solution.py:220
  2.1 0.0 copy-start.3
  2.1 0.0 copy-start.1
  2.1 16.2 %all-to-all-start = ((bf16[64,7,4,128]{3,2,1,0:T(4,128)(2,1)}), bf16[64,7,4,128]{3,2,1,0:T(4,128)(2,1)S(1)}, u32[]{:S(2)}, u32[]{:S(2)}) async-start(bf16[64,7,4,128]{3,2,1,0:T(4,128)(2,1)} %pad_maximum_fusion), calls=%async_computation | async-start | bytes 917504 | tf_op jit(solution)/shard_map/all_to_all | solution.py:22
  18.3 0.0 copy-done.3
  18.3 8.2 %collective-permute-start = (bf16[2,4,2,16,128]{4,3,2,1,0:T(8,128)(2,1)S(1)}, bf16[2,4,2,16,128]{4,3,2,1,0:T(8,128)(2,1)S(1)}, u32[]{:S(2)}, u32[]{:S(2)}) collective-permute-start(bf16[2,4,2,16,128]{4,3,2,1,0:T(8,128)(2,1)S(1)} %bitcast.61), channel_id=1, source_target_pairs={{0,1},{1,0},{2,3},{3,2},{4,5},{5,4},{6,7},{7,6},{8,9},{9,8},{10,11... | collective-permute-start | bytes 196616 | tf_op jit(solution)/shard_map/ppermute | solution.py:199
  27.2 0.0 copy-start.2
  27.2 8.3 %collective-permute-done = bf16[2,4,2,16,128]{4,3,2,1,0:T(8,128)(2,1)S(1)} collective-permute-done((bf16[2,4,2,16,128]{4,3,2,1,0:T(8,128)(2,1)S(1)}, bf16[2,4,2,16,128]{4,3,2,1,0:T(8,128)(2,1)S(1)}, u32[]{:S(2)}, u32[]{:S(2)}) %collective-permute-start) | collective-permute-done | bytes 65568 | tf_op jit(solution)/shard_map/ppermute | solution.py:199
  35.5 14.4 %all-to-all-done.spread_ref = bf16[64,7,4,128]{3,2,1,0:T(4,128)(2,1)S(1)} async-done(((bf16[64,7,4,128]{3,2,1,0:T(4,128)(2,1)}), bf16[64,7,4,128]{3,2,1,0:T(4,128)(2,1)S(1)}, u32[]{:S(2)}, u32[]{:S(2)}) %all-to-all-start) | async-done | bytes 458784 | tf_op jit(solution)/shard_map/all_to_all | solution.py:22
  49.9 0.0 copy-done.1
  49.9 0.0 copy-done.2
  49.9 1.8 %mirror_pieces.1 = bf16[128,4,128]{2,1,0:T(4,128)(2,1)} custom-call(s32[64,64]{1,0:T(8,128)S(1)} %copy-done.1, s32[2]{0:T(128)S(1)} %copy-done.2, s32[1]{0:T(128)S(6)} %copy.12.shift_ref, s32[1]{0:T(128)} %bitcast.4.row_ref, bf16[64,7,4,128]{3,2,1,0:T(4,128)(2,1)S(1)} %all-to-all-done.spread_ref), custom_call_target="tpu_custom_call" | custom-call | bytes 700000 | tf_op jit(solution)/shard_map/mirror_pieces/pallas_call | solution.py:65
  51.7 11.9 %all-to-all-start.1 = ((bf16[128,4,128]{2,1,0:T(4,128)(2,1)}), bf16[128,4,128]{2,1,0:T(4,128)(2,1)S(1)}, u32[]{:S(2)}, u32[]{:S(2)}) async-start(bf16[128,4,128]{2,1,0:T(4,128)(2,1)} %mirror_pieces.1), calls=%async_computation.1 | async-start | bytes 262144 | tf_op jit(solution)/shard_map/all_to_all | solution.py:27
  63.6 2.1 %factor_pieces.1 = bf16[64,12,4,128]{3,2,1,0:T(4,128)(2,1)} custom-call(s32[64,64]{1,0:T(8,128)S(1)} %copy-done.1, s32[2]{0:T(128)S(1)} %copy-done.2, s32[1]{0:T(128)S(6)} %copy.12.shift_ref, bf16[64,7,4,128]{3,2,1,0:T(4,128)(2,1)S(1)} %all-to-all-done.spread_ref), custom_call_target="tpu_custom_call" | custom-call | bytes 1300000 | tf_op jit(solution)/shard_map/factor_pieces/pallas_call | solution.py:84
  65.8 14.0 %all-to-all-done.1 = bf16[128,4,128]{2,1,0:T(4,128)(2,1)S(1)} async-done(((bf16[128,4,128]{2,1,0:T(4,128)(2,1)}), bf16[128,4,128]{2,1,0:T(4,128)(2,1)S(1)}, u32[]{:S(2)}, u32[]{:S(2)}) %all-to-all-start.1) | async-done | bytes 131104 | tf_op jit(solution)/shard_map/all_to_all | solution.py:27
  79.8 2.1 %collective-permute-start.1 = (bf16[2,2,16,16,128]{4,3,2,1,0:T(8,128)(2,1)S(1)}, bf16[2,2,16,16,128]{4,3,2,1,0:T(8,128)(2,1)S(1)}, u32[]{:S(2)}, u32[]{:S(2)}) collective-permute-start(bf16[2,2,16,16,128]{4,3,2,1,0:T(8,128)(2,1)S(1)} %pad_maximum_fusion.1.now_ref), channel_id=1, source_target_pairs={{0,8},{1,9},{2,10},{3,11},{4,12},{5,13},{6,14},{7,15},{8,16},{9,17... | collective-permute-start | bytes 786440 | tf_op jit(solution)/shard_map/ppermute | solution.py:206
  81.9 7.9 %all-to-all-start.2 = ((bf16[64,48,128]{2,1,0:T(8,128)(2,1)}), bf16[64,48,128]{2,1,0:T(8,128)(2,1)S(1)}, u32[]{:S(2)}, u32[]{:S(2)}) async-start(bf16[64,48,128]{2,1,0:T(8,128)(2,1)} %bitcast.14), calls=%async_computation.2 | async-start | bytes 1572864 | tf_op jit(solution)/shard_map/all_to_all | solution.py:22
  89.8 0.0 copy-start
  89.8 0.0 collective-permute-done.1.before_ref
  89.8 0.1 joined.1
  89.9 5.1 %collective-permute-start.4 = (bf16[4,2,16,16,128]{4,3,2,1,0:T(8,128)(2,1)S(1)}, bf16[4,2,16,16,128]{4,3,2,1,0:T(8,128)(2,1)S(1)}, u32[]{:S(2)}, u32[]{:S(2)}) collective-permute-start(bf16[4,2,16,16,128]{4,3,2,1,0:T(8,128)(2,1)S(1)} %bitcast.52), channel_id=1, source_target_pairs={{0,6},{1,7},{2,0},{3,1},{4,2},{5,3},{6,4},{7,5},{8,14},{9,15},{10,... | collective-permute-start | bytes 1572872 | tf_op jit(solution)/shard_map/ppermute | solution.py:193
  95.0 2.5 %collective-permute-start.3 = (bf16[4,2,16,16,128]{4,3,2,1,0:T(8,128)(2,1)S(1)}, bf16[4,2,16,16,128]{4,3,2,1,0:T(8,128)(2,1)S(1)}, u32[]{:S(2)}, u32[]{:S(2)}) collective-permute-start(bf16[4,2,16,16,128]{4,3,2,1,0:T(8,128)(2,1)S(1)} %bitcast.53), channel_id=1, source_target_pairs={{0,4},{1,5},{2,6},{3,7},{4,0},{5,1},{6,2},{7,3},{8,12},{9,13},{10,... | collective-permute-start | bytes 1572872 | tf_op jit(solution)/shard_map/ppermute | solution.py:193
  97.5 2.9 %collective-permute-start.2 = (bf16[4,2,16,16,128]{4,3,2,1,0:T(8,128)(2,1)S(1)}, bf16[4,2,16,16,128]{4,3,2,1,0:T(8,128)(2,1)S(1)}, u32[]{:S(2)}, u32[]{:S(2)}) collective-permute-start(bf16[4,2,16,16,128]{4,3,2,1,0:T(8,128)(2,1)S(1)} %bitcast.54), channel_id=1, source_target_pairs={{0,2},{1,3},{2,4},{3,5},{4,6},{5,7},{6,0},{7,1},{8,10},{9,11},{10,... | collective-permute-start | bytes 1572872 | tf_op jit(solution)/shard_map/ppermute | solution.py:193
  100.4 0.1 pad_add_fusion.place_ref
  100.5 17.2 %collective-permute-done.4.refs_3_ = bf16[4,2,16,16,128]{4,3,2,1,0:T(8,128)(2,1)S(1)} collective-permute-done((bf16[4,2,16,16,128]{4,3,2,1,0:T(8,128)(2,1)S(1)}, bf16[4,2,16,16,128]{4,3,2,1,0:T(8,128)(2,1)S(1)}, u32[]{:S(2)}, u32[]{:S(2)}) %collective-permute-start.4) | collective-permute-done | bytes 524320 | tf_op jit(solution)/shard_map/ppermute | solution.py:193
  117.7 0.0 collective-permute-done.3.refs_2_
  117.7 5.6 %collective-permute-done.2.refs_1_ = bf16[4,2,16,16,128]{4,3,2,1,0:T(8,128)(2,1)S(1)} collective-permute-done((bf16[4,2,16,16,128]{4,3,2,1,0:T(8,128)(2,1)S(1)}, bf16[4,2,16,16,128]{4,3,2,1,0:T(8,128)(2,1)S(1)}, u32[]{:S(2)}, u32[]{:S(2)}) %collective-permute-start.2) | collective-permute-done | bytes 524320 | tf_op jit(solution)/shard_map/ppermute | solution.py:193
  123.3 6.6 %all-to-all-done.2.refs_5_ = bf16[64,48,128]{2,1,0:T(8,128)(2,1)S(1)} async-done(((bf16[64,48,128]{2,1,0:T(8,128)(2,1)}), bf16[64,48,128]{2,1,0:T(8,128)(2,1)S(1)}, u32[]{:S(2)}, u32[]{:S(2)}) %all-to-all-start.2) | async-done | bytes 786464 | tf_op jit(solution)/shard_map/all_to_all | solution.py:22
  129.9 0.0 copy-done
  129.9 2.8 %ladder.1 = bf16[4,2,4,2,32,128]{5,4,3,2,1,0:T(8,128)(2,1)S(1)} custom-call(s32[4]{0:T(128)S(1)} %pad_add_fusion.place_ref, bf16[4,2,16,16,128]{4,3,2,1,0:T(8,128)(2,1)S(1)} %bitcast.55, bf16[4,2,16,16,128]{4,3,2,1,0:T(8,128)(2,1)S(1)} %collective-permute-done.2.refs_1_, bf16[4,2,16,16,128]{4,3,2,1,0:T(8,128)(2,1)S(1)} %collective-permute-done.3.refs_2_, ...), custom_call_target="tpu_custom_call" | custom-call | flops 1610612736 | bytes 4000000 | tf_op jit(solution)/shard_map/ladder/pallas_call | solution.py:171
  132.7 13.3 %all_to_all.20 = bf16[4,2,4,2,32,128]{5,4,3,2,1,0:T(8,128)(2,1)S(1)} all-to-all(bf16[4,2,4,2,32,128]{5,4,3,2,1,0:T(8,128)(2,1)S(1)} %ladder.1), channel_id=1, replica_groups={{0,2,4,6},{1,3,5,7},{8,10,12,14},{9,11,13,15},{16,18,20,22},{17,19,21,2..., dimensions={0} | all-to-all | bytes 1048576 | tf_op jit(solution)/shard_map/all_to_all | solution.py:238
  146.0 0.1 convert_reduce_fusion
  146.1 9.1 %collective-permute-start.5 = (bf16[2,4,2,16,128]{4,3,2,1,0:T(8,128)(2,1)S(1)}, bf16[2,4,2,16,128]{4,3,2,1,0:T(8,128)(2,1)S(1)}, u32[]{:S(2)}, u32[]{:S(2)}) collective-permute-start(bf16[2,4,2,16,128]{4,3,2,1,0:T(8,128)(2,1)S(1)} %fusion.3), channel_id=1, source_target_pairs={{0,1},{1,0},{2,3},{3,2},{4,5},{5,4},{6,7},{7,6},{8,9},{9,8},{10,11... | collective-permute-start | bytes 196616 | tf_op jit(solution)/shard_map/ppermute | solution.py:199
  155.2 8.5 %collective-permute-done.5 = bf16[2,4,2,16,128]{4,3,2,1,0:T(8,128)(2,1)S(1)} collective-permute-done((bf16[2,4,2,16,128]{4,3,2,1,0:T(8,128)(2,1)S(1)}, bf16[2,4,2,16,128]{4,3,2,1,0:T(8,128)(2,1)S(1)}, u32[]{:S(2)}, u32[]{:S(2)}) %collective-permute-start.5) | collective-permute-done | bytes 65568 | tf_op jit(solution)/shard_map/ppermute | solution.py:199
  163.7 0.7 fusion.4
  (3 shorter events, 0.1 us)
Async XLA Ops:
  2.1 16.2 %copy-start.3 = (bf16[2,1,4,2,16,128]{5,4,3,2,1,0:T(8,128)(2,1)S(1)}, bf16[2,1,4,2,16,128]{5,4,3,2,1,0:T(8,128)(2,1)}, u32[]{:S(2)}) copy-start(bf16[2,1,4,2,16,128]{5,4,3,2,1,0:T(8,128)(2,1)} %param.5) | copy-start | bytes 196612
  2.1 47.8 %copy-start.1 = (s32[64,64]{1,0:T(8,128)S(1)}, s32[64,64]{1,0:T(8,128)}, u32[]{:S(2)}) copy-start(s32[64,64]{1,0:T(8,128)} %kminus_ref.3) | copy-start | bytes 49156
  2.1 47.8 %all-to-all-start = ((bf16[64,7,4,128]{3,2,1,0:T(4,128)(2,1)}), bf16[64,7,4,128]{3,2,1,0:T(4,128)(2,1)S(1)}, u32[]{:S(2)}, u32[]{:S(2)}) async-start(bf16[64,7,4,128]{3,2,1,0:T(4,128)(2,1)} %pad_maximum_fusion), calls=%async_computation | async-start | bytes 917504 | tf_op jit(solution)/shard_map/all_to_all | solution.py:22
  18.3 17.2 %collective-permute-start = (bf16[2,4,2,16,128]{4,3,2,1,0:T(8,128)(2,1)S(1)}, bf16[2,4,2,16,128]{4,3,2,1,0:T(8,128)(2,1)S(1)}, u32[]{:S(2)}, u32[]{:S(2)}) collective-permute-start(bf16[2,4,2,16,128]{4,3,2,1,0:T(8,128)(2,1)S(1)} %bitcast.61), channel_id=1, source_target_pairs={{0,1},{1,0},{2,3},{3,2},{4,5},{5,4},{6,7},{7,6},{8,9},{9,8},{10,11... | collective-permute-start | bytes 196616 | tf_op jit(solution)/shard_map/ppermute | solution.py:199
  27.2 22.7 %copy-start.2 = (s32[2]{0:T(128)S(1)}, s32[2]{0:T(128)}, u32[]{:S(2)}) copy-start(s32[2]{0:T(128)} %rows_ref.3) | copy-start | bytes 28
  51.7 28.0 %all-to-all-start.1 = ((bf16[128,4,128]{2,1,0:T(4,128)(2,1)}), bf16[128,4,128]{2,1,0:T(4,128)(2,1)S(1)}, u32[]{:S(2)}, u32[]{:S(2)}) async-start(bf16[128,4,128]{2,1,0:T(4,128)(2,1)} %mirror_pieces.1), calls=%async_computation.1 | async-start | bytes 262144 | tf_op jit(solution)/shard_map/all_to_all | solution.py:27
  79.8 10.0 %collective-permute-start.1 = (bf16[2,2,16,16,128]{4,3,2,1,0:T(8,128)(2,1)S(1)}, bf16[2,2,16,16,128]{4,3,2,1,0:T(8,128)(2,1)S(1)}, u32[]{:S(2)}, u32[]{:S(2)}) collective-permute-start(bf16[2,2,16,16,128]{4,3,2,1,0:T(8,128)(2,1)S(1)} %pad_maximum_fusion.1.now_ref), channel_id=1, source_target_pairs={{0,8},{1,9},{2,10},{3,11},{4,12},{5,13},{6,14},{7,15},{8,16},{9,17... | collective-permute-start | bytes 786440 | tf_op jit(solution)/shard_map/ppermute | solution.py:206
  81.9 48.0 %all-to-all-start.2 = ((bf16[64,48,128]{2,1,0:T(8,128)(2,1)}), bf16[64,48,128]{2,1,0:T(8,128)(2,1)S(1)}, u32[]{:S(2)}, u32[]{:S(2)}) async-start(bf16[64,48,128]{2,1,0:T(8,128)(2,1)} %bitcast.14), calls=%async_computation.2 | async-start | bytes 1572864 | tf_op jit(solution)/shard_map/all_to_all | solution.py:22
  89.8 40.1 %copy-start = (bf16[2,1,2,3,128,128]{5,4,3,2,1,0:T(8,128)(2,1)S(1)}, bf16[2,1,2,3,128,128]{5,4,3,2,1,0:T(8,128)(2,1)}, u32[]{:S(2)}) copy-start(bf16[2,1,2,3,128,128]{5,4,3,2,1,0:T(8,128)(2,1)} %param.6) | copy-start | bytes 1179652
  89.9 27.8 %collective-permute-start.4 = (bf16[4,2,16,16,128]{4,3,2,1,0:T(8,128)(2,1)S(1)}, bf16[4,2,16,16,128]{4,3,2,1,0:T(8,128)(2,1)S(1)}, u32[]{:S(2)}, u32[]{:S(2)}) collective-permute-start(bf16[4,2,16,16,128]{4,3,2,1,0:T(8,128)(2,1)S(1)} %bitcast.52), channel_id=1, source_target_pairs={{0,6},{1,7},{2,0},{3,1},{4,2},{5,3},{6,4},{7,5},{8,14},{9,15},{10,... | collective-permute-start | bytes 1572872 | tf_op jit(solution)/shard_map/ppermute | solution.py:193
  95.0 22.7 %collective-permute-start.3 = (bf16[4,2,16,16,128]{4,3,2,1,0:T(8,128)(2,1)S(1)}, bf16[4,2,16,16,128]{4,3,2,1,0:T(8,128)(2,1)S(1)}, u32[]{:S(2)}, u32[]{:S(2)}) collective-permute-start(bf16[4,2,16,16,128]{4,3,2,1,0:T(8,128)(2,1)S(1)} %bitcast.53), channel_id=1, source_target_pairs={{0,4},{1,5},{2,6},{3,7},{4,0},{5,1},{6,2},{7,3},{8,12},{9,13},{10,... | collective-permute-start | bytes 1572872 | tf_op jit(solution)/shard_map/ppermute | solution.py:193
  97.5 25.8 %collective-permute-start.2 = (bf16[4,2,16,16,128]{4,3,2,1,0:T(8,128)(2,1)S(1)}, bf16[4,2,16,16,128]{4,3,2,1,0:T(8,128)(2,1)S(1)}, u32[]{:S(2)}, u32[]{:S(2)}) collective-permute-start(bf16[4,2,16,16,128]{4,3,2,1,0:T(8,128)(2,1)S(1)} %bitcast.54), channel_id=1, source_target_pairs={{0,2},{1,3},{2,4},{3,5},{4,6},{5,7},{6,0},{7,1},{8,10},{9,11},{10,... | collective-permute-start | bytes 1572872 | tf_op jit(solution)/shard_map/ppermute | solution.py:193
  146.1 17.6 %collective-permute-start.5 = (bf16[2,4,2,16,128]{4,3,2,1,0:T(8,128)(2,1)S(1)}, bf16[2,4,2,16,128]{4,3,2,1,0:T(8,128)(2,1)S(1)}, u32[]{:S(2)}, u32[]{:S(2)}) collective-permute-start(bf16[2,4,2,16,128]{4,3,2,1,0:T(8,128)(2,1)S(1)} %fusion.3), channel_id=1, source_target_pairs={{0,1},{1,0},{2,3},{3,2},{4,5},{5,4},{6,7},{7,6},{8,9},{9,8},{10,11... | collective-permute-start | bytes 196616 | tf_op jit(solution)/shard_map/ppermute | solution.py:199

commit v5 on v4

--- a/solution.py
+++ b/solution.py
@@ -29,10 +29,13 @@
     )
 
 
-def join_kernel(now_ref, before_ref, out_ref, done):
+def join_kernel(high_ref, here_ref, there_ref, now_ref, before_ref, out_ref, done):
+    high = high_ref[0]
     copies = [
-        pltpu.make_async_copy(ref, out_ref.at[:, step], done.at[step])
-        for step, ref in enumerate((now_ref, before_ref))
+        pltpu.make_async_copy(here_ref, out_ref.at[pl.ds(0, 2), high], done.at[0]),
+        pltpu.make_async_copy(there_ref, out_ref.at[pl.ds(0, 2), 1 - high], done.at[1]),
+        pltpu.make_async_copy(now_ref, out_ref.at[2], done.at[2]),
+        pltpu.make_async_copy(before_ref, out_ref.at[3], done.at[3]),
     ]
     for copy in copies:
         copy.start()
@@ -40,17 +43,19 @@
         copy.wait()
 
 
-def joined(now, before):
+def joined(high, *parts):
     return pl.pallas_call(
         join_kernel,
-        out_shape=jax.ShapeDtypeStruct((2, 2, 2, 16, 16, 128), jnp.bfloat16),
-        in_specs=[ANY, ANY],
-        out_specs=VMEM,
-        scratch_shapes=[pltpu.SemaphoreType.DMA((2,))],
+        out_shape=jax.ShapeDtypeStruct((4, 2, 16, 16, 128), jnp.bfloat16),
+        in_specs=[SMEM] + [ANY] * 4,
+        out_specs=VMEM,
+        scratch_shapes=[pltpu.SemaphoreType.DMA((4,))],
         compiler_params=params(8),
-        cost_estimate=pl.CostEstimate(flops=115000000000, bytes_accessed=1000000, transcendentals=0),
+        cost_estimate=pl.CostEstimate(
+            flops=115000000000, bytes_accessed=1000000, transcendentals=0
+        ),
         name="joined",
-    )(now, before)
+    )(high, *parts)
 
 
 def mirror_kernel(kminus_ref, rows_ref, shift_ref, row_ref, spread_ref, out_ref):
@@ -199,6 +204,10 @@
     return lax.ppermute(value, "vert", [(v, v ^ 1) for v in range(8)])
 
 
+def passed(value):
+    return lax.ppermute(value, "ka", [(k, (k + 1) % 64) for k in range(64)])
+
+
 def ahead(value):
     pairs = [
         (k * 8 + v, (k + 1) * 8 + v if k < 63 else v ^ 1) for k in range(64) for v in range(8)
@@ -219,19 +228,21 @@
     spread = exchange(
         jnp.concatenate([factors[:, 0].reshape(64, 6, 4, 128), shard.reshape(64, 1, 4, 128)], 1)
     )
-    other_half = swapped(shard)
-    spread, other_half = lax.optimization_barrier((spread, other_half))
+    behind = passed(shard)
+    spread, behind = lax.optimization_barrier((spread, behind))
 
     mirror = exchange_both(mirror_pieces(lookup, row, spread))
-    own = jnp.where(
-        high == 0, jnp.stack([shard, other_half]), jnp.stack([other_half, shard])
-    )
+    here = jnp.stack([shard, behind]).reshape(2, 16, 16, 128)
     chosen = factor_pieces(lookup, spread)
-    mirror, own, chosen = lax.optimization_barrier((mirror, own, chosen))
+    here, chosen = lax.optimization_barrier((here, chosen))
+    there = swapped(here)
+    mirror, chosen = lax.optimization_barrier((mirror, chosen))
 
     other = exchange(chosen.reshape(64, 48, 128))
-    now = jnp.stack([own.reshape(2, 16, 16, 128), mirror.reshape(2, 16, 16, 128)])
-    turns = turned(joined(now, ahead(now)).reshape(4, 2, 16, 16, 128))
+    mirror = mirror.reshape(2, 16, 16, 128)
+    turns = turned(
+        joined(high.astype(jnp.int32).reshape(1), here, there, mirror, ahead(mirror))
+    )
     partial = ladder(place, turns, factors[:, 0], other)
 
     groups = [[0, 2, 4, 6], [1, 3, 5, 7]]

time: 165 us -> 161 us (0.976)
  the two profiles are of different devices: /device:TPU:6 before, /device:TPU:4 now
where the time goes in v5:
time: 161 us
  starting transfers between devices  77 us (48%)
  waiting for transfers between devices  71.9 us (45%)
  Pallas kernels  8.12 us (5%)
  other arithmetic  2.95 us (2%)
    all_to_all x2, waiting for transfers between devices, exchange(): return lax.all_to_all(value, 'ka', split_axis=0, concat_axis=0, tiled=True)  26.7 us
    all_to_all x2, starting transfers between devices, exchange(): return lax.all_to_all(value, 'ka', split_axis=0, concat_axis=0, tiled=True)  24.3 us
    ppermute x3, waiting for transfers between devices, turned(): lax.ppermute(value, 'vert', [(v, (v + 2 * turn) % 8) for v in range(8)])  22.8 us
    ppermute x2, starting transfers between devices, swapped(): return lax.ppermute(value, 'vert', [(v, v ^ 1) for v in range(8)])  21.5 us
    all_to_all x1, starting transfers between devices, exchange_both(): lax.all_to_all(value, ('ka', 'vert'), split_axis=0, concat_axis=0, tiled=...  12.3 us
    ppermute x3, starting transfers between devices, turned(): lax.ppermute(value, 'vert', [(v, (v + 2 * turn) % 8) for v in range(8)])  10.3 us
    all_to_all x1, waiting for transfers between devices, per_device(): lax.all_to_all(partial, 'vert', split_axis=0, concat_axis=0, tiled=True,...  9.68 us
    ppermute x2, waiting for transfers between devices, swapped(): return lax.ppermute(value, 'vert', [(v, v ^ 1) for v in range(8)])  8.49 us
  transfers between devices with their start and end apart: 11, of which 8 were waited for; matrix products, arithmetic and copies ran while one was open for 0% of the time, Pallas kernels for 2%

profile of v5, /device:TPU:4, one launch (start us, length us, event | category | flops | bytes accessed | tf_op | source)
XLA Modules:
  0.0 160.9 jit_solution(17345065357645842089)
XLA Ops:
  0.0 2.1 %pad_maximum_fusion = bf16[64,7,4,128]{3,2,1,0:T(4,128)(2,1)} fusion(bf16[64,1,4,128]{3,2,1,0:T(4,128)(2,1)} %bitcast.55, bf16[64,6,4,128]{3,2,1,0:T(4,128)(2,1)} %bitcast.49), kind=kLoop, calls=%fused_computation.1 | loop fusion | flops 229376 | bytes 917504 | tf_op jit(solution)/shard_map/concatenate | solution.py:229
  2.1 0.0 copy-start.3
  2.1 0.0 copy-start.1
  2.1 16.2 %all-to-all-start = ((bf16[64,7,4,128]{3,2,1,0:T(4,128)(2,1)}), bf16[64,7,4,128]{3,2,1,0:T(4,128)(2,1)S(1)}, u32[]{:S(2)}, u32[]{:S(2)}) async-start(bf16[64,7,4,128]{3,2,1,0:T(4,128)(2,1)} %pad_maximum_fusion), calls=%async_computation | async-start | bytes 917504 | tf_op jit(solution)/shard_map/all_to_all | solution.py:22
  18.3 0.0 copy-done.3
  18.3 2.1 %collective-permute-start = (bf16[2,4,2,16,128]{4,3,2,1,0:T(8,128)(2,1)S(1)}, bf16[2,4,2,16,128]{4,3,2,1,0:T(8,128)(2,1)S(1)}, u32[]{:S(2)}, u32[]{:S(2)}) collective-permute-start(bf16[2,4,2,16,128]{4,3,2,1,0:T(8,128)(2,1)S(1)} %bitcast.56), channel_id=1, source_target_pairs={{0,8},{8,16},{16,24},{24,32},{32,40},{40,48},{48,56},{56,64},{64,7... | collective-permute-start | bytes 196616 | tf_op jit(solution)/shard_map/ppermute | solution.py:208
  21.0 0.0 copy-start.2
  21.1 2.9 %collective-permute-done = bf16[2,4,2,16,128]{4,3,2,1,0:T(8,128)(2,1)S(1)} collective-permute-done((bf16[2,4,2,16,128]{4,3,2,1,0:T(8,128)(2,1)S(1)}, bf16[2,4,2,16,128]{4,3,2,1,0:T(8,128)(2,1)S(1)}, u32[]{:S(2)}, u32[]{:S(2)}) %collective-permute-start) | collective-permute-done | bytes 65568 | tf_op jit(solution)/shard_map/ppermute | solution.py:208
  23.9 20.5 %all-to-all-done.spread_ref = bf16[64,7,4,128]{3,2,1,0:T(4,128)(2,1)S(1)} async-done(((bf16[64,7,4,128]{3,2,1,0:T(4,128)(2,1)}), bf16[64,7,4,128]{3,2,1,0:T(4,128)(2,1)S(1)}, u32[]{:S(2)}, u32[]{:S(2)}) %all-to-all-start) | async-done | bytes 458784 | tf_op jit(solution)/shard_map/all_to_all | solution.py:22
  44.4 0.0 copy-done.1
  44.4 0.0 copy-done.2
  44.4 1.8 %mirror_pieces.1 = bf16[128,4,128]{2,1,0:T(4,128)(2,1)} custom-call(s32[64,64]{1,0:T(8,128)S(1)} %copy-done.1, s32[2]{0:T(128)S(1)} %copy-done.2, s32[1]{0:T(128)S(6)} %copy.12.shift_ref, s32[1]{0:T(128)} %bitcast.10.row_ref, bf16[64,7,4,128]{3,2,1,0:T(4,128)(2,1)S(1)} %all-to-all-done.spread_ref), custom_call_target="tpu_custom_call" | custom-call | bytes 700000 | tf_op jit(solution)/shard_map/mirror_pieces/pallas_call | solution.py:70
  46.2 12.3 %all-to-all-start.1 = ((bf16[128,4,128]{2,1,0:T(4,128)(2,1)}), bf16[128,4,128]{2,1,0:T(4,128)(2,1)S(1)}, u32[]{:S(2)}, u32[]{:S(2)}) async-start(bf16[128,4,128]{2,1,0:T(4,128)(2,1)} %mirror_pieces.1), calls=%async_computation.1 | async-start | bytes 262144 | tf_op jit(solution)/shard_map/all_to_all | solution.py:27
  58.5 2.1 %factor_pieces.1 = bf16[64,12,4,128]{3,2,1,0:T(4,128)(2,1)} custom-call(s32[64,64]{1,0:T(8,128)S(1)} %copy-done.1, s32[2]{0:T(128)S(1)} %copy-done.2, s32[1]{0:T(128)S(6)} %copy.12.shift_ref, bf16[64,7,4,128]{3,2,1,0:T(4,128)(2,1)S(1)} %all-to-all-done.spread_ref), custom_call_target="tpu_custom_call" | custom-call | bytes 1300000 | tf_op jit(solution)/shard_map/factor_pieces/pallas_call | solution.py:89
  60.7 12.4 %collective-permute-start.1 = (bf16[2,16,16,128]{3,2,1,0:T(8,128)(2,1)S(1)}, bf16[2,16,16,128]{3,2,1,0:T(8,128)(2,1)S(1)}, u32[]{:S(2)}, u32[]{:S(2)}) collective-permute-start(bf16[2,16,16,128]{3,2,1,0:T(8,128)(2,1)S(1)} %pad_maximum_fusion.1.here_ref), channel_id=1, source_target_pairs={{0,1},{1,0},{2,3},{3,2},{4,5},{5,4},{6,7},{7,6},{8,9},{9,8},{10,11... | collective-permute-start | bytes 393224 | tf_op jit(solution)/shard_map/ppermute | solution.py:204
  73.1 1.4 all-to-all-done.1
  74.6 2.0 %collective-permute-start.2 = (bf16[2,16,16,128]{3,2,1,0:T(8,128)(2,1)S(1)}, bf16[2,16,16,128]{3,2,1,0:T(8,128)(2,1)S(1)}, u32[]{:S(2)}, u32[]{:S(2)}) collective-permute-start(bf16[2,16,16,128]{3,2,1,0:T(8,128)(2,1)S(1)} %bitcast.51), channel_id=1, source_target_pairs={{0,8},{1,9},{2,10},{3,11},{4,12},{5,13},{6,14},{7,15},{8,16},{9,17... | collective-permute-start | bytes 393224 | tf_op jit(solution)/shard_map/ppermute | solution.py:215
  76.6 8.1 %all-to-all-start.2 = ((bf16[64,48,128]{2,1,0:T(8,128)(2,1)}), bf16[64,48,128]{2,1,0:T(8,128)(2,1)S(1)}, u32[]{:S(2)}, u32[]{:S(2)}) async-start(bf16[64,48,128]{2,1,0:T(8,128)(2,1)} %bitcast.13), calls=%async_computation.2 | async-start | bytes 1572864 | tf_op jit(solution)/shard_map/all_to_all | solution.py:22
  84.7 0.0 collective-permute-done.1.there_ref
  84.7 0.0 collective-permute-done.2.before_ref
  84.7 0.0 copy-start
  84.7 0.6 joined.1.refs_0_
  85.3 4.9 %collective-permute-start.5 = (bf16[4,2,16,16,128]{4,3,2,1,0:T(8,128)(2,1)S(1)}, bf16[4,2,16,16,128]{4,3,2,1,0:T(8,128)(2,1)S(1)}, u32[]{:S(2)}, u32[]{:S(2)}) collective-permute-start(bf16[4,2,16,16,128]{4,3,2,1,0:T(8,128)(2,1)S(1)} %joined.1.refs_0_), channel_id=1, source_target_pairs={{0,6},{1,7},{2,0},{3,1},{4,2},{5,3},{6,4},{7,5},{8,14},{9,15},{10,... | collective-permute-start | bytes 1572872 | tf_op jit(solution)/shard_map/ppermute | solution.py:198
  90.2 2.5 %collective-permute-start.4 = (bf16[4,2,16,16,128]{4,3,2,1,0:T(8,128)(2,1)S(1)}, bf16[4,2,16,16,128]{4,3,2,1,0:T(8,128)(2,1)S(1)}, u32[]{:S(2)}, u32[]{:S(2)}) collective-permute-start(bf16[4,2,16,16,128]{4,3,2,1,0:T(8,128)(2,1)S(1)} %joined.1.refs_0_), channel_id=1, source_target_pairs={{0,4},{1,5},{2,6},{3,7},{4,0},{5,1},{6,2},{7,3},{8,12},{9,13},{10,... | collective-permute-start | bytes 1572872 | tf_op jit(solution)/shard_map/ppermute | solution.py:198
  92.8 2.9 %collective-permute-start.3 = (bf16[4,2,16,16,128]{4,3,2,1,0:T(8,128)(2,1)S(1)}, bf16[4,2,16,16,128]{4,3,2,1,0:T(8,128)(2,1)S(1)}, u32[]{:S(2)}, u32[]{:S(2)}) collective-permute-start(bf16[4,2,16,16,128]{4,3,2,1,0:T(8,128)(2,1)S(1)} %joined.1.refs_0_), channel_id=1, source_target_pairs={{0,2},{1,3},{2,4},{3,5},{4,6},{5,7},{6,0},{7,1},{8,10},{9,11},{10,... | collective-permute-start | bytes 1572872 | tf_op jit(solution)/shard_map/ppermute | solution.py:198
  95.7 0.1 pad_add_fusion.place_ref
  95.8 17.2 %collective-permute-done.5.refs_3_ = bf16[4,2,16,16,128]{4,3,2,1,0:T(8,128)(2,1)S(1)} collective-permute-done((bf16[4,2,16,16,128]{4,3,2,1,0:T(8,128)(2,1)S(1)}, bf16[4,2,16,16,128]{4,3,2,1,0:T(8,128)(2,1)S(1)}, u32[]{:S(2)}, u32[]{:S(2)}) %collective-permute-start.5) | collective-permute-done | bytes 524320 | tf_op jit(solution)/shard_map/ppermute | solution.py:198
  112.9 0.0 collective-permute-done.4.refs_2_
  112.9 5.6 %collective-permute-done.3.refs_1_ = bf16[4,2,16,16,128]{4,3,2,1,0:T(8,128)(2,1)S(1)} collective-permute-done((bf16[4,2,16,16,128]{4,3,2,1,0:T(8,128)(2,1)S(1)}, bf16[4,2,16,16,128]{4,3,2,1,0:T(8,128)(2,1)S(1)}, u32[]{:S(2)}, u32[]{:S(2)}) %collective-permute-start.3) | collective-permute-done | bytes 524320 | tf_op jit(solution)/shard_map/ppermute | solution.py:198
  118.5 6.2 %all-to-all-done.2.refs_5_ = bf16[64,48,128]{2,1,0:T(8,128)(2,1)S(1)} async-done(((bf16[64,48,128]{2,1,0:T(8,128)(2,1)}), bf16[64,48,128]{2,1,0:T(8,128)(2,1)S(1)}, u32[]{:S(2)}, u32[]{:S(2)}) %all-to-all-start.2) | async-done | bytes 786464 | tf_op jit(solution)/shard_map/all_to_all | solution.py:22
  124.7 0.0 copy-done
  124.7 3.6 %ladder.1 = bf16[4,2,4,2,32,128]{5,4,3,2,1,0:T(8,128)(2,1)} custom-call(s32[4]{0:T(128)S(1)} %pad_add_fusion.place_ref, bf16[4,2,16,16,128]{4,3,2,1,0:T(8,128)(2,1)S(1)} %joined.1.refs_0_, bf16[4,2,16,16,128]{4,3,2,1,0:T(8,128)(2,1)S(1)} %collective-permute-done.3.refs_1_, bf16[4,2,16,16,128]{4,3,2,1,0:T(8,128)(2,1)S(1)} %collective-permute-done.4.refs_2_, ...), custom_call_target="tpu_custom_call" | custom-call | flops 1610612736 | bytes 4000000 | tf_op jit(solution)/shard_map/ladder/pallas_call | solution.py:176
  128.4 4.5 %all-to-all-start.3 = ((bf16[4,2,4,2,32,128]{5,4,3,2,1,0:T(8,128)(2,1)}), bf16[4,2,4,2,32,128]{5,4,3,2,1,0:T(8,128)(2,1)S(1)}, u32[]{:S(2)}, u32[]{:S(2)}) async-start(bf16[4,2,4,2,32,128]{5,4,3,2,1,0:T(8,128)(2,1)} %ladder.1), calls=%async_computation.3 | async-start | bytes 1048576 | tf_op jit(solution)/shard_map/all_to_all | solution.py:249
  132.8 9.7 %all-to-all-done.3 = bf16[4,2,4,2,32,128]{5,4,3,2,1,0:T(8,128)(2,1)S(1)} async-done(((bf16[4,2,4,2,32,128]{5,4,3,2,1,0:T(8,128)(2,1)}), bf16[4,2,4,2,32,128]{5,4,3,2,1,0:T(8,128)(2,1)S(1)}, u32[]{:S(2)}, u32[]{:S(2)}) %all-to-all-start.3) | async-done | bytes 524320 | tf_op jit(solution)/shard_map/all_to_all | solution.py:249
  142.5 0.1 convert_reduce_fusion
  142.6 9.1 %collective-permute-start.6 = (bf16[2,4,2,16,128]{4,3,2,1,0:T(8,128)(2,1)S(1)}, bf16[2,4,2,16,128]{4,3,2,1,0:T(8,128)(2,1)S(1)}, u32[]{:S(2)}, u32[]{:S(2)}) collective-permute-start(bf16[2,4,2,16,128]{4,3,2,1,0:T(8,128)(2,1)S(1)} %fusion.3), channel_id=1, source_target_pairs={{0,1},{1,0},{2,3},{3,2},{4,5},{5,4},{6,7},{7,6},{8,9},{9,8},{10,11... | collective-permute-start | bytes 196616 | tf_op jit(solution)/shard_map/ppermute | solution.py:204
  151.7 8.5 %collective-permute-done.6 = bf16[2,4,2,16,128]{4,3,2,1,0:T(8,128)(2,1)S(1)} collective-permute-done((bf16[2,4,2,16,128]{4,3,2,1,0:T(8,128)(2,1)S(1)}, bf16[2,4,2,16,128]{4,3,2,1,0:T(8,128)(2,1)S(1)}, u32[]{:S(2)}, u32[]{:S(2)}) %collective-permute-start.6) | collective-permute-done | bytes 65568 | tf_op jit(solution)/shard_map/ppermute | solution.py:204
  160.2 0.7 fusion.4
  (2 shorter events, 0.0 us)
Async XLA Ops:
  2.1 16.2 %copy-start.3 = (bf16[2,1,4,2,16,128]{5,4,3,2,1,0:T(8,128)(2,1)S(1)}, bf16[2,1,4,2,16,128]{5,4,3,2,1,0:T(8,128)(2,1)}, u32[]{:S(2)}) copy-start(bf16[2,1,4,2,16,128]{5,4,3,2,1,0:T(8,128)(2,1)} %param.5) | copy-start | bytes 196612
  2.1 42.3 %copy-start.1 = (s32[64,64]{1,0:T(8,128)S(1)}, s32[64,64]{1,0:T(8,128)}, u32[]{:S(2)}) copy-start(s32[64,64]{1,0:T(8,128)} %kminus_ref.3) | copy-start | bytes 49156
  2.1 42.3 %all-to-all-start = ((bf16[64,7,4,128]{3,2,1,0:T(4,128)(2,1)}), bf16[64,7,4,128]{3,2,1,0:T(4,128)(2,1)S(1)}, u32[]{:S(2)}, u32[]{:S(2)}) async-start(bf16[64,7,4,128]{3,2,1,0:T(4,128)(2,1)} %pad_maximum_fusion), calls=%async_computation | async-start | bytes 917504 | tf_op jit(solution)/shard_map/all_to_all | solution.py:22
  18.3 5.6 %collective-permute-start = (bf16[2,4,2,16,128]{4,3,2,1,0:T(8,128)(2,1)S(1)}, bf16[2,4,2,16,128]{4,3,2,1,0:T(8,128)(2,1)S(1)}, u32[]{:S(2)}, u32[]{:S(2)}) collective-permute-start(bf16[2,4,2,16,128]{4,3,2,1,0:T(8,128)(2,1)S(1)} %bitcast.56), channel_id=1, source_target_pairs={{0,8},{8,16},{16,24},{24,32},{32,40},{40,48},{48,56},{56,64},{64,7... | collective-permute-start | bytes 196616 | tf_op jit(solution)/shard_map/ppermute | solution.py:208
  21.0 23.3 %copy-start.2 = (s32[2]{0:T(128)S(1)}, s32[2]{0:T(128)}, u32[]{:S(2)}) copy-start(s32[2]{0:T(128)} %rows_ref.3) | copy-start | bytes 28
  46.2 28.4 %all-to-all-start.1 = ((bf16[128,4,128]{2,1,0:T(4,128)(2,1)}), bf16[128,4,128]{2,1,0:T(4,128)(2,1)S(1)}, u32[]{:S(2)}, u32[]{:S(2)}) async-start(bf16[128,4,128]{2,1,0:T(4,128)(2,1)} %mirror_pieces.1), calls=%async_computation.1 | async-start | bytes 262144 | tf_op jit(solution)/shard_map/all_to_all | solution.py:27
  60.7 24.0 %collective-permute-start.1 = (bf16[2,16,16,128]{3,2,1,0:T(8,128)(2,1)S(1)}, bf16[2,16,16,128]{3,2,1,0:T(8,128)(2,1)S(1)}, u32[]{:S(2)}, u32[]{:S(2)}) collective-permute-start(bf16[2,16,16,128]{3,2,1,0:T(8,128)(2,1)S(1)} %pad_maximum_fusion.1.here_ref), channel_id=1, source_target_pairs={{0,1},{1,0},{2,3},{3,2},{4,5},{5,4},{6,7},{7,6},{8,9},{9,8},{10,11... | collective-permute-start | bytes 393224 | tf_op jit(solution)/shard_map/ppermute | solution.py:204
  74.6 10.1 %collective-permute-start.2 = (bf16[2,16,16,128]{3,2,1,0:T(8,128)(2,1)S(1)}, bf16[2,16,16,128]{3,2,1,0:T(8,128)(2,1)S(1)}, u32[]{:S(2)}, u32[]{:S(2)}) collective-permute-start(bf16[2,16,16,128]{3,2,1,0:T(8,128)(2,1)S(1)} %bitcast.51), channel_id=1, source_target_pairs={{0,8},{1,9},{2,10},{3,11},{4,12},{5,13},{6,14},{7,15},{8,16},{9,17... | collective-permute-start | bytes 393224 | tf_op jit(solution)/shard_map/ppermute | solution.py:215
  76.6 48.1 %all-to-all-start.2 = ((bf16[64,48,128]{2,1,0:T(8,128)(2,1)}), bf16[64,48,128]{2,1,0:T(8,128)(2,1)S(1)}, u32[]{:S(2)}, u32[]{:S(2)}) async-start(bf16[64,48,128]{2,1,0:T(8,128)(2,1)} %bitcast.13), calls=%async_computation.2 | async-start | bytes 1572864 | tf_op jit(solution)/shard_map/all_to_all | solution.py:22
  84.7 40.0 %copy-start = (bf16[2,1,2,3,128,128]{5,4,3,2,1,0:T(8,128)(2,1)S(1)}, bf16[2,1,2,3,128,128]{5,4,3,2,1,0:T(8,128)(2,1)}, u32[]{:S(2)}) copy-start(bf16[2,1,2,3,128,128]{5,4,3,2,1,0:T(8,128)(2,1)} %param.6) | copy-start | bytes 1179652
  85.3 27.6 %collective-permute-start.5 = (bf16[4,2,16,16,128]{4,3,2,1,0:T(8,128)(2,1)S(1)}, bf16[4,2,16,16,128]{4,3,2,1,0:T(8,128)(2,1)S(1)}, u32[]{:S(2)}, u32[]{:S(2)}) collective-permute-start(bf16[4,2,16,16,128]{4,3,2,1,0:T(8,128)(2,1)S(1)} %joined.1.refs_0_), channel_id=1, source_target_pairs={{0,6},{1,7},{2,0},{3,1},{4,2},{5,3},{6,4},{7,5},{8,14},{9,15},{10,... | collective-permute-start | bytes 1572872 | tf_op jit(solution)/shard_map/ppermute | solution.py:198
  90.2 22.7 %collective-permute-start.4 = (bf16[4,2,16,16,128]{4,3,2,1,0:T(8,128)(2,1)S(1)}, bf16[4,2,16,16,128]{4,3,2,1,0:T(8,128)(2,1)S(1)}, u32[]{:S(2)}, u32[]{:S(2)}) collective-permute-start(bf16[4,2,16,16,128]{4,3,2,1,0:T(8,128)(2,1)S(1)} %joined.1.refs_0_), channel_id=1, source_target_pairs={{0,4},{1,5},{2,6},{3,7},{4,0},{5,1},{6,2},{7,3},{8,12},{9,13},{10,... | collective-permute-start | bytes 1572872 | tf_op jit(solution)/shard_map/ppermute | solution.py:198
  92.8 25.8 %collective-permute-start.3 = (bf16[4,2,16,16,128]{4,3,2,1,0:T(8,128)(2,1)S(1)}, bf16[4,2,16,16,128]{4,3,2,1,0:T(8,128)(2,1)S(1)}, u32[]{:S(2)}, u32[]{:S(2)}) collective-permute-start(bf16[4,2,16,16,128]{4,3,2,1,0:T(8,128)(2,1)S(1)} %joined.1.refs_0_), channel_id=1, source_target_pairs={{0,2},{1,3},{2,4},{3,5},{4,6},{5,7},{6,0},{7,1},{8,10},{9,11},{10,... | collective-permute-start | bytes 1572872 | tf_op jit(solution)/shard_map/ppermute | solution.py:198
  128.4 14.2 %all-to-all-start.3 = ((bf16[4,2,4,2,32,128]{5,4,3,2,1,0:T(8,128)(2,1)}), bf16[4,2,4,2,32,128]{5,4,3,2,1,0:T(8,128)(2,1)S(1)}, u32[]{:S(2)}, u32[]{:S(2)}) async-start(bf16[4,2,4,2,32,128]{5,4,3,2,1,0:T(8,128)(2,1)} %ladder.1), calls=%async_computation.3 | async-start | bytes 1048576 | tf_op jit(solution)/shard_map/all_to_all | solution.py:249
  142.6 17.6 %collective-permute-start.6 = (bf16[2,4,2,16,128]{4,3,2,1,0:T(8,128)(2,1)S(1)}, bf16[2,4,2,16,128]{4,3,2,1,0:T(8,128)(2,1)S(1)}, u32[]{:S(2)}, u32[]{:S(2)}) collective-permute-start(bf16[2,4,2,16,128]{4,3,2,1,0:T(8,128)(2,1)S(1)} %fusion.3), channel_id=1, source_target_pairs={{0,1},{1,0},{2,3},{3,2},{4,5},{5,4},{6,7},{7,6},{8,9},{9,8},{10,11... | collective-permute-start | bytes 196616 | tf_op jit(solution)/shard_map/ppermute | solution.py:204

commit v6 on v5

--- a/solution.py
+++ b/solution.py
@@ -5,6 +5,14 @@
 from jax.experimental.pallas import tpu as pltpu
 from jax.sharding import PartitionSpec as P
 
+ORDER = [
+    36, 0, 50, 59, 23, 52, 35, 28, 53, 32, 1, 30, 46, 27, 9, 10,
+    13, 60, 29, 54, 17, 62, 44, 57, 12, 14, 61, 16, 2, 25, 19, 48,
+    6, 55, 24, 5, 42, 33, 41, 58, 4, 38, 3, 39, 37, 20, 26, 51,
+    47, 21, 56, 31, 49, 34, 7, 63, 11, 18, 43, 22, 8, 45, 15, 40,
+]
+RANK = [ORDER.index(k) for k in range(64)]
+
 SMEM = pl.BlockSpec(memory_space=pltpu.SMEM)
 VMEM = pl.BlockSpec(memory_space=pltpu.VMEM)
 ANY = pl.BlockSpec(memory_space=pl.ANY)
@@ -19,11 +27,13 @@
 
 
 def exchange(value):
-    return lax.all_to_all(value, "ka", split_axis=0, concat_axis=0, tiled=True)
+    return lax.all_to_all(
+        value, "ka", split_axis=0, concat_axis=0, tiled=True, axis_index_groups=[ORDER]
+    )
 
 
 def exchange_both(value):
-    groups = [[k * 8 + 2 * y + h for h in range(2) for k in range(64)] for y in range(4)]
+    groups = [[k * 8 + 2 * y + h for h in range(2) for k in ORDER] for y in range(4)]
     return lax.all_to_all(
         value, ("ka", "vert"), split_axis=0, concat_axis=0, tiled=True, axis_index_groups=groups
     )
@@ -58,19 +68,19 @@
     )(high, *parts)
 
 
-def mirror_kernel(kminus_ref, rows_ref, shift_ref, row_ref, spread_ref, out_ref):
+def mirror_kernel(rank_ref, kminus_ref, rows_ref, shift_ref, row_ref, spread_ref, out_ref):
     target = kminus_ref[rows_ref[row_ref[0]], shift_ref[0]]
-    for k in range(64):
-        piece = spread_ref[kminus_ref[target, k], 6]
-        out_ref[k] = piece
-        out_ref[64 + k] = piece
+    for at, k in enumerate(ORDER):
+        piece = spread_ref[rank_ref[kminus_ref[target, k]], 6]
+        out_ref[at] = piece
+        out_ref[64 + at] = piece
 
 
 def mirror_pieces(lookup, row, spread):
     return pl.pallas_call(
         mirror_kernel,
         out_shape=jax.ShapeDtypeStruct((128, 4, 128), jnp.bfloat16),
-        in_specs=[SMEM] * 4 + [VMEM],
+        in_specs=[SMEM] * 5 + [VMEM],
         out_specs=VMEM,
         compiler_params=params(12),
         cost_estimate=pl.CostEstimate(flops=0, bytes_accessed=700000, transcendentals=0),
@@ -78,18 +88,20 @@
     )(*lookup, row, spread)
 
 
-def factor_kernel(kminus_ref, rows_ref, shift_ref, spread_ref, out_ref):
+def factor_kernel(rank_ref, kminus_ref, rows_ref, shift_ref, spread_ref, out_ref):
     for row in range(2):
         target = kminus_ref[rows_ref[row], shift_ref[0]]
-        for k in range(64):
-            out_ref[k, row * 6 : row * 6 + 6] = spread_ref[kminus_ref[target, k], 0:6]
+        for at, k in enumerate(ORDER):
+            out_ref[at, row * 6 : row * 6 + 6] = spread_ref[
+                rank_ref[kminus_ref[target, k]], 0:6
+            ]
 
 
 def factor_pieces(lookup, spread):
     return pl.pallas_call(
         factor_kernel,
         out_shape=jax.ShapeDtypeStruct((64, 12, 4, 128), jnp.bfloat16),
-        in_specs=[SMEM] * 3 + [VMEM],
+        in_specs=[SMEM] * 4 + [VMEM],
         out_specs=VMEM,
         compiler_params=params(12),
         cost_estimate=pl.CostEstimate(flops=0, bytes_accessed=1300000, transcendentals=0),
@@ -219,10 +231,11 @@
     vert = lax.axis_index("vert")
     high = lax.rem(vert, 2)
     level = lax.div(vert, 2)
-    lookup = (kminus, kj_rows, kshift)
+    rank = jnp.array(RANK, jnp.int32)
+    lookup = (rank, kminus, kj_rows, kshift)
     place = jnp.stack([lax.rem(level + 4 - turn, 4) * 32 for turn in range(4)]).astype(jnp.int32)
 
-    row = lax.div(lax.axis_index("ka"), 32).astype(jnp.int32).reshape(1)
+    row = lax.div(rank[lax.axis_index("ka")], 32).reshape(1)
 
     shard = amplitudes[:, 0]
     spread = exchange(

time: 161 us -> 156 us (0.969)
  waiting for transfers between devices: 71.9 us -> 67 us
  starting transfers between devices: 77 us -> 73.4 us
  between operations: 0.86 us -> 2.82 us
    ppermute x2, starting transfers between devices: 21.5 us -> 14.4 us  [swapped(): return lax.ppermute(value, 'vert', [(v, v ^ 1) for v in range(8)])]
    all_to_all x2, waiting for transfers between devices: 26.7 us -> 20.8 us  [exchange(): lax.all_to_all(value, 'ka', split_axis=0, concat_axis=0, tiled=True, axis...]
    ppermute x2, waiting for transfers between devices: 8.49 us -> 11.4 us  [swapped(): return lax.ppermute(value, 'vert', [(v, v ^ 1) for v in range(8)])]
    ppermute x1, waiting for transfers between devices: 2.85 us -> 0.67 us  [passed(): return lax.ppermute(value, 'ka', [(k, (k + 1) % 64) for k in range(64)])]
    all_to_all x1, starting transfers between devices: 12.3 us -> 14.3 us  [exchange_both(): lax.all_to_all(value, ('ka', 'vert'), split_axis=0, concat_axis=0, tiled=...]
    all_to_all x1, waiting for transfers between devices: 1.44 us -> 3.43 us  [exchange_both(): lax.all_to_all(value, ('ka', 'vert'), split_axis=0, concat_axis=0, tiled=...]
where the time goes in v6:
time: 156 us; the launch traced here: 155 us
  starting transfers between devices  73.4 us (47%)
  waiting for transfers between devices  67 us (43%)
  Pallas kernels  8.19 us (5%)
  other arithmetic  2.94 us (2%)
  between operations  2.82 us (2%)
    all_to_all x2, starting transfers between devices, exchange(): lax.all_to_all(value, 'ka', split_axis=0, concat_axis=0, tiled=True, axis...  25.9 us
    ppermute x3, waiting for transfers between devices, turned(): lax.ppermute(value, 'vert', [(v, (v + 2 * turn) % 8) for v in range(8)])  22.7 us
    all_to_all x2, waiting for transfers between devices, exchange(): lax.all_to_all(value, 'ka', split_axis=0, concat_axis=0, tiled=True, axis...  20.8 us
    ppermute x2, starting transfers between devices, swapped(): return lax.ppermute(value, 'vert', [(v, v ^ 1) for v in range(8)])  14.4 us
    all_to_all x1, starting transfers between devices, exchange_both(): lax.all_to_all(value, ('ka', 'vert'), split_axis=0, concat_axis=0, tiled=...  14.3 us
    ppermute x2, waiting for transfers between devices, swapped(): return lax.ppermute(value, 'vert', [(v, v ^ 1) for v in range(8)])  11.4 us
    ppermute x3, starting transfers between devices, turned(): lax.ppermute(value, 'vert', [(v, (v + 2 * turn) % 8) for v in range(8)])  10.3 us
    all_to_all x1, waiting for transfers between devices, per_device(): lax.all_to_all(partial, 'vert', split_axis=0, concat_axis=0, tiled=True,...  8.08 us
  transfers between devices with their start and end apart: 11, of which 8 were waited for; matrix products, arithmetic and copies ran while one was open for 0% of the time, Pallas kernels for 2%

profile of v6, /device:TPU:4, one launch (start us, length us, event | category | flops | bytes accessed | tf_op | source)
XLA Modules:
  0.0 155.0 jit_solution(4096641661004458639)
XLA Ops:
  0.0 2.1 %pad_maximum_fusion = bf16[64,7,4,128]{3,2,1,0:T(4,128)(2,1)} fusion(bf16[64,1,4,128]{3,2,1,0:T(4,128)(2,1)} %bitcast.56, bf16[64,6,4,128]{3,2,1,0:T(4,128)(2,1)} %bitcast.50), kind=kLoop, calls=%fused_computation.1 | loop fusion | flops 229376 | bytes 917504 | tf_op jit(solution)/shard_map/concatenate | solution.py:242
  2.1 0.0 copy-start.4
  2.1 0.0 copy-start.3
  2.1 14.6 %all-to-all-start = ((bf16[64,7,4,128]{3,2,1,0:T(4,128)(2,1)}), bf16[64,7,4,128]{3,2,1,0:T(4,128)(2,1)S(1)}, u32[]{:S(2)}, u32[]{:S(2)}) async-start(bf16[64,7,4,128]{3,2,1,0:T(4,128)(2,1)} %pad_maximum_fusion), calls=%async_computation | async-start | bytes 917504 | tf_op jit(solution)/shard_map/all_to_all | solution.py:30
  16.7 0.0 copy-start.1
  16.7 0.0 copy-done.4
  16.7 2.0 %collective-permute-start = (bf16[2,4,2,16,128]{4,3,2,1,0:T(8,128)(2,1)S(1)}, bf16[2,4,2,16,128]{4,3,2,1,0:T(8,128)(2,1)S(1)}, u32[]{:S(2)}, u32[]{:S(2)}) collective-permute-start(bf16[2,4,2,16,128]{4,3,2,1,0:T(8,128)(2,1)S(1)} %bitcast.57), channel_id=1, source_target_pairs={{0,8},{8,16},{16,24},{24,32},{32,40},{40,48},{48,56},{56,64},{64,7... | collective-permute-start | bytes 196616 | tf_op jit(solution)/shard_map/ppermute | solution.py:220
  18.7 0.0 copy-done.3
  18.7 0.6 dynamic_slice.3
  21.9 0.0 copy-start.2
  21.9 0.7 collective-permute-done
  22.6 17.4 %all-to-all-done.spread_ref = bf16[64,7,4,128]{3,2,1,0:T(4,128)(2,1)S(1)} async-done(((bf16[64,7,4,128]{3,2,1,0:T(4,128)(2,1)}), bf16[64,7,4,128]{3,2,1,0:T(4,128)(2,1)S(1)}, u32[]{:S(2)}, u32[]{:S(2)}) %all-to-all-start) | async-done | bytes 458784 | tf_op jit(solution)/shard_map/all_to_all | solution.py:30
  40.0 0.0 copy-done.1
  40.0 0.0 copy-done.2
  40.0 1.8 %mirror_pieces.1 = bf16[128,4,128]{2,1,0:T(4,128)(2,1)} custom-call(s32[64]{0:T(128)S(1)} %copy-done.3, s32[64,64]{1,0:T(8,128)S(1)} %copy-done.1, s32[2]{0:T(128)S(1)} %copy-done.2, s32[1]{0:T(128)S(6)} %copy.13.shift_ref, s32[1]{0:T(128)} %bitcast.11.row_ref, bf16[64,7,4,128]{3,2,1,0:T(4,128)(2,1)S(1)} %all-to-all-done.spread_ref), custom_call_target="tpu_custom_call" | custom-call | bytes 700000 | tf_op jit(solution)/shard_map/mirror_pieces/pallas_call | solution.py:80
  41.8 14.3 %all-to-all-start.1 = ((bf16[128,4,128]{2,1,0:T(4,128)(2,1)}), bf16[128,4,128]{2,1,0:T(4,128)(2,1)S(1)}, u32[]{:S(2)}, u32[]{:S(2)}) async-start(bf16[128,4,128]{2,1,0:T(4,128)(2,1)} %mirror_pieces.1), calls=%async_computation.1 | async-start | bytes 262144 | tf_op jit(solution)/shard_map/all_to_all | solution.py:37
  56.1 2.2 %factor_pieces.1 = bf16[64,12,4,128]{3,2,1,0:T(4,128)(2,1)} custom-call(s32[64]{0:T(128)S(1)} %copy-done.3, s32[64,64]{1,0:T(8,128)S(1)} %copy-done.1, s32[2]{0:T(128)S(1)} %copy-done.2, s32[1]{0:T(128)S(6)} %copy.13.shift_ref, bf16[64,7,4,128]{3,2,1,0:T(4,128)(2,1)S(1)} %all-to-all-done.spread_ref), custom_call_target="tpu_custom_call" | custom-call | bytes 1300000 | tf_op jit(solution)/shard_map/factor_pieces/pallas_call | solution.py:101
  58.4 7.7 %collective-permute-start.1 = (bf16[2,16,16,128]{3,2,1,0:T(8,128)(2,1)S(1)}, bf16[2,16,16,128]{3,2,1,0:T(8,128)(2,1)S(1)}, u32[]{:S(2)}, u32[]{:S(2)}) collective-permute-start(bf16[2,16,16,128]{3,2,1,0:T(8,128)(2,1)S(1)} %pad_maximum_fusion.1.here_ref), channel_id=1, source_target_pairs={{0,1},{1,0},{2,3},{3,2},{4,5},{5,4},{6,7},{7,6},{8,9},{9,8},{10,11... | collective-permute-start | bytes 393224 | tf_op jit(solution)/shard_map/ppermute | solution.py:216
  66.1 3.4 %all-to-all-done.1 = bf16[128,4,128]{2,1,0:T(4,128)(2,1)S(1)} async-done(((bf16[128,4,128]{2,1,0:T(4,128)(2,1)}), bf16[128,4,128]{2,1,0:T(4,128)(2,1)S(1)}, u32[]{:S(2)}, u32[]{:S(2)}) %all-to-all-start.1) | async-done | bytes 131104 | tf_op jit(solution)/shard_map/all_to_all | solution.py:37
  69.5 2.0 %collective-permute-start.2 = (bf16[2,16,16,128]{3,2,1,0:T(8,128)(2,1)S(1)}, bf16[2,16,16,128]{3,2,1,0:T(8,128)(2,1)S(1)}, u32[]{:S(2)}, u32[]{:S(2)}) collective-permute-start(bf16[2,16,16,128]{3,2,1,0:T(8,128)(2,1)S(1)} %bitcast.52), channel_id=1, source_target_pairs={{0,8},{1,9},{2,10},{3,11},{4,12},{5,13},{6,14},{7,15},{8,16},{9,17... | collective-permute-start | bytes 393224 | tf_op jit(solution)/shard_map/ppermute | solution.py:227
  71.5 11.3 %all-to-all-start.2 = ((bf16[64,48,128]{2,1,0:T(8,128)(2,1)}), bf16[64,48,128]{2,1,0:T(8,128)(2,1)S(1)}, u32[]{:S(2)}, u32[]{:S(2)}) async-start(bf16[64,48,128]{2,1,0:T(8,128)(2,1)} %bitcast.14), calls=%async_computation.2 | async-start | bytes 1572864 | tf_op jit(solution)/shard_map/all_to_all | solution.py:30
  82.8 0.0 collective-permute-done.1.there_ref
  82.8 0.0 collective-permute-done.2.before_ref
  82.8 0.0 copy-start
  82.8 0.6 joined.1.refs_0_
  83.4 4.9 %collective-permute-start.5 = (bf16[4,2,16,16,128]{4,3,2,1,0:T(8,128)(2,1)S(1)}, bf16[4,2,16,16,128]{4,3,2,1,0:T(8,128)(2,1)S(1)}, u32[]{:S(2)}, u32[]{:S(2)}) collective-permute-start(bf16[4,2,16,16,128]{4,3,2,1,0:T(8,128)(2,1)S(1)} %joined.1.refs_0_), channel_id=1, source_target_pairs={{0,6},{1,7},{2,0},{3,1},{4,2},{5,3},{6,4},{7,5},{8,14},{9,15},{10,... | collective-permute-start | bytes 1572872 | tf_op jit(solution)/shard_map/ppermute | solution.py:210
  88.3 2.5 %collective-permute-start.4 = (bf16[4,2,16,16,128]{4,3,2,1,0:T(8,128)(2,1)S(1)}, bf16[4,2,16,16,128]{4,3,2,1,0:T(8,128)(2,1)S(1)}, u32[]{:S(2)}, u32[]{:S(2)}) collective-permute-start(bf16[4,2,16,16,128]{4,3,2,1,0:T(8,128)(2,1)S(1)} %joined.1.refs_0_), channel_id=1, source_target_pairs={{0,4},{1,5},{2,6},{3,7},{4,0},{5,1},{6,2},{7,3},{8,12},{9,13},{10,... | collective-permute-start | bytes 1572872 | tf_op jit(solution)/shard_map/ppermute | solution.py:210
  90.9 2.9 %collective-permute-start.3 = (bf16[4,2,16,16,128]{4,3,2,1,0:T(8,128)(2,1)S(1)}, bf16[4,2,16,16,128]{4,3,2,1,0:T(8,128)(2,1)S(1)}, u32[]{:S(2)}, u32[]{:S(2)}) collective-permute-start(bf16[4,2,16,16,128]{4,3,2,1,0:T(8,128)(2,1)S(1)} %joined.1.refs_0_), channel_id=1, source_target_pairs={{0,2},{1,3},{2,4},{3,5},{4,6},{5,7},{6,0},{7,1},{8,10},{9,11},{10,... | collective-permute-start | bytes 1572872 | tf_op jit(solution)/shard_map/ppermute | solution.py:210
  93.8 0.1 pad_add_fusion.place_ref
  93.9 17.1 %collective-permute-done.5.refs_3_ = bf16[4,2,16,16,128]{4,3,2,1,0:T(8,128)(2,1)S(1)} collective-permute-done((bf16[4,2,16,16,128]{4,3,2,1,0:T(8,128)(2,1)S(1)}, bf16[4,2,16,16,128]{4,3,2,1,0:T(8,128)(2,1)S(1)}, u32[]{:S(2)}, u32[]{:S(2)}) %collective-permute-start.5) | collective-permute-done | bytes 524320 | tf_op jit(solution)/shard_map/ppermute | solution.py:210
  111.0 0.0 collective-permute-done.4.refs_2_
  111.0 5.6 %collective-permute-done.3.refs_1_ = bf16[4,2,16,16,128]{4,3,2,1,0:T(8,128)(2,1)S(1)} collective-permute-done((bf16[4,2,16,16,128]{4,3,2,1,0:T(8,128)(2,1)S(1)}, bf16[4,2,16,16,128]{4,3,2,1,0:T(8,128)(2,1)S(1)}, u32[]{:S(2)}, u32[]{:S(2)}) %collective-permute-start.3) | collective-permute-done | bytes 524320 | tf_op jit(solution)/shard_map/ppermute | solution.py:210
  116.6 3.4 %all-to-all-done.2.refs_5_ = bf16[64,48,128]{2,1,0:T(8,128)(2,1)S(1)} async-done(((bf16[64,48,128]{2,1,0:T(8,128)(2,1)}), bf16[64,48,128]{2,1,0:T(8,128)(2,1)S(1)}, u32[]{:S(2)}, u32[]{:S(2)}) %all-to-all-start.2) | async-done | bytes 786464 | tf_op jit(solution)/shard_map/all_to_all | solution.py:30
  120.0 0.0 copy-done
  120.0 3.6 %ladder.1 = bf16[4,2,4,2,32,128]{5,4,3,2,1,0:T(8,128)(2,1)} custom-call(s32[4]{0:T(128)S(1)} %pad_add_fusion.place_ref, bf16[4,2,16,16,128]{4,3,2,1,0:T(8,128)(2,1)S(1)} %joined.1.refs_0_, bf16[4,2,16,16,128]{4,3,2,1,0:T(8,128)(2,1)S(1)} %collective-permute-done.3.refs_1_, bf16[4,2,16,16,128]{4,3,2,1,0:T(8,128)(2,1)S(1)} %collective-permute-done.4.refs_2_, ...), custom_call_target="tpu_custom_call" | custom-call | flops 1610612736 | bytes 4000000 | tf_op jit(solution)/shard_map/ladder/pallas_call | solution.py:188
  123.6 4.5 %all-to-all-start.3 = ((bf16[4,2,4,2,32,128]{5,4,3,2,1,0:T(8,128)(2,1)}), bf16[4,2,4,2,32,128]{5,4,3,2,1,0:T(8,128)(2,1)S(1)}, u32[]{:S(2)}, u32[]{:S(2)}) async-start(bf16[4,2,4,2,32,128]{5,4,3,2,1,0:T(8,128)(2,1)} %ladder.1), calls=%async_computation.3 | async-start | bytes 1048576 | tf_op jit(solution)/shard_map/all_to_all | solution.py:262
  128.1 8.1 %all-to-all-done.3 = bf16[4,2,4,2,32,128]{5,4,3,2,1,0:T(8,128)(2,1)S(1)} async-done(((bf16[4,2,4,2,32,128]{5,4,3,2,1,0:T(8,128)(2,1)}), bf16[4,2,4,2,32,128]{5,4,3,2,1,0:T(8,128)(2,1)S(1)}, u32[]{:S(2)}, u32[]{:S(2)}) %all-to-all-start.3) | async-done | bytes 524320 | tf_op jit(solution)/shard_map/all_to_all | solution.py:262
  136.2 0.1 convert_reduce_fusion
  136.3 6.7 %collective-permute-start.6 = (bf16[2,4,2,16,128]{4,3,2,1,0:T(8,128)(2,1)S(1)}, bf16[2,4,2,16,128]{4,3,2,1,0:T(8,128)(2,1)S(1)}, u32[]{:S(2)}, u32[]{:S(2)}) collective-permute-start(bf16[2,4,2,16,128]{4,3,2,1,0:T(8,128)(2,1)S(1)} %fusion.3), channel_id=1, source_target_pairs={{0,1},{1,0},{2,3},{3,2},{4,5},{5,4},{6,7},{7,6},{8,9},{9,8},{10,11... | collective-permute-start | bytes 196616 | tf_op jit(solution)/shard_map/ppermute | solution.py:216
  143.0 11.4 %collective-permute-done.6 = bf16[2,4,2,16,128]{4,3,2,1,0:T(8,128)(2,1)S(1)} collective-permute-done((bf16[2,4,2,16,128]{4,3,2,1,0:T(8,128)(2,1)S(1)}, bf16[2,4,2,16,128]{4,3,2,1,0:T(8,128)(2,1)S(1)}, u32[]{:S(2)}, u32[]{:S(2)}) %collective-permute-start.6) | collective-permute-done | bytes 65568 | tf_op jit(solution)/shard_map/ppermute | solution.py:216
  154.3 0.7 fusion.4
  (2 shorter events, 0.0 us)
Async XLA Ops:
  2.1 14.6 %copy-start.4 = (bf16[2,1,4,2,16,128]{5,4,3,2,1,0:T(8,128)(2,1)S(1)}, bf16[2,1,4,2,16,128]{5,4,3,2,1,0:T(8,128)(2,1)}, u32[]{:S(2)}) copy-start(bf16[2,1,4,2,16,128]{5,4,3,2,1,0:T(8,128)(2,1)} %param.6) | copy-start | bytes 196612
  2.1 16.6 %copy-start.3 = (s32[64]{0:T(128)S(1)}, s32[64]{0:T(128)}, u32[]{:S(2)}) copy-start(s32[64]{0:T(128)} %constant.48.clone.rank_ref) | copy-start | bytes 772
  2.1 37.8 %all-to-all-start = ((bf16[64,7,4,128]{3,2,1,0:T(4,128)(2,1)}), bf16[64,7,4,128]{3,2,1,0:T(4,128)(2,1)S(1)}, u32[]{:S(2)}, u32[]{:S(2)}) async-start(bf16[64,7,4,128]{3,2,1,0:T(4,128)(2,1)} %pad_maximum_fusion), calls=%async_computation | async-start | bytes 917504 | tf_op jit(solution)/shard_map/all_to_all | solution.py:30
  16.7 23.2 %copy-start.1 = (s32[64,64]{1,0:T(8,128)S(1)}, s32[64,64]{1,0:T(8,128)}, u32[]{:S(2)}) copy-start(s32[64,64]{1,0:T(8,128)} %kminus_ref.3) | copy-start | bytes 49156
  16.7 5.9 %collective-permute-start = (bf16[2,4,2,16,128]{4,3,2,1,0:T(8,128)(2,1)S(1)}, bf16[2,4,2,16,128]{4,3,2,1,0:T(8,128)(2,1)S(1)}, u32[]{:S(2)}, u32[]{:S(2)}) collective-permute-start(bf16[2,4,2,16,128]{4,3,2,1,0:T(8,128)(2,1)S(1)} %bitcast.57), channel_id=1, source_target_pairs={{0,8},{8,16},{16,24},{24,32},{32,40},{40,48},{48,56},{56,64},{64,7... | collective-permute-start | bytes 196616 | tf_op jit(solution)/shard_map/ppermute | solution.py:220
  21.9 18.1 %copy-start.2 = (s32[2]{0:T(128)S(1)}, s32[2]{0:T(128)}, u32[]{:S(2)}) copy-start(s32[2]{0:T(128)} %rows_ref.3) | copy-start | bytes 28
  41.8 27.7 %all-to-all-start.1 = ((bf16[128,4,128]{2,1,0:T(4,128)(2,1)}), bf16[128,4,128]{2,1,0:T(4,128)(2,1)S(1)}, u32[]{:S(2)}, u32[]{:S(2)}) async-start(bf16[128,4,128]{2,1,0:T(4,128)(2,1)} %mirror_pieces.1), calls=%async_computation.1 | async-start | bytes 262144 | tf_op jit(solution)/shard_map/all_to_all | solution.py:37
  58.4 24.5 %collective-permute-start.1 = (bf16[2,16,16,128]{3,2,1,0:T(8,128)(2,1)S(1)}, bf16[2,16,16,128]{3,2,1,0:T(8,128)(2,1)S(1)}, u32[]{:S(2)}, u32[]{:S(2)}) collective-permute-start(bf16[2,16,16,128]{3,2,1,0:T(8,128)(2,1)S(1)} %pad_maximum_fusion.1.here_ref), channel_id=1, source_target_pairs={{0,1},{1,0},{2,3},{3,2},{4,5},{5,4},{6,7},{7,6},{8,9},{9,8},{10,11... | collective-permute-start | bytes 393224 | tf_op jit(solution)/shard_map/ppermute | solution.py:216
  69.5 13.3 %collective-permute-start.2 = (bf16[2,16,16,128]{3,2,1,0:T(8,128)(2,1)S(1)}, bf16[2,16,16,128]{3,2,1,0:T(8,128)(2,1)S(1)}, u32[]{:S(2)}, u32[]{:S(2)}) collective-permute-start(bf16[2,16,16,128]{3,2,1,0:T(8,128)(2,1)S(1)} %bitcast.52), channel_id=1, source_target_pairs={{0,8},{1,9},{2,10},{3,11},{4,12},{5,13},{6,14},{7,15},{8,16},{9,17... | collective-permute-start | bytes 393224 | tf_op jit(solution)/shard_map/ppermute | solution.py:227
  71.5 48.5 %all-to-all-start.2 = ((bf16[64,48,128]{2,1,0:T(8,128)(2,1)}), bf16[64,48,128]{2,1,0:T(8,128)(2,1)S(1)}, u32[]{:S(2)}, u32[]{:S(2)}) async-start(bf16[64,48,128]{2,1,0:T(8,128)(2,1)} %bitcast.14), calls=%async_computation.2 | async-start | bytes 1572864 | tf_op jit(solution)/shard_map/all_to_all | solution.py:30
  82.8 37.2 %copy-start = (bf16[2,1,2,3,128,128]{5,4,3,2,1,0:T(8,128)(2,1)S(1)}, bf16[2,1,2,3,128,128]{5,4,3,2,1,0:T(8,128)(2,1)}, u32[]{:S(2)}) copy-start(bf16[2,1,2,3,128,128]{5,4,3,2,1,0:T(8,128)(2,1)} %param.7) | copy-start | bytes 1179652
  83.4 27.6 %collective-permute-start.5 = (bf16[4,2,16,16,128]{4,3,2,1,0:T(8,128)(2,1)S(1)}, bf16[4,2,16,16,128]{4,3,2,1,0:T(8,128)(2,1)S(1)}, u32[]{:S(2)}, u32[]{:S(2)}) collective-permute-start(bf16[4,2,16,16,128]{4,3,2,1,0:T(8,128)(2,1)S(1)} %joined.1.refs_0_), channel_id=1, source_target_pairs={{0,6},{1,7},{2,0},{3,1},{4,2},{5,3},{6,4},{7,5},{8,14},{9,15},{10,... | collective-permute-start | bytes 1572872 | tf_op jit(solution)/shard_map/ppermute | solution.py:210
  88.3 22.6 %collective-permute-start.4 = (bf16[4,2,16,16,128]{4,3,2,1,0:T(8,128)(2,1)S(1)}, bf16[4,2,16,16,128]{4,3,2,1,0:T(8,128)(2,1)S(1)}, u32[]{:S(2)}, u32[]{:S(2)}) collective-permute-start(bf16[4,2,16,16,128]{4,3,2,1,0:T(8,128)(2,1)S(1)} %joined.1.refs_0_), channel_id=1, source_target_pairs={{0,4},{1,5},{2,6},{3,7},{4,0},{5,1},{6,2},{7,3},{8,12},{9,13},{10,... | collective-permute-start | bytes 1572872 | tf_op jit(solution)/shard_map/ppermute | solution.py:210
  90.9 25.7 %collective-permute-start.3 = (bf16[4,2,16,16,128]{4,3,2,1,0:T(8,128)(2,1)S(1)}, bf16[4,2,16,16,128]{4,3,2,1,0:T(8,128)(2,1)S(1)}, u32[]{:S(2)}, u32[]{:S(2)}) collective-permute-start(bf16[4,2,16,16,128]{4,3,2,1,0:T(8,128)(2,1)S(1)} %joined.1.refs_0_), channel_id=1, source_target_pairs={{0,2},{1,3},{2,4},{3,5},{4,6},{5,7},{6,0},{7,1},{8,10},{9,11},{10,... | collective-permute-start | bytes 1572872 | tf_op jit(solution)/shard_map/ppermute | solution.py:210
  123.6 12.6 %all-to-all-start.3 = ((bf16[4,2,4,2,32,128]{5,4,3,2,1,0:T(8,128)(2,1)}), bf16[4,2,4,2,32,128]{5,4,3,2,1,0:T(8,128)(2,1)S(1)}, u32[]{:S(2)}, u32[]{:S(2)}) async-start(bf16[4,2,4,2,32,128]{5,4,3,2,1,0:T(8,128)(2,1)} %ladder.1), calls=%async_computation.3 | async-start | bytes 1048576 | tf_op jit(solution)/shard_map/all_to_all | solution.py:262
  136.3 18.1 %collective-permute-start.6 = (bf16[2,4,2,16,128]{4,3,2,1,0:T(8,128)(2,1)S(1)}, bf16[2,4,2,16,128]{4,3,2,1,0:T(8,128)(2,1)S(1)}, u32[]{:S(2)}, u32[]{:S(2)}) collective-permute-start(bf16[2,4,2,16,128]{4,3,2,1,0:T(8,128)(2,1)S(1)} %fusion.3), channel_id=1, source_target_pairs={{0,1},{1,0},{2,3},{3,2},{4,5},{5,4},{6,7},{7,6},{8,9},{9,8},{10,11... | collective-permute-start | bytes 196616 | tf_op jit(solution)/shard_map/ppermute | solution.py:216

commit v7 on v6

--- a/solution.py
+++ b/solution.py
@@ -6,10 +6,10 @@
 from jax.sharding import PartitionSpec as P
 
 ORDER = [
-    36, 0, 50, 59, 23, 52, 35, 28, 53, 32, 1, 30, 46, 27, 9, 10,
-    13, 60, 29, 54, 17, 62, 44, 57, 12, 14, 61, 16, 2, 25, 19, 48,
-    6, 55, 24, 5, 42, 33, 41, 58, 4, 38, 3, 39, 37, 20, 26, 51,
-    47, 21, 56, 31, 49, 34, 7, 63, 11, 18, 43, 22, 8, 45, 15, 40,
+    29, 59, 17, 8, 28, 7, 44, 46, 23, 57, 24, 21, 51, 43, 47, 19,
+    31, 55, 4, 1, 15, 14, 45, 37, 26, 9, 42, 62, 61, 20, 16, 38,
+    54, 41, 32, 30, 33, 39, 36, 35, 53, 18, 50, 56, 40, 0, 10, 63,
+    34, 25, 13, 5, 52, 60, 22, 48, 12, 58, 3, 2, 49, 6, 27, 11,
 ]
 RANK = [ORDER.index(k) for k in range(64)]
 

time: 156 us -> 153 us (0.981)
  the two profiles are of different devices: /device:TPU:4 before, /device:TPU:36 now
where the time goes in v7:
time: 153 us; the launch traced here: 152 us
  starting transfers between devices  71 us (46%)
  waiting for transfers between devices  66.8 us (44%)
  Pallas kernels  8.18 us (5%)
  other arithmetic  2.94 us (2%)
  between operations  2.8 us (2%)
    ppermute x3, waiting for transfers between devices, turned(): lax.ppermute(value, 'vert', [(v, (v + 2 * turn) % 8) for v in range(8)])  22.3 us
    all_to_all x2, starting transfers between devices, exchange(): lax.all_to_all(value, 'ka', split_axis=0, concat_axis=0, tiled=True, axis...  19.8 us
    ppermute x2, starting transfers between devices, swapped(): return lax.ppermute(value, 'vert', [(v, v ^ 1) for v in range(8)])  19.8 us
    all_to_all x2, waiting for transfers between devices, exchange(): lax.all_to_all(value, 'ka', split_axis=0, concat_axis=0, tiled=True, axis...  18.6 us
    all_to_all x1, starting transfers between devices, exchange_both(): lax.all_to_all(value, ('ka', 'vert'), split_axis=0, concat_axis=0, tiled=...  12.1 us
    ppermute x2, waiting for transfers between devices, swapped(): return lax.ppermute(value, 'vert', [(v, v ^ 1) for v in range(8)])  11.1 us
    all_to_all x1, waiting for transfers between devices, per_device(): lax.all_to_all(partial, 'vert', split_axis=0, concat_axis=0, tiled=True,...  10.9 us
    ppermute x3, starting transfers between devices, turned(): lax.ppermute(value, 'vert', [(v, (v + 2 * turn) % 8) for v in range(8)])  10.3 us
  transfers between devices with their start and end apart: 11, of which 9 were waited for; matrix products, arithmetic and copies ran while one was open for 0% of the time, Pallas kernels for 2%

profile of v7, /device:TPU:36, one launch (start us, length us, event | category | flops | bytes accessed | tf_op | source)
XLA Modules:
  0.0 152.3 jit_solution(11254801680730167014)
XLA Ops:
  0.0 2.1 %pad_maximum_fusion = bf16[64,7,4,128]{3,2,1,0:T(4,128)(2,1)} fusion(bf16[64,1,4,128]{3,2,1,0:T(4,128)(2,1)} %bitcast.56, bf16[64,6,4,128]{3,2,1,0:T(4,128)(2,1)} %bitcast.50), kind=kLoop, calls=%fused_computation.1 | loop fusion | flops 229376 | bytes 917504 | tf_op jit(solution)/shard_map/concatenate | solution.py:242
  2.1 0.0 copy-start.4
  2.1 0.0 copy-start.3
  2.1 13.0 %all-to-all-start = ((bf16[64,7,4,128]{3,2,1,0:T(4,128)(2,1)}), bf16[64,7,4,128]{3,2,1,0:T(4,128)(2,1)S(1)}, u32[]{:S(2)}, u32[]{:S(2)}) async-start(bf16[64,7,4,128]{3,2,1,0:T(4,128)(2,1)} %pad_maximum_fusion), calls=%async_computation | async-start | bytes 917504 | tf_op jit(solution)/shard_map/all_to_all | solution.py:30
  15.2 0.0 copy-start.1
  15.2 0.0 copy-done.4
  15.2 2.0 %collective-permute-start = (bf16[2,4,2,16,128]{4,3,2,1,0:T(8,128)(2,1)S(1)}, bf16[2,4,2,16,128]{4,3,2,1,0:T(8,128)(2,1)S(1)}, u32[]{:S(2)}, u32[]{:S(2)}) collective-permute-start(bf16[2,4,2,16,128]{4,3,2,1,0:T(8,128)(2,1)S(1)} %bitcast.57), channel_id=1, source_target_pairs={{0,8},{8,16},{16,24},{24,32},{32,40},{40,48},{48,56},{56,64},{64,7... | collective-permute-start | bytes 196616 | tf_op jit(solution)/shard_map/ppermute | solution.py:220
  17.2 0.0 copy-done.3
  17.2 0.6 dynamic_slice.3
  20.4 0.0 copy-start.2
  20.4 0.9 collective-permute-done
  21.3 16.9 %all-to-all-done.spread_ref = bf16[64,7,4,128]{3,2,1,0:T(4,128)(2,1)S(1)} async-done(((bf16[64,7,4,128]{3,2,1,0:T(4,128)(2,1)}), bf16[64,7,4,128]{3,2,1,0:T(4,128)(2,1)S(1)}, u32[]{:S(2)}, u32[]{:S(2)}) %all-to-all-start) | async-done | bytes 458784 | tf_op jit(solution)/shard_map/all_to_all | solution.py:30
  38.2 0.0 copy-done.1
  38.2 0.0 copy-done.2
  38.2 1.8 %mirror_pieces.1 = bf16[128,4,128]{2,1,0:T(4,128)(2,1)} custom-call(s32[64]{0:T(128)S(1)} %copy-done.3, s32[64,64]{1,0:T(8,128)S(1)} %copy-done.1, s32[2]{0:T(128)S(1)} %copy-done.2, s32[1]{0:T(128)S(6)} %copy.13.shift_ref, s32[1]{0:T(128)} %bitcast.11.row_ref, bf16[64,7,4,128]{3,2,1,0:T(4,128)(2,1)S(1)} %all-to-all-done.spread_ref), custom_call_target="tpu_custom_call" | custom-call | bytes 700000 | tf_op jit(solution)/shard_map/mirror_pieces/pallas_call | solution.py:80
  40.0 12.1 %all-to-all-start.1 = ((bf16[128,4,128]{2,1,0:T(4,128)(2,1)}), bf16[128,4,128]{2,1,0:T(4,128)(2,1)S(1)}, u32[]{:S(2)}, u32[]{:S(2)}) async-start(bf16[128,4,128]{2,1,0:T(4,128)(2,1)} %mirror_pieces.1), calls=%async_computation.1 | async-start | bytes 262144 | tf_op jit(solution)/shard_map/all_to_all | solution.py:37
  52.1 2.2 %factor_pieces.1 = bf16[64,12,4,128]{3,2,1,0:T(4,128)(2,1)} custom-call(s32[64]{0:T(128)S(1)} %copy-done.3, s32[64,64]{1,0:T(8,128)S(1)} %copy-done.1, s32[2]{0:T(128)S(1)} %copy-done.2, s32[1]{0:T(128)S(6)} %copy.13.shift_ref, bf16[64,7,4,128]{3,2,1,0:T(4,128)(2,1)S(1)} %all-to-all-done.spread_ref), custom_call_target="tpu_custom_call" | custom-call | bytes 1300000 | tf_op jit(solution)/shard_map/factor_pieces/pallas_call | solution.py:101
  54.3 10.7 %collective-permute-start.1 = (bf16[2,16,16,128]{3,2,1,0:T(8,128)(2,1)S(1)}, bf16[2,16,16,128]{3,2,1,0:T(8,128)(2,1)S(1)}, u32[]{:S(2)}, u32[]{:S(2)}) collective-permute-start(bf16[2,16,16,128]{3,2,1,0:T(8,128)(2,1)S(1)} %pad_maximum_fusion.1.here_ref), channel_id=1, source_target_pairs={{0,1},{1,0},{2,3},{3,2},{4,5},{5,4},{6,7},{7,6},{8,9},{9,8},{10,11... | collective-permute-start | bytes 393224 | tf_op jit(solution)/shard_map/ppermute | solution.py:216
  65.1 3.0 %all-to-all-done.1 = bf16[128,4,128]{2,1,0:T(4,128)(2,1)S(1)} async-done(((bf16[128,4,128]{2,1,0:T(4,128)(2,1)}), bf16[128,4,128]{2,1,0:T(4,128)(2,1)S(1)}, u32[]{:S(2)}, u32[]{:S(2)}) %all-to-all-start.1) | async-done | bytes 131104 | tf_op jit(solution)/shard_map/all_to_all | solution.py:37
  68.1 2.4 %collective-permute-start.2 = (bf16[2,16,16,128]{3,2,1,0:T(8,128)(2,1)S(1)}, bf16[2,16,16,128]{3,2,1,0:T(8,128)(2,1)S(1)}, u32[]{:S(2)}, u32[]{:S(2)}) collective-permute-start(bf16[2,16,16,128]{3,2,1,0:T(8,128)(2,1)S(1)} %bitcast.52), channel_id=1, source_target_pairs={{0,8},{1,9},{2,10},{3,11},{4,12},{5,13},{6,14},{7,15},{8,16},{9,17... | collective-permute-start | bytes 393224 | tf_op jit(solution)/shard_map/ppermute | solution.py:227
  70.5 6.8 %all-to-all-start.2 = ((bf16[64,48,128]{2,1,0:T(8,128)(2,1)}), bf16[64,48,128]{2,1,0:T(8,128)(2,1)S(1)}, u32[]{:S(2)}, u32[]{:S(2)}) async-start(bf16[64,48,128]{2,1,0:T(8,128)(2,1)} %bitcast.14), calls=%async_computation.2 | async-start | bytes 1572864 | tf_op jit(solution)/shard_map/all_to_all | solution.py:30
  77.3 1.9 %collective-permute-done.1.there_ref = bf16[2,16,16,128]{3,2,1,0:T(8,128)(2,1)S(1)} collective-permute-done((bf16[2,16,16,128]{3,2,1,0:T(8,128)(2,1)S(1)}, bf16[2,16,16,128]{3,2,1,0:T(8,128)(2,1)S(1)}, u32[]{:S(2)}, u32[]{:S(2)}) %collective-permute-start.1) | collective-permute-done | bytes 131104 | tf_op jit(solution)/shard_map/ppermute | solution.py:216
  79.3 0.0 collective-permute-done.2.before_ref
  79.3 0.0 copy-start
  79.3 0.5 joined.1.refs_0_
  79.8 4.9 %collective-permute-start.5 = (bf16[4,2,16,16,128]{4,3,2,1,0:T(8,128)(2,1)S(1)}, bf16[4,2,16,16,128]{4,3,2,1,0:T(8,128)(2,1)S(1)}, u32[]{:S(2)}, u32[]{:S(2)}) collective-permute-start(bf16[4,2,16,16,128]{4,3,2,1,0:T(8,128)(2,1)S(1)} %joined.1.refs_0_), channel_id=1, source_target_pairs={{0,6},{1,7},{2,0},{3,1},{4,2},{5,3},{6,4},{7,5},{8,14},{9,15},{10,... | collective-permute-start | bytes 1572872 | tf_op jit(solution)/shard_map/ppermute | solution.py:210
  84.8 2.5 %collective-permute-start.4 = (bf16[4,2,16,16,128]{4,3,2,1,0:T(8,128)(2,1)S(1)}, bf16[4,2,16,16,128]{4,3,2,1,0:T(8,128)(2,1)S(1)}, u32[]{:S(2)}, u32[]{:S(2)}) collective-permute-start(bf16[4,2,16,16,128]{4,3,2,1,0:T(8,128)(2,1)S(1)} %joined.1.refs_0_), channel_id=1, source_target_pairs={{0,4},{1,5},{2,6},{3,7},{4,0},{5,1},{6,2},{7,3},{8,12},{9,13},{10,... | collective-permute-start | bytes 1572872 | tf_op jit(solution)/shard_map/ppermute | solution.py:210
  87.3 2.9 %collective-permute-start.3 = (bf16[4,2,16,16,128]{4,3,2,1,0:T(8,128)(2,1)S(1)}, bf16[4,2,16,16,128]{4,3,2,1,0:T(8,128)(2,1)S(1)}, u32[]{:S(2)}, u32[]{:S(2)}) collective-permute-start(bf16[4,2,16,16,128]{4,3,2,1,0:T(8,128)(2,1)S(1)} %joined.1.refs_0_), channel_id=1, source_target_pairs={{0,2},{1,3},{2,4},{3,5},{4,6},{5,7},{6,0},{7,1},{8,10},{9,11},{10,... | collective-permute-start | bytes 1572872 | tf_op jit(solution)/shard_map/ppermute | solution.py:210
  90.2 0.1 pad_add_fusion.place_ref
  90.3 16.7 %collective-permute-done.5.refs_3_ = bf16[4,2,16,16,128]{4,3,2,1,0:T(8,128)(2,1)S(1)} collective-permute-done((bf16[4,2,16,16,128]{4,3,2,1,0:T(8,128)(2,1)S(1)}, bf16[4,2,16,16,128]{4,3,2,1,0:T(8,128)(2,1)S(1)}, u32[]{:S(2)}, u32[]{:S(2)}) %collective-permute-start.5) | collective-permute-done | bytes 524320 | tf_op jit(solution)/shard_map/ppermute | solution.py:210
  107.0 0.0 collective-permute-done.4.refs_2_
  107.0 5.6 %collective-permute-done.3.refs_1_ = bf16[4,2,16,16,128]{4,3,2,1,0:T(8,128)(2,1)S(1)} collective-permute-done((bf16[4,2,16,16,128]{4,3,2,1,0:T(8,128)(2,1)S(1)}, bf16[4,2,16,16,128]{4,3,2,1,0:T(8,128)(2,1)S(1)}, u32[]{:S(2)}, u32[]{:S(2)}) %collective-permute-start.3) | collective-permute-done | bytes 524320 | tf_op jit(solution)/shard_map/ppermute | solution.py:210
  112.6 1.7 %all-to-all-done.2.refs_5_ = bf16[64,48,128]{2,1,0:T(8,128)(2,1)S(1)} async-done(((bf16[64,48,128]{2,1,0:T(8,128)(2,1)}), bf16[64,48,128]{2,1,0:T(8,128)(2,1)S(1)}, u32[]{:S(2)}, u32[]{:S(2)}) %all-to-all-start.2) | async-done | bytes 786464 | tf_op jit(solution)/shard_map/all_to_all | solution.py:30
  114.3 0.0 copy-done
  114.3 3.6 %ladder.1 = bf16[4,2,4,2,32,128]{5,4,3,2,1,0:T(8,128)(2,1)} custom-call(s32[4]{0:T(128)S(1)} %pad_add_fusion.place_ref, bf16[4,2,16,16,128]{4,3,2,1,0:T(8,128)(2,1)S(1)} %joined.1.refs_0_, bf16[4,2,16,16,128]{4,3,2,1,0:T(8,128)(2,1)S(1)} %collective-permute-done.3.refs_1_, bf16[4,2,16,16,128]{4,3,2,1,0:T(8,128)(2,1)S(1)} %collective-permute-done.4.refs_2_, ...), custom_call_target="tpu_custom_call" | custom-call | flops 1610612736 | bytes 4000000 | tf_op jit(solution)/shard_map/ladder/pallas_call | solution.py:188
  117.9 4.5 %all-to-all-start.3 = ((bf16[4,2,4,2,32,128]{5,4,3,2,1,0:T(8,128)(2,1)}), bf16[4,2,4,2,32,128]{5,4,3,2,1,0:T(8,128)(2,1)S(1)}, u32[]{:S(2)}, u32[]{:S(2)}) async-start(bf16[4,2,4,2,32,128]{5,4,3,2,1,0:T(8,128)(2,1)} %ladder.1), calls=%async_computation.3 | async-start | bytes 1048576 | tf_op jit(solution)/shard_map/all_to_all | solution.py:262
  122.4 10.9 %all-to-all-done.3 = bf16[4,2,4,2,32,128]{5,4,3,2,1,0:T(8,128)(2,1)S(1)} async-done(((bf16[4,2,4,2,32,128]{5,4,3,2,1,0:T(8,128)(2,1)}), bf16[4,2,4,2,32,128]{5,4,3,2,1,0:T(8,128)(2,1)S(1)}, u32[]{:S(2)}, u32[]{:S(2)}) %all-to-all-start.3) | async-done | bytes 524320 | tf_op jit(solution)/shard_map/all_to_all | solution.py:262
  133.3 0.1 convert_reduce_fusion
  133.4 9.0 %collective-permute-start.6 = (bf16[2,4,2,16,128]{4,3,2,1,0:T(8,128)(2,1)S(1)}, bf16[2,4,2,16,128]{4,3,2,1,0:T(8,128)(2,1)S(1)}, u32[]{:S(2)}, u32[]{:S(2)}) collective-permute-start(bf16[2,4,2,16,128]{4,3,2,1,0:T(8,128)(2,1)S(1)} %fusion.3), channel_id=1, source_target_pairs={{0,1},{1,0},{2,3},{3,2},{4,5},{5,4},{6,7},{7,6},{8,9},{9,8},{10,11... | collective-permute-start | bytes 196616 | tf_op jit(solution)/shard_map/ppermute | solution.py:216
  142.4 9.2 %collective-permute-done.6 = bf16[2,4,2,16,128]{4,3,2,1,0:T(8,128)(2,1)S(1)} collective-permute-done((bf16[2,4,2,16,128]{4,3,2,1,0:T(8,128)(2,1)S(1)}, bf16[2,4,2,16,128]{4,3,2,1,0:T(8,128)(2,1)S(1)}, u32[]{:S(2)}, u32[]{:S(2)}) %collective-permute-start.6) | collective-permute-done | bytes 65568 | tf_op jit(solution)/shard_map/ppermute | solution.py:216
  151.6 0.7 fusion.4
  (2 shorter events, 0.0 us)
Async XLA Ops:
  2.1 13.1 %copy-start.4 = (bf16[2,1,4,2,16,128]{5,4,3,2,1,0:T(8,128)(2,1)S(1)}, bf16[2,1,4,2,16,128]{5,4,3,2,1,0:T(8,128)(2,1)}, u32[]{:S(2)}) copy-start(bf16[2,1,4,2,16,128]{5,4,3,2,1,0:T(8,128)(2,1)} %param.6) | copy-start | bytes 196612
  2.1 15.1 %copy-start.3 = (s32[64]{0:T(128)S(1)}, s32[64]{0:T(128)}, u32[]{:S(2)}) copy-start(s32[64]{0:T(128)} %constant.48.clone.rank_ref) | copy-start | bytes 772
  2.1 36.0 %all-to-all-start = ((bf16[64,7,4,128]{3,2,1,0:T(4,128)(2,1)}), bf16[64,7,4,128]{3,2,1,0:T(4,128)(2,1)S(1)}, u32[]{:S(2)}, u32[]{:S(2)}) async-start(bf16[64,7,4,128]{3,2,1,0:T(4,128)(2,1)} %pad_maximum_fusion), calls=%async_computation | async-start | bytes 917504 | tf_op jit(solution)/shard_map/all_to_all | solution.py:30
  15.2 23.0 %copy-start.1 = (s32[64,64]{1,0:T(8,128)S(1)}, s32[64,64]{1,0:T(8,128)}, u32[]{:S(2)}) copy-start(s32[64,64]{1,0:T(8,128)} %kminus_ref.3) | copy-start | bytes 49156
  15.2 6.1 %collective-permute-start = (bf16[2,4,2,16,128]{4,3,2,1,0:T(8,128)(2,1)S(1)}, bf16[2,4,2,16,128]{4,3,2,1,0:T(8,128)(2,1)S(1)}, u32[]{:S(2)}, u32[]{:S(2)}) collective-permute-start(bf16[2,4,2,16,128]{4,3,2,1,0:T(8,128)(2,1)S(1)} %bitcast.57), channel_id=1, source_target_pairs={{0,8},{8,16},{16,24},{24,32},{32,40},{40,48},{48,56},{56,64},{64,7... | collective-permute-start | bytes 196616 | tf_op jit(solution)/shard_map/ppermute | solution.py:220
  20.4 17.8 %copy-start.2 = (s32[2]{0:T(128)S(1)}, s32[2]{0:T(128)}, u32[]{:S(2)}) copy-start(s32[2]{0:T(128)} %rows_ref.3) | copy-start | bytes 28
  40.0 28.1 %all-to-all-start.1 = ((bf16[128,4,128]{2,1,0:T(4,128)(2,1)}), bf16[128,4,128]{2,1,0:T(4,128)(2,1)S(1)}, u32[]{:S(2)}, u32[]{:S(2)}) async-start(bf16[128,4,128]{2,1,0:T(4,128)(2,1)} %mirror_pieces.1), calls=%async_computation.1 | async-start | bytes 262144 | tf_op jit(solution)/shard_map/all_to_all | solution.py:37
  54.3 24.9 %collective-permute-start.1 = (bf16[2,16,16,128]{3,2,1,0:T(8,128)(2,1)S(1)}, bf16[2,16,16,128]{3,2,1,0:T(8,128)(2,1)S(1)}, u32[]{:S(2)}, u32[]{:S(2)}) collective-permute-start(bf16[2,16,16,128]{3,2,1,0:T(8,128)(2,1)S(1)} %pad_maximum_fusion.1.here_ref), channel_id=1, source_target_pairs={{0,1},{1,0},{2,3},{3,2},{4,5},{5,4},{6,7},{7,6},{8,9},{9,8},{10,11... | collective-permute-start | bytes 393224 | tf_op jit(solution)/shard_map/ppermute | solution.py:216
  68.1 11.2 %collective-permute-start.2 = (bf16[2,16,16,128]{3,2,1,0:T(8,128)(2,1)S(1)}, bf16[2,16,16,128]{3,2,1,0:T(8,128)(2,1)S(1)}, u32[]{:S(2)}, u32[]{:S(2)}) collective-permute-start(bf16[2,16,16,128]{3,2,1,0:T(8,128)(2,1)S(1)} %bitcast.52), channel_id=1, source_target_pairs={{0,8},{1,9},{2,10},{3,11},{4,12},{5,13},{6,14},{7,15},{8,16},{9,17... | collective-permute-start | bytes 393224 | tf_op jit(solution)/shard_map/ppermute | solution.py:227
  70.5 43.8 %all-to-all-start.2 = ((bf16[64,48,128]{2,1,0:T(8,128)(2,1)}), bf16[64,48,128]{2,1,0:T(8,128)(2,1)S(1)}, u32[]{:S(2)}, u32[]{:S(2)}) async-start(bf16[64,48,128]{2,1,0:T(8,128)(2,1)} %bitcast.14), calls=%async_computation.2 | async-start | bytes 1572864 | tf_op jit(solution)/shard_map/all_to_all | solution.py:30
  79.3 35.0 %copy-start = (bf16[2,1,2,3,128,128]{5,4,3,2,1,0:T(8,128)(2,1)S(1)}, bf16[2,1,2,3,128,128]{5,4,3,2,1,0:T(8,128)(2,1)}, u32[]{:S(2)}) copy-start(bf16[2,1,2,3,128,128]{5,4,3,2,1,0:T(8,128)(2,1)} %param.7) | copy-start | bytes 1179652
  79.8 27.2 %collective-permute-start.5 = (bf16[4,2,16,16,128]{4,3,2,1,0:T(8,128)(2,1)S(1)}, bf16[4,2,16,16,128]{4,3,2,1,0:T(8,128)(2,1)S(1)}, u32[]{:S(2)}, u32[]{:S(2)}) collective-permute-start(bf16[4,2,16,16,128]{4,3,2,1,0:T(8,128)(2,1)S(1)} %joined.1.refs_0_), channel_id=1, source_target_pairs={{0,6},{1,7},{2,0},{3,1},{4,2},{5,3},{6,4},{7,5},{8,14},{9,15},{10,... | collective-permute-start | bytes 1572872 | tf_op jit(solution)/shard_map/ppermute | solution.py:210
  84.8 22.2 %collective-permute-start.4 = (bf16[4,2,16,16,128]{4,3,2,1,0:T(8,128)(2,1)S(1)}, bf16[4,2,16,16,128]{4,3,2,1,0:T(8,128)(2,1)S(1)}, u32[]{:S(2)}, u32[]{:S(2)}) collective-permute-start(bf16[4,2,16,16,128]{4,3,2,1,0:T(8,128)(2,1)S(1)} %joined.1.refs_0_), channel_id=1, source_target_pairs={{0,4},{1,5},{2,6},{3,7},{4,0},{5,1},{6,2},{7,3},{8,12},{9,13},{10,... | collective-permute-start | bytes 1572872 | tf_op jit(solution)/shard_map/ppermute | solution.py:210
  87.3 25.3 %collective-permute-start.3 = (bf16[4,2,16,16,128]{4,3,2,1,0:T(8,128)(2,1)S(1)}, bf16[4,2,16,16,128]{4,3,2,1,0:T(8,128)(2,1)S(1)}, u32[]{:S(2)}, u32[]{:S(2)}) collective-permute-start(bf16[4,2,16,16,128]{4,3,2,1,0:T(8,128)(2,1)S(1)} %joined.1.refs_0_), channel_id=1, source_target_pairs={{0,2},{1,3},{2,4},{3,5},{4,6},{5,7},{6,0},{7,1},{8,10},{9,11},{10,... | collective-permute-start | bytes 1572872 | tf_op jit(solution)/shard_map/ppermute | solution.py:210
  117.9 15.3 %all-to-all-start.3 = ((bf16[4,2,4,2,32,128]{5,4,3,2,1,0:T(8,128)(2,1)}), bf16[4,2,4,2,32,128]{5,4,3,2,1,0:T(8,128)(2,1)S(1)}, u32[]{:S(2)}, u32[]{:S(2)}) async-start(bf16[4,2,4,2,32,128]{5,4,3,2,1,0:T(8,128)(2,1)} %ladder.1), calls=%async_computation.3 | async-start | bytes 1048576 | tf_op jit(solution)/shard_map/all_to_all | solution.py:262
  133.4 18.3 %collective-permute-start.6 = (bf16[2,4,2,16,128]{4,3,2,1,0:T(8,128)(2,1)S(1)}, bf16[2,4,2,16,128]{4,3,2,1,0:T(8,128)(2,1)S(1)}, u32[]{:S(2)}, u32[]{:S(2)}) collective-permute-start(bf16[2,4,2,16,128]{4,3,2,1,0:T(8,128)(2,1)S(1)} %fusion.3), channel_id=1, source_target_pairs={{0,1},{1,0},{2,3},{3,2},{4,5},{5,4},{6,7},{7,6},{8,9},{9,8},{10,11... | collective-permute-start | bytes 196616 | tf_op jit(solution)/shard_map/ppermute | solution.py:216

commit v8 on v7

--- a/solution.py
+++ b/solution.py
@@ -37,6 +37,34 @@
     return lax.all_to_all(
         value, ("ka", "vert"), split_axis=0, concat_axis=0, tiled=True, axis_index_groups=groups
     )
+
+
+def pack_kernel(factor_ref, shard_ref, out_ref, held, done):
+    first = pltpu.make_async_copy(factor_ref, held.at[:, 0:6], done.at[0])
+    second = pltpu.make_async_copy(shard_ref, held.at[:, 6:7], done.at[1])
+    first.start()
+    second.start()
+    first.wait()
+    second.wait()
+    last = pltpu.make_async_copy(held, out_ref, done.at[2])
+    last.start()
+    last.wait()
+
+
+def packed(factor, shard):
+    return pl.pallas_call(
+        pack_kernel,
+        out_shape=jax.ShapeDtypeStruct((64, 7, 4, 128), jnp.bfloat16),
+        in_specs=[ANY, ANY],
+        out_specs=ANY,
+        scratch_shapes=[
+            pltpu.VMEM((64, 7, 4, 128), jnp.bfloat16),
+            pltpu.SemaphoreType.DMA((3,)),
+        ],
+        compiler_params=params(56),
+        cost_estimate=pl.CostEstimate(flops=0, bytes_accessed=900000, transcendentals=0),
+        name="packed",
+    )(factor, shard)
 
 
 def join_kernel(high_ref, here_ref, there_ref, now_ref, before_ref, out_ref, done):
@@ -117,7 +145,7 @@
 
 def ladder_kernel(place_ref, *refs):
     turns = refs[0:4]
-    factor_ref, other_ref, out_ref, blocks, left, right, inner, arrived = refs[4:12]
+    factor_ref, other_ref, out_ref, blocks, left, right, inner, result, arrived, leaving = refs[4:14]
     copies = []
     for turn in range(4):
         for high in range(2):
@@ -139,6 +167,7 @@
             )
     for copy in copies:
         copy.wait()
+    leaves = []
     for row in range(2):
         other = jnp.concatenate(
             [wide(other_ref[m])[row * 24 : (row + 1) * 24] for m in range(64)], 0
@@ -179,9 +208,20 @@
             for part in range(2):
                 for place in range(4):
                     at = part * 128 + place * 32
-                    out_ref[place, row, occ, part] = total[
+                    result[row, place, occ, part] = total[
                         at : at + 32, occ * 128 : (occ + 1) * 128
                     ]
+        copies = [
+            pltpu.make_async_copy(
+                result.at[row, place], out_ref.at[place, row], leaving.at[row * 4 + place]
+            )
+            for place in range(4)
+        ]
+        for copy in copies:
+            copy.start()
+        leaves = leaves + copies
+    for copy in leaves:
+        copy.wait()
 
 
 def ladder(place, turns, factor, other):
@@ -189,12 +229,14 @@
         ladder_kernel,
         out_shape=jax.ShapeDtypeStruct((4, 2, 4, 2, 32, 128), jnp.bfloat16),
         in_specs=[SMEM] + [ANY] * 4 + [VMEM, VMEM],
-        out_specs=VMEM,
+        out_specs=ANY,
         scratch_shapes=[
             pltpu.VMEM((4, 16, 128, 128), jnp.bfloat16),
             pltpu.VMEM((256, 1536), jnp.bfloat16),
             pltpu.VMEM((768, 256), jnp.bfloat16),
             pltpu.VMEM((1536, 512), jnp.bfloat16),
+            pltpu.VMEM((2, 4, 4, 2, 32, 128), jnp.bfloat16),
+            pltpu.SemaphoreType.DMA((8,)),
             pltpu.SemaphoreType.DMA((8,)),
         ],
         compiler_params=params(16),
@@ -239,7 +281,7 @@
 
     shard = amplitudes[:, 0]
     spread = exchange(
-        jnp.concatenate([factors[:, 0].reshape(64, 6, 4, 128), shard.reshape(64, 1, 4, 128)], 1)
+        packed(factors[:, 0].reshape(64, 6, 4, 128), shard.reshape(64, 1, 4, 128))
     )
     behind = passed(shard)
     spread, behind = lax.optimization_barrier((spread, behind))

time: 153 us -> 153 us (level)
  other arithmetic: 2.94 us -> 0.83 us
  Pallas kernels: 8.18 us -> 9.94 us
    concatenate x1 -> x0, other arithmetic: 2.11 us -> none  [per_device(): jnp.concatenate([factors[:, 0].reshape(64, 6, 4, 128), shard.reshape(64,...]
    pallas_call x0 -> x1, Pallas kernels: none -> 1.79 us  [packed(): pl.pallas_call(pack_kernel, out_shape=jax.ShapeDtypeStruct((64, 7, 4, 128...]
where the time goes in v8:
time: 153 us; the launch traced here: 152 us
  starting transfers between devices  71 us (46%)
  waiting for transfers between devices  66.8 us (44%)
  Pallas kernels  9.94 us (6%)
  between operations  2.82 us (2%)
    ppermute x3, waiting for transfers between devices, turned(): lax.ppermute(value, 'vert', [(v, (v + 2 * turn) % 8) for v in range(8)])  22.3 us
    all_to_all x2, starting transfers between devices, exchange(): lax.all_to_all(value, 'ka', split_axis=0, concat_axis=0, tiled=True, axis...  19.9 us
    ppermute x2, starting transfers between devices, swapped(): return lax.ppermute(value, 'vert', [(v, v ^ 1) for v in range(8)])  19.8 us
    all_to_all x2, waiting for transfers between devices, exchange(): lax.all_to_all(value, 'ka', split_axis=0, concat_axis=0, tiled=True, axis...  18.6 us
    all_to_all x1, starting transfers between devices, exchange_both(): lax.all_to_all(value, ('ka', 'vert'), split_axis=0, concat_axis=0, tiled=...  12.1 us
    ppermute x2, waiting for transfers between devices, swapped(): return lax.ppermute(value, 'vert', [(v, v ^ 1) for v in range(8)])  11.2 us
    all_to_all x1, waiting for transfers between devices, per_device(): lax.all_to_all(partial, 'vert', split_axis=0, concat_axis=0, tiled=True,...  10.9 us
    ppermute x3, starting transfers between devices, turned(): lax.ppermute(value, 'vert', [(v, (v + 2 * turn) % 8) for v in range(8)])  10.3 us
  transfers between devices with their start and end apart: 11, of which 9 were waited for; matrix products, arithmetic and copies ran while one was open for 0% of the time, Pallas kernels for 2%

profile of v8, /device:TPU:36, one launch (start us, length us, event | category | flops | bytes accessed | tf_op | source)
XLA Modules:
  0.0 152.0 jit_solution(17237539510990020491)
XLA Ops:
  0.0 1.8 %packed.1 = bf16[64,7,4,128]{3,2,1,0:T(4,128)(2,1)} custom-call(bf16[64,6,4,128]{3,2,1,0:T(4,128)(2,1)} %bitcast.50, bf16[64,1,4,128]{3,2,1,0:T(4,128)(2,1)} %bitcast.56), custom_call_target="tpu_custom_call" | custom-call | bytes 900000 | tf_op jit(solution)/shard_map/packed/pallas_call | solution.py:55
  1.8 0.0 copy-start.4
  1.8 0.0 copy-start.3
  1.8 13.1 %all-to-all-start = ((bf16[64,7,4,128]{3,2,1,0:T(4,128)(2,1)}), bf16[64,7,4,128]{3,2,1,0:T(4,128)(2,1)S(1)}, u32[]{:S(2)}, u32[]{:S(2)}) async-start(bf16[64,7,4,128]{3,2,1,0:T(4,128)(2,1)} %packed.1), calls=%async_computation | async-start | bytes 917504 | tf_op jit(solution)/shard_map/all_to_all | solution.py:30
  14.9 0.0 copy-start.1
  14.9 0.0 copy-done.4
  14.9 2.0 %collective-permute-start = (bf16[2,4,2,16,128]{4,3,2,1,0:T(8,128)(2,1)S(1)}, bf16[2,4,2,16,128]{4,3,2,1,0:T(8,128)(2,1)S(1)}, u32[]{:S(2)}, u32[]{:S(2)}) collective-permute-start(bf16[2,4,2,16,128]{4,3,2,1,0:T(8,128)(2,1)S(1)} %bitcast.57), channel_id=1, source_target_pairs={{0,8},{8,16},{16,24},{24,32},{32,40},{40,48},{48,56},{56,64},{64,7... | collective-permute-start | bytes 196616 | tf_op jit(solution)/shard_map/ppermute | solution.py:262
  16.9 0.0 copy-done.3
  16.9 0.6 dynamic_slice.3
  20.1 0.0 copy-start.2
  20.1 0.9 collective-permute-done
  21.0 16.9 %all-to-all-done.spread_ref = bf16[64,7,4,128]{3,2,1,0:T(4,128)(2,1)S(1)} async-done(((bf16[64,7,4,128]{3,2,1,0:T(4,128)(2,1)}), bf16[64,7,4,128]{3,2,1,0:T(4,128)(2,1)S(1)}, u32[]{:S(2)}, u32[]{:S(2)}) %all-to-all-start) | async-done | bytes 458784 | tf_op jit(solution)/shard_map/all_to_all | solution.py:30
  37.9 0.0 copy-done.1
  37.9 0.0 copy-done.2
  37.9 1.8 %mirror_pieces.1 = bf16[128,4,128]{2,1,0:T(4,128)(2,1)} custom-call(s32[64]{0:T(128)S(1)} %copy-done.3, s32[64,64]{1,0:T(8,128)S(1)} %copy-done.1, s32[2]{0:T(128)S(1)} %copy-done.2, s32[1]{0:T(128)S(6)} %copy.13.shift_ref, s32[1]{0:T(128)} %bitcast.11.row_ref, bf16[64,7,4,128]{3,2,1,0:T(4,128)(2,1)S(1)} %all-to-all-done.spread_ref), custom_call_target="tpu_custom_call" | custom-call | bytes 700000 | tf_op jit(solution)/shard_map/mirror_pieces/pallas_call | solution.py:108
  39.7 12.1 %all-to-all-start.1 = ((bf16[128,4,128]{2,1,0:T(4,128)(2,1)}), bf16[128,4,128]{2,1,0:T(4,128)(2,1)S(1)}, u32[]{:S(2)}, u32[]{:S(2)}) async-start(bf16[128,4,128]{2,1,0:T(4,128)(2,1)} %mirror_pieces.1), calls=%async_computation.1 | async-start | bytes 262144 | tf_op jit(solution)/shard_map/all_to_all | solution.py:37
  51.9 2.2 %factor_pieces.1 = bf16[64,12,4,128]{3,2,1,0:T(4,128)(2,1)} custom-call(s32[64]{0:T(128)S(1)} %copy-done.3, s32[64,64]{1,0:T(8,128)S(1)} %copy-done.1, s32[2]{0:T(128)S(1)} %copy-done.2, s32[1]{0:T(128)S(6)} %copy.13.shift_ref, bf16[64,7,4,128]{3,2,1,0:T(4,128)(2,1)S(1)} %all-to-all-done.spread_ref), custom_call_target="tpu_custom_call" | custom-call | bytes 1300000 | tf_op jit(solution)/shard_map/factor_pieces/pallas_call | solution.py:129
  54.1 10.7 %collective-permute-start.1 = (bf16[2,16,16,128]{3,2,1,0:T(8,128)(2,1)S(1)}, bf16[2,16,16,128]{3,2,1,0:T(8,128)(2,1)S(1)}, u32[]{:S(2)}, u32[]{:S(2)}) collective-permute-start(bf16[2,16,16,128]{3,2,1,0:T(8,128)(2,1)S(1)} %pad_maximum_fusion.here_ref), channel_id=1, source_target_pairs={{0,1},{1,0},{2,3},{3,2},{4,5},{5,4},{6,7},{7,6},{8,9},{9,8},{10,11... | collective-permute-start | bytes 393224 | tf_op jit(solution)/shard_map/ppermute | solution.py:258
  64.8 3.0 %all-to-all-done.1 = bf16[128,4,128]{2,1,0:T(4,128)(2,1)S(1)} async-done(((bf16[128,4,128]{2,1,0:T(4,128)(2,1)}), bf16[128,4,128]{2,1,0:T(4,128)(2,1)S(1)}, u32[]{:S(2)}, u32[]{:S(2)}) %all-to-all-start.1) | async-done | bytes 131104 | tf_op jit(solution)/shard_map/all_to_all | solution.py:37
  67.8 2.4 %collective-permute-start.2 = (bf16[2,16,16,128]{3,2,1,0:T(8,128)(2,1)S(1)}, bf16[2,16,16,128]{3,2,1,0:T(8,128)(2,1)S(1)}, u32[]{:S(2)}, u32[]{:S(2)}) collective-permute-start(bf16[2,16,16,128]{3,2,1,0:T(8,128)(2,1)S(1)} %bitcast.52), channel_id=1, source_target_pairs={{0,8},{1,9},{2,10},{3,11},{4,12},{5,13},{6,14},{7,15},{8,16},{9,17... | collective-permute-start | bytes 393224 | tf_op jit(solution)/shard_map/ppermute | solution.py:269
  70.2 6.8 %all-to-all-start.2 = ((bf16[64,48,128]{2,1,0:T(8,128)(2,1)}), bf16[64,48,128]{2,1,0:T(8,128)(2,1)S(1)}, u32[]{:S(2)}, u32[]{:S(2)}) async-start(bf16[64,48,128]{2,1,0:T(8,128)(2,1)} %bitcast.14), calls=%async_computation.2 | async-start | bytes 1572864 | tf_op jit(solution)/shard_map/all_to_all | solution.py:30
  77.1 1.9 %collective-permute-done.1.there_ref = bf16[2,16,16,128]{3,2,1,0:T(8,128)(2,1)S(1)} collective-permute-done((bf16[2,16,16,128]{3,2,1,0:T(8,128)(2,1)S(1)}, bf16[2,16,16,128]{3,2,1,0:T(8,128)(2,1)S(1)}, u32[]{:S(2)}, u32[]{:S(2)}) %collective-permute-start.1) | collective-permute-done | bytes 131104 | tf_op jit(solution)/shard_map/ppermute | solution.py:258
  79.0 0.0 collective-permute-done.2.before_ref
  79.0 0.0 copy-start
  79.0 0.5 joined.1.refs_0_
  79.5 4.9 %collective-permute-start.5 = (bf16[4,2,16,16,128]{4,3,2,1,0:T(8,128)(2,1)S(1)}, bf16[4,2,16,16,128]{4,3,2,1,0:T(8,128)(2,1)S(1)}, u32[]{:S(2)}, u32[]{:S(2)}) collective-permute-start(bf16[4,2,16,16,128]{4,3,2,1,0:T(8,128)(2,1)S(1)} %joined.1.refs_0_), channel_id=1, source_target_pairs={{0,6},{1,7},{2,0},{3,1},{4,2},{5,3},{6,4},{7,5},{8,14},{9,15},{10,... | collective-permute-start | bytes 1572872 | tf_op jit(solution)/shard_map/ppermute | solution.py:252
  84.5 2.5 %collective-permute-start.4 = (bf16[4,2,16,16,128]{4,3,2,1,0:T(8,128)(2,1)S(1)}, bf16[4,2,16,16,128]{4,3,2,1,0:T(8,128)(2,1)S(1)}, u32[]{:S(2)}, u32[]{:S(2)}) collective-permute-start(bf16[4,2,16,16,128]{4,3,2,1,0:T(8,128)(2,1)S(1)} %joined.1.refs_0_), channel_id=1, source_target_pairs={{0,4},{1,5},{2,6},{3,7},{4,0},{5,1},{6,2},{7,3},{8,12},{9,13},{10,... | collective-permute-start | bytes 1572872 | tf_op jit(solution)/shard_map/ppermute | solution.py:252
  87.0 2.9 %collective-permute-start.3 = (bf16[4,2,16,16,128]{4,3,2,1,0:T(8,128)(2,1)S(1)}, bf16[4,2,16,16,128]{4,3,2,1,0:T(8,128)(2,1)S(1)}, u32[]{:S(2)}, u32[]{:S(2)}) collective-permute-start(bf16[4,2,16,16,128]{4,3,2,1,0:T(8,128)(2,1)S(1)} %joined.1.refs_0_), channel_id=1, source_target_pairs={{0,2},{1,3},{2,4},{3,5},{4,6},{5,7},{6,0},{7,1},{8,10},{9,11},{10,... | collective-permute-start | bytes 1572872 | tf_op jit(solution)/shard_map/ppermute | solution.py:252
  89.9 0.1 pad_add_fusion.place_ref
  90.0 16.7 %collective-permute-done.5.refs_3_ = bf16[4,2,16,16,128]{4,3,2,1,0:T(8,128)(2,1)S(1)} collective-permute-done((bf16[4,2,16,16,128]{4,3,2,1,0:T(8,128)(2,1)S(1)}, bf16[4,2,16,16,128]{4,3,2,1,0:T(8,128)(2,1)S(1)}, u32[]{:S(2)}, u32[]{:S(2)}) %collective-permute-start.5) | collective-permute-done | bytes 524320 | tf_op jit(solution)/shard_map/ppermute | solution.py:252
  106.7 0.0 collective-permute-done.4.refs_2_
  106.7 5.6 %collective-permute-done.3.refs_1_ = bf16[4,2,16,16,128]{4,3,2,1,0:T(8,128)(2,1)S(1)} collective-permute-done((bf16[4,2,16,16,128]{4,3,2,1,0:T(8,128)(2,1)S(1)}, bf16[4,2,16,16,128]{4,3,2,1,0:T(8,128)(2,1)S(1)}, u32[]{:S(2)}, u32[]{:S(2)}) %collective-permute-start.3) | collective-permute-done | bytes 524320 | tf_op jit(solution)/shard_map/ppermute | solution.py:252
  112.3 1.7 %all-to-all-done.2.refs_5_ = bf16[64,48,128]{2,1,0:T(8,128)(2,1)S(1)} async-done(((bf16[64,48,128]{2,1,0:T(8,128)(2,1)}), bf16[64,48,128]{2,1,0:T(8,128)(2,1)S(1)}, u32[]{:S(2)}, u32[]{:S(2)}) %all-to-all-start.2) | async-done | bytes 786464 | tf_op jit(solution)/shard_map/all_to_all | solution.py:30
  114.0 0.0 copy-done
  114.0 3.6 %ladder.1 = bf16[4,2,4,2,32,128]{5,4,3,2,1,0:T(8,128)(2,1)} custom-call(s32[4]{0:T(128)S(1)} %pad_add_fusion.place_ref, bf16[4,2,16,16,128]{4,3,2,1,0:T(8,128)(2,1)S(1)} %joined.1.refs_0_, bf16[4,2,16,16,128]{4,3,2,1,0:T(8,128)(2,1)S(1)} %collective-permute-done.3.refs_1_, bf16[4,2,16,16,128]{4,3,2,1,0:T(8,128)(2,1)S(1)} %collective-permute-done.4.refs_2_, ...), custom_call_target="tpu_custom_call" | custom-call | flops 1610612736 | bytes 4000000 | tf_op jit(solution)/shard_map/ladder/pallas_call | solution.py:228
  117.6 4.5 %all-to-all-start.3 = ((bf16[4,2,4,2,32,128]{5,4,3,2,1,0:T(8,128)(2,1)}), bf16[4,2,4,2,32,128]{5,4,3,2,1,0:T(8,128)(2,1)S(1)}, u32[]{:S(2)}, u32[]{:S(2)}) async-start(bf16[4,2,4,2,32,128]{5,4,3,2,1,0:T(8,128)(2,1)} %ladder.1), calls=%async_computation.3 | async-start | bytes 1048576 | tf_op jit(solution)/shard_map/all_to_all | solution.py:304
  122.1 10.9 %all-to-all-done.3 = bf16[4,2,4,2,32,128]{5,4,3,2,1,0:T(8,128)(2,1)S(1)} async-done(((bf16[4,2,4,2,32,128]{5,4,3,2,1,0:T(8,128)(2,1)}), bf16[4,2,4,2,32,128]{5,4,3,2,1,0:T(8,128)(2,1)S(1)}, u32[]{:S(2)}, u32[]{:S(2)}) %all-to-all-start.3) | async-done | bytes 524320 | tf_op jit(solution)/shard_map/all_to_all | solution.py:304
  133.0 0.1 convert_reduce_fusion
  133.1 9.0 %collective-permute-start.6 = (bf16[2,4,2,16,128]{4,3,2,1,0:T(8,128)(2,1)S(1)}, bf16[2,4,2,16,128]{4,3,2,1,0:T(8,128)(2,1)S(1)}, u32[]{:S(2)}, u32[]{:S(2)}) collective-permute-start(bf16[2,4,2,16,128]{4,3,2,1,0:T(8,128)(2,1)S(1)} %fusion.3), channel_id=1, source_target_pairs={{0,1},{1,0},{2,3},{3,2},{4,5},{5,4},{6,7},{7,6},{8,9},{9,8},{10,11... | collective-permute-start | bytes 196616 | tf_op jit(solution)/shard_map/ppermute | solution.py:258
  142.1 9.2 %collective-permute-done.6 = bf16[2,4,2,16,128]{4,3,2,1,0:T(8,128)(2,1)S(1)} collective-permute-done((bf16[2,4,2,16,128]{4,3,2,1,0:T(8,128)(2,1)S(1)}, bf16[2,4,2,16,128]{4,3,2,1,0:T(8,128)(2,1)S(1)}, u32[]{:S(2)}, u32[]{:S(2)}) %collective-permute-start.6) | collective-permute-done | bytes 65568 | tf_op jit(solution)/shard_map/ppermute | solution.py:258
  151.3 0.7 fusion.4
  (2 shorter events, 0.0 us)
Async XLA Ops:
  1.8 13.1 %copy-start.4 = (bf16[2,1,4,2,16,128]{5,4,3,2,1,0:T(8,128)(2,1)S(1)}, bf16[2,1,4,2,16,128]{5,4,3,2,1,0:T(8,128)(2,1)}, u32[]{:S(2)}) copy-start(bf16[2,1,4,2,16,128]{5,4,3,2,1,0:T(8,128)(2,1)} %param.6) | copy-start | bytes 196612
  1.8 15.1 %copy-start.3 = (s32[64]{0:T(128)S(1)}, s32[64]{0:T(128)}, u32[]{:S(2)}) copy-start(s32[64]{0:T(128)} %constant.48.clone.rank_ref) | copy-start | bytes 772
  1.8 36.1 %all-to-all-start = ((bf16[64,7,4,128]{3,2,1,0:T(4,128)(2,1)}), bf16[64,7,4,128]{3,2,1,0:T(4,128)(2,1)S(1)}, u32[]{:S(2)}, u32[]{:S(2)}) async-start(bf16[64,7,4,128]{3,2,1,0:T(4,128)(2,1)} %packed.1), calls=%async_computation | async-start | bytes 917504 | tf_op jit(solution)/shard_map/all_to_all | solution.py:30
  14.9 23.0 %copy-start.1 = (s32[64,64]{1,0:T(8,128)S(1)}, s32[64,64]{1,0:T(8,128)}, u32[]{:S(2)}) copy-start(s32[64,64]{1,0:T(8,128)} %kminus_ref.3) | copy-start | bytes 49156
  14.9 6.1 %collective-permute-start = (bf16[2,4,2,16,128]{4,3,2,1,0:T(8,128)(2,1)S(1)}, bf16[2,4,2,16,128]{4,3,2,1,0:T(8,128)(2,1)S(1)}, u32[]{:S(2)}, u32[]{:S(2)}) collective-permute-start(bf16[2,4,2,16,128]{4,3,2,1,0:T(8,128)(2,1)S(1)} %bitcast.57), channel_id=1, source_target_pairs={{0,8},{8,16},{16,24},{24,32},{32,40},{40,48},{48,56},{56,64},{64,7... | collective-permute-start | bytes 196616 | tf_op jit(solution)/shard_map/ppermute | solution.py:262
  20.1 17.8 %copy-start.2 = (s32[2]{0:T(128)S(1)}, s32[2]{0:T(128)}, u32[]{:S(2)}) copy-start(s32[2]{0:T(128)} %rows_ref.3) | copy-start | bytes 28
  39.7 28.1 %all-to-all-start.1 = ((bf16[128,4,128]{2,1,0:T(4,128)(2,1)}), bf16[128,4,128]{2,1,0:T(4,128)(2,1)S(1)}, u32[]{:S(2)}, u32[]{:S(2)}) async-start(bf16[128,4,128]{2,1,0:T(4,128)(2,1)} %mirror_pieces.1), calls=%async_computation.1 | async-start | bytes 262144 | tf_op jit(solution)/shard_map/all_to_all | solution.py:37
  54.1 24.9 %collective-permute-start.1 = (bf16[2,16,16,128]{3,2,1,0:T(8,128)(2,1)S(1)}, bf16[2,16,16,128]{3,2,1,0:T(8,128)(2,1)S(1)}, u32[]{:S(2)}, u32[]{:S(2)}) collective-permute-start(bf16[2,16,16,128]{3,2,1,0:T(8,128)(2,1)S(1)} %pad_maximum_fusion.here_ref), channel_id=1, source_target_pairs={{0,1},{1,0},{2,3},{3,2},{4,5},{5,4},{6,7},{7,6},{8,9},{9,8},{10,11... | collective-permute-start | bytes 393224 | tf_op jit(solution)/shard_map/ppermute | solution.py:258
  67.8 11.2 %collective-permute-start.2 = (bf16[2,16,16,128]{3,2,1,0:T(8,128)(2,1)S(1)}, bf16[2,16,16,128]{3,2,1,0:T(8,128)(2,1)S(1)}, u32[]{:S(2)}, u32[]{:S(2)}) collective-permute-start(bf16[2,16,16,128]{3,2,1,0:T(8,128)(2,1)S(1)} %bitcast.52), channel_id=1, source_target_pairs={{0,8},{1,9},{2,10},{3,11},{4,12},{5,13},{6,14},{7,15},{8,16},{9,17... | collective-permute-start | bytes 393224 | tf_op jit(solution)/shard_map/ppermute | solution.py:269
  70.2 43.8 %all-to-all-start.2 = ((bf16[64,48,128]{2,1,0:T(8,128)(2,1)}), bf16[64,48,128]{2,1,0:T(8,128)(2,1)S(1)}, u32[]{:S(2)}, u32[]{:S(2)}) async-start(bf16[64,48,128]{2,1,0:T(8,128)(2,1)} %bitcast.14), calls=%async_computation.2 | async-start | bytes 1572864 | tf_op jit(solution)/shard_map/all_to_all | solution.py:30
  79.0 35.0 %copy-start = (bf16[2,1,2,3,128,128]{5,4,3,2,1,0:T(8,128)(2,1)S(1)}, bf16[2,1,2,3,128,128]{5,4,3,2,1,0:T(8,128)(2,1)}, u32[]{:S(2)}) copy-start(bf16[2,1,2,3,128,128]{5,4,3,2,1,0:T(8,128)(2,1)} %param.7) | copy-start | bytes 1179652
  79.5 27.2 %collective-permute-start.5 = (bf16[4,2,16,16,128]{4,3,2,1,0:T(8,128)(2,1)S(1)}, bf16[4,2,16,16,128]{4,3,2,1,0:T(8,128)(2,1)S(1)}, u32[]{:S(2)}, u32[]{:S(2)}) collective-permute-start(bf16[4,2,16,16,128]{4,3,2,1,0:T(8,128)(2,1)S(1)} %joined.1.refs_0_), channel_id=1, source_target_pairs={{0,6},{1,7},{2,0},{3,1},{4,2},{5,3},{6,4},{7,5},{8,14},{9,15},{10,... | collective-permute-start | bytes 1572872 | tf_op jit(solution)/shard_map/ppermute | solution.py:252
  84.5 22.2 %collective-permute-start.4 = (bf16[4,2,16,16,128]{4,3,2,1,0:T(8,128)(2,1)S(1)}, bf16[4,2,16,16,128]{4,3,2,1,0:T(8,128)(2,1)S(1)}, u32[]{:S(2)}, u32[]{:S(2)}) collective-permute-start(bf16[4,2,16,16,128]{4,3,2,1,0:T(8,128)(2,1)S(1)} %joined.1.refs_0_), channel_id=1, source_target_pairs={{0,4},{1,5},{2,6},{3,7},{4,0},{5,1},{6,2},{7,3},{8,12},{9,13},{10,... | collective-permute-start | bytes 1572872 | tf_op jit(solution)/shard_map/ppermute | solution.py:252
  87.0 25.3 %collective-permute-start.3 = (bf16[4,2,16,16,128]{4,3,2,1,0:T(8,128)(2,1)S(1)}, bf16[4,2,16,16,128]{4,3,2,1,0:T(8,128)(2,1)S(1)}, u32[]{:S(2)}, u32[]{:S(2)}) collective-permute-start(bf16[4,2,16,16,128]{4,3,2,1,0:T(8,128)(2,1)S(1)} %joined.1.refs_0_), channel_id=1, source_target_pairs={{0,2},{1,3},{2,4},{3,5},{4,6},{5,7},{6,0},{7,1},{8,10},{9,11},{10,... | collective-permute-start | bytes 1572872 | tf_op jit(solution)/shard_map/ppermute | solution.py:252
  117.6 15.3 %all-to-all-start.3 = ((bf16[4,2,4,2,32,128]{5,4,3,2,1,0:T(8,128)(2,1)}), bf16[4,2,4,2,32,128]{5,4,3,2,1,0:T(8,128)(2,1)S(1)}, u32[]{:S(2)}, u32[]{:S(2)}) async-start(bf16[4,2,4,2,32,128]{5,4,3,2,1,0:T(8,128)(2,1)} %ladder.1), calls=%async_computation.3 | async-start | bytes 1048576 | tf_op jit(solution)/shard_map/all_to_all | solution.py:304
  133.1 18.3 %collective-permute-start.6 = (bf16[2,4,2,16,128]{4,3,2,1,0:T(8,128)(2,1)S(1)}, bf16[2,4,2,16,128]{4,3,2,1,0:T(8,128)(2,1)S(1)}, u32[]{:S(2)}, u32[]{:S(2)}) collective-permute-start(bf16[2,4,2,16,128]{4,3,2,1,0:T(8,128)(2,1)S(1)} %fusion.3), channel_id=1, source_target_pairs={{0,1},{1,0},{2,3},{3,2},{4,5},{5,4},{6,7},{7,6},{8,9},{9,8},{10,11... | collective-permute-start | bytes 196616 | tf_op jit(solution)/shard_map/ppermute | solution.py:258
